TPU v7x, 512 devices: a whole 4x8x8 slice. The times are simulated.
512 devices in a mesh: frame: 32 (over y, x), pix: 16 (over z, core).
Axes of the slice: x: 4, y: 8, z: 8, core: 2. Of those that a mesh axis runs over, the one named last changes fastest.
Arguments:
- query_s: bfloat16 [2, 32, 1024, 576], P(None, 'frame', 'pix'), may hold values from -6 to 6
- key_s: bfloat16 [2, 32, 1024, 576], P(None, 'frame', 'pix'), may hold values from -6 to 6
- value_s: bfloat16 [2, 32, 1024, 576], P(None, 'frame', 'pix'), may hold values from -6 to 6
- query_t: bfloat16 [2, 32, 1024, 576], P(None, 'frame', 'pix'), may hold values from -6 to 6
- key_t: bfloat16 [2, 32, 1024, 576], P(None, 'frame', 'pix'), may hold values from -6 to 6
- value_t: bfloat16 [2, 32, 1024, 576], P(None, 'frame', 'pix'), may hold values from -6 to 6
- grad_out: bfloat16 [2, 32, 1024, 1152], P(None, 'frame', 'pix'), may hold values from -6 to 6
- proj_s: bfloat16 [576, 1152], replicated, may hold values from -0.25 to 0.25
- proj_t: bfloat16 [576, 1152], replicated, may hold values from -0.25 to 0.25
Outputs:
- grad_query_s: bfloat16 [2, 32, 1024, 576], P(None, 'frame', 'pix')
- grad_key_s: bfloat16 [2, 32, 1024, 576], P(None, 'frame', 'pix')
- grad_value_s: bfloat16 [2, 32, 1024, 576], P(None, 'frame', 'pix')
- grad_query_t: bfloat16 [2, 32, 1024, 576], P(None, 'frame', 'pix')
- grad_key_t: bfloat16 [2, 32, 1024, 576], P(None, 'frame', 'pix')
- grad_value_t: bfloat16 [2, 32, 1024, 576], P(None, 'frame', 'pix')
- grad_proj_s: float32 [576, 1152], P('frame', 'pix')
- grad_proj_t: float32 [576, 1152], P('frame', 'pix')
All inputs are finite; a program needn't handle non-finite values.
Results may differ from a plain program's by a relative error of at most 0.034.
Values may be sent and summed in bfloat16 or wider, within the bound.
No kernel may reach another device: no remote copies, remote signals or barrier semaphores. Data moves between devices by JAX's collectives and lax.ppermute only.
A program may use at most 128 MiB of HBM per device.

v0:
```python
import jax
import jax.numpy as jnp
from jax import lax
from jax.sharding import PartitionSpec as P

HSIZE = 72
HEADS = 8


def split_heads(block):
    return block.reshape(block.shape[0], block.shape[2], HEADS, HSIZE)


def local_attend(queries, key_rows, value_rows):
    factor = HSIZE ** (-0.5)
    scores = (
        jnp.einsum("bqhe,bkhe->bhqk", queries, key_rows, preferred_element_type=jnp.float32)
        * factor
    )
    highest = scores.max(-1)
    exp_scores = jnp.exp(scores - highest[..., None])
    totals = exp_scores.sum(-1)
    mixed = jnp.einsum(
        "bhqk,bkhe->bqhe",
        exp_scores.astype(jnp.bfloat16),
        value_rows,
        preferred_element_type=jnp.float32,
    )
    mixed = mixed / totals.transpose(0, 2, 1)[..., None]
    return (mixed.astype(jnp.bfloat16), highest + jnp.log(totals))


def local_back(queries, key_rows, value_rows, outputs, log_totals, grad_outputs):
    factor = HSIZE ** (-0.5)
    scores = (
        jnp.einsum("bqhe,bkhe->bhqk", queries, key_rows, preferred_element_type=jnp.float32)
        * factor
    )
    weights = jnp.exp(scores - log_totals[..., None])
    grad_values = jnp.einsum(
        "bhqk,bqhe->bkhe",
        weights.astype(jnp.bfloat16),
        grad_outputs,
        preferred_element_type=jnp.float32,
    )
    dprob = jnp.einsum(
        "bqhe,bkhe->bhqk", grad_outputs, value_rows, preferred_element_type=jnp.float32
    )
    delta = jnp.sum(grad_outputs.astype(jnp.float32) * outputs.astype(jnp.float32), -1).transpose(
        0, 2, 1
    )
    dscore = (weights * (dprob - delta[..., None])).astype(jnp.bfloat16)
    grad_queries = factor * jnp.einsum(
        "bhqk,bkhe->bqhe", dscore, key_rows, preferred_element_type=jnp.float32
    )
    grad_keys = factor * jnp.einsum(
        "bhqk,bqhe->bkhe", dscore, queries, preferred_element_type=jnp.float32
    )
    return (
        grad_queries.astype(jnp.bfloat16),
        grad_keys.astype(jnp.bfloat16),
        grad_values.astype(jnp.bfloat16),
    )


def on_device(query_s, key_s, value_s, query_t, key_t, value_t, grad_out, proj_s, proj_t):
    clip_count = query_s.shape[0]
    pix_rows = query_s.shape[2]
    attn_width = query_s.shape[3]
    frame_count = lax.axis_size("frame")
    pos_rows = pix_rows // frame_count
    factor = HSIZE ** (-0.5)
    grad_rows = grad_out[:, 0]
    spatial_grad = jnp.einsum(
        "cpd,ed->cpe", grad_rows, proj_s, preferred_element_type=jnp.float32
    ).astype(jnp.bfloat16)
    temporal_grad = jnp.einsum(
        "cpd,ed->cpe", grad_rows, proj_t, preferred_element_type=jnp.float32
    ).astype(jnp.bfloat16)
    spatial_do = spatial_grad.reshape(clip_count, 1, pix_rows, attn_width)
    temporal_do = temporal_grad.reshape(clip_count, 1, pix_rows, attn_width)
    queries = split_heads(query_s)
    own_keys = split_heads(key_s)
    own_values = split_heads(value_s)
    grad_heads = split_heads(spatial_do)
    whole_frame = (
        lax.all_gather(key_s, "pix", axis=2, tiled=True),
        lax.all_gather(value_s, "pix", axis=2, tiled=True),
    )
    running = jnp.full((clip_count, HEADS, pix_rows), -1e30, jnp.float32)
    key_piece = split_heads(whole_frame[0])
    value_piece = split_heads(whole_frame[1])
    scores = (
        jnp.einsum("cqhe,ckhe->chqk", queries, key_piece, preferred_element_type=jnp.float32)
        * factor
    )
    newest = jnp.maximum(running, scores.max(-1))
    weights = jnp.exp(scores - newest[..., None])
    totals = weights.sum(-1)
    accum = jnp.einsum(
        "chqk,ckhe->cqhe",
        weights.astype(jnp.bfloat16),
        value_piece,
        preferred_element_type=jnp.float32,
    )
    running, totals, accum = (newest, totals, accum)
    spatial_out = (accum / totals.transpose(0, 2, 1)[..., None]).astype(jnp.bfloat16)
    log_totals = running + jnp.log(totals)
    delta = jnp.sum(grad_heads.astype(jnp.float32) * spatial_out.astype(jnp.float32), -1).transpose(
        0, 2, 1
    )
    key_piece = split_heads(whole_frame[0])
    value_piece = split_heads(whole_frame[1])
    scores = (
        jnp.einsum("cqhe,ckhe->chqk", queries, key_piece, preferred_element_type=jnp.float32)
        * factor
    )
    weights = jnp.exp(scores - log_totals[..., None])
    dprob = jnp.einsum(
        "cqhe,ckhe->chqk", grad_heads, value_piece, preferred_element_type=jnp.float32
    )
    dscore = (weights * (dprob - delta[..., None])).astype(jnp.bfloat16)
    grad_queries = factor * jnp.einsum(
        "chqk,ckhe->cqhe", dscore, key_piece, preferred_element_type=jnp.float32
    )
    stats = (
        lax.all_gather(log_totals, "pix", axis=2, tiled=True),
        lax.all_gather(delta, "pix", axis=2, tiled=True),
    )
    query_piece = split_heads(lax.all_gather(query_s, "pix", axis=2, tiled=True))
    grad_piece = split_heads(lax.all_gather(spatial_do, "pix", axis=2, tiled=True))
    log_piece = stats[0]
    delta_piece = stats[1]
    scores = (
        jnp.einsum("cqhe,ckhe->chqk", query_piece, own_keys, preferred_element_type=jnp.float32)
        * factor
    )
    weights = jnp.exp(scores - log_piece[..., None])
    grad_values = jnp.einsum(
        "chqk,cqhe->ckhe",
        weights.astype(jnp.bfloat16),
        grad_piece,
        preferred_element_type=jnp.float32,
    )
    dprob = jnp.einsum(
        "cqhe,ckhe->chqk", grad_piece, own_values, preferred_element_type=jnp.float32
    )
    dscore = (weights * (dprob - delta_piece[..., None])).astype(jnp.bfloat16)
    grad_keys = factor * jnp.einsum(
        "chqk,cqhe->ckhe", dscore, query_piece, preferred_element_type=jnp.float32
    )
    grad_keys, grad_values = (grad_keys, grad_values)

    def to_batch(block):
        return block.transpose(0, 2, 1, 3).reshape(clip_count * pos_rows, frame_count, HEADS, HSIZE)

    def from_batch(block):
        return block.reshape(clip_count, pos_rows, frame_count, attn_width).transpose(0, 2, 1, 3)

    moved = (
        lax.all_to_all(query_t, "frame", split_axis=2, concat_axis=1, tiled=True),
        lax.all_to_all(key_t, "frame", split_axis=2, concat_axis=1, tiled=True),
        lax.all_to_all(value_t, "frame", split_axis=2, concat_axis=1, tiled=True),
    )
    batch_q = to_batch(moved[0])
    batch_k = to_batch(moved[1])
    batch_v = to_batch(moved[2])
    batch_out, batch_lse = local_attend(batch_q, batch_k, batch_v)
    temporal_out = lax.all_to_all(
        from_batch(batch_out), "frame", split_axis=1, concat_axis=2, tiled=True
    )
    batch_do = to_batch(
        lax.all_to_all(temporal_do, "frame", split_axis=2, concat_axis=1, tiled=True)
    )
    batch_dq, batch_dk, batch_dv = local_back(
        batch_q, batch_k, batch_v, batch_out, batch_lse, batch_do
    )
    homed = (
        lax.all_to_all(from_batch(batch_dq), "frame", split_axis=1, concat_axis=2, tiled=True),
        lax.all_to_all(from_batch(batch_dk), "frame", split_axis=1, concat_axis=2, tiled=True),
        lax.all_to_all(from_batch(batch_dv), "frame", split_axis=1, concat_axis=2, tiled=True),
    )
    temp_dq, temp_dk, temp_dv = homed
    flat_grad = grad_rows.reshape(clip_count * pix_rows, grad_rows.shape[2])
    spatial_flat = spatial_out.reshape(clip_count * pix_rows, attn_width)
    temporal_flat = temporal_out.reshape(clip_count * pix_rows, attn_width)
    partial_sums = jnp.stack(
        [
            jnp.einsum("re,rd->ed", spatial_flat, flat_grad, preferred_element_type=jnp.float32),
            jnp.einsum("re,rd->ed", temporal_flat, flat_grad, preferred_element_type=jnp.float32),
        ]
    )
    frame_sums = lax.psum_scatter(
        partial_sums.astype(jnp.bfloat16), "pix", scatter_dimension=2, tiled=True
    )
    totals_all = lax.psum_scatter(frame_sums, "frame", scatter_dimension=1, tiled=True).astype(
        jnp.float32
    )
    out_shape = (clip_count, 1, pix_rows, attn_width)
    return (
        grad_queries.reshape(out_shape).astype(jnp.bfloat16),
        grad_keys.reshape(out_shape).astype(jnp.bfloat16),
        grad_values.reshape(out_shape).astype(jnp.bfloat16),
        temp_dq,
        temp_dk,
        temp_dv,
        totals_all[0],
        totals_all[1],
    )


def solution(mesh):
    in_specs = (
        P(None, "frame", "pix", None),
        P(None, "frame", "pix", None),
        P(None, "frame", "pix", None),
        P(None, "frame", "pix", None),
        P(None, "frame", "pix", None),
        P(None, "frame", "pix", None),
        P(None, "frame", "pix", None),
        P(),
        P(),
    )
    out_specs = (
        P(None, "frame", "pix", None),
        P(None, "frame", "pix", None),
        P(None, "frame", "pix", None),
        P(None, "frame", "pix", None),
        P(None, "frame", "pix", None),
        P(None, "frame", "pix", None),
        P("frame", "pix"),
        P("frame", "pix"),
    )
    return jax.shard_map(
        on_device, mesh=mesh, in_specs=in_specs, out_specs=out_specs, check_vma=False
    )
```

profile of v0, /device:TPU:1, one launch (start us, length us, event | category | flops | bytes accessed | tf_op | source)
XLA Modules:
  0.0 480.0 jit_solution(5050677965105131221)
XLA Ops:
  11.2 10.5 %all-to-all-start.1 = ((bf16[2,1,64,576]{3,0,1,2:T(2,128)(2,1)}), bf16[2,1,64,576]{3,0,1,2:T(2,128)(2,1)S(1)}, u32[]{:S(2)}, u32[]{:S(2)}) async-start(bf16[2,1,64,576]{3,0,1,2:T(2,128)(2,1)} %copy.241), calls=%async_computation.1 | async-start | bytes 327680 | tf_op jit(solution)/shard_map/all_to_all | solution.py:162
  21.7 1.8 copy.239
  23.4 7.9 %all-to-all-done.1 = bf16[2,1,64,576]{3,0,1,2:T(2,128)(2,1)S(1)} async-done(((bf16[2,1,64,576]{3,0,1,2:T(2,128)(2,1)}), bf16[2,1,64,576]{3,0,1,2:T(2,128)(2,1)S(1)}, u32[]{:S(2)}, u32[]{:S(2)}) %all-to-all-start.1) | async-done | bytes 147488 | tf_op jit(solution)/shard_map/all_to_all | solution.py:162
  31.3 4.1 all-to-all-start
  37.8 7.2 %all-to-all-done = bf16[2,1,64,576]{3,0,1,2:T(2,128)(2,1)S(1)} async-done(((bf16[2,1,64,576]{3,0,1,2:T(2,128)(2,1)}), bf16[2,1,64,576]{3,0,1,2:T(2,128)(2,1)S(1)}, u32[]{:S(2)}, u32[]{:S(2)}) %all-to-all-start) | async-done | bytes 147488 | tf_op jit(solution)/shard_map/all_to_all | solution.py:161
  45.1 3.9 all-to-all-start.2
  52.9 5.7 %all-to-all-done.2 = bf16[2,1,64,576]{3,0,1,2:T(2,128)(2,1)S(1)} async-done(((bf16[2,1,64,576]{3,0,1,2:T(2,128)(2,1)}), bf16[2,1,64,576]{3,0,1,2:T(2,128)(2,1)S(1)}, u32[]{:S(2)}, u32[]{:S(2)}) %all-to-all-start.2) | async-done | bytes 147488 | tf_op jit(solution)/shard_map/all_to_all | solution.py:173
  58.6 3.9 all-to-all-start.3
  63.0 9.2 %all-to-all-done.3 = bf16[2,1,64,576]{3,0,1,2:T(2,128)(2,1)S(1)} async-done(((bf16[2,1,64,576]{3,0,1,2:T(2,128)(2,1)}), bf16[2,1,64,576]{3,0,1,2:T(2,128)(2,1)S(1)}, u32[]{:S(2)}, u32[]{:S(2)}) %all-to-all-start.3) | async-done | bytes 147488 | tf_op jit(solution)/shard_map/all_to_all | solution.py:163
  76.8 3.9 all-to-all-start.4
  82.0 8.3 %all-to-all-done.4 = bf16[2,32,2,576]{3,2,0,1:T(2,128)(2,1)S(1)} async-done(((bf16[2,32,2,576]{3,2,0,1:T(2,128)(2,1)}), bf16[2,32,2,576]{3,2,0,1:T(2,128)(2,1)S(1)}, u32[]{:S(2)}, u32[]{:S(2)}) %all-to-all-start.4) | async-done | bytes 147488 | tf_op jit(solution)/shard_map/all_to_all | solution.py:179
  90.3 4.6 all-to-all-start.5
  96.3 8.3 %all-to-all-done.5 = bf16[2,32,2,576]{3,2,0,1:T(2,128)(2,1)} async-done(((bf16[2,32,2,576]{3,2,0,1:T(2,128)(2,1)}), bf16[2,32,2,576]{3,2,0,1:T(2,128)(2,1)}, u32[]{:S(2)}, u32[]{:S(2)}) %all-to-all-start.5) | async-done | bytes 147488 | tf_op jit(solution)/shard_map/all_to_all | solution.py:180
  104.6 3.9 all-to-all-start.6
  110.5 7.6 %all-to-all-done.6 = bf16[2,32,2,576]{3,2,0,1:T(2,128)(2,1)S(1)} async-done(((bf16[2,32,2,576]{3,2,0,1:T(2,128)(2,1)}), bf16[2,32,2,576]{3,2,0,1:T(2,128)(2,1)S(1)}, u32[]{:S(2)}, u32[]{:S(2)}) %all-to-all-start.6) | async-done | bytes 147488 | tf_op jit(solution)/shard_map/all_to_all | solution.py:181
  118.1 3.9 all-to-all-start.7
  135.3 4.5 copy.223
  139.8 4.4 copy.225
  144.2 2.5 multiply_reduce_fusion
  147.7 2.2 copy-done.3
  153.6 1.8 pad_maximum_fusion
  155.4 10.4 %copy.272 = bf16[2,576,1152]{1,0,2:T(2,128)(2,1)} copy(bf16[2,576,1152]{2,1,0:T(8,128)(2,1)} %pad_maximum_fusion) | data formatting | bytes 5308416 | tf_op jit(solution)/shard_map/stack | solution.py:187
  165.8 4.5 copy.229
  170.2 4.3 fusion.67
  174.8 35.1 %all_gather.23 = f32[2,8,1024]{1,0,2:T(2,128)S(1)} all-gather(f32[2,8,64]{1,0,2:T(2,128)S(1)} %copy.235), channel_id=1, replica_groups=mesh['frame'=32,'pix'=16] {'pix'}, dimensions={2}, use_global_device_ids=true | all-gather | bytes 69632 | tf_op jit(solution)/shard_map/all_gather | solution.py:128
  210.4 19.9 %all_gather.21 = f32[2,8,1024]{1,0,2:T(2,128)S(1)} all-gather(f32[2,8,64]{1,0,2:T(2,128)S(1)} %copy.231), channel_id=1, replica_groups=mesh['frame'=32,'pix'=16] {'pix'}, dimensions={2}, use_global_device_ids=true | all-gather | bytes 69632 | tf_op jit(solution)/shard_map/all_gather | solution.py:127
  230.8 4.5 copy.233
  235.2 5.7 %fusion.41 = bf16[2,64,8,72]{3,1,2,0:T(8,128)(2,1)S(1)} fusion(bf16[2,1024,8,72]{1,3,2,0:T(8,128)(2,1)} %bitcast.134, f32[2,8,64,1024]{3,2,1,0:T(8,128)} %copy-done.1, bf16[2,1024,8,72]{1,3,2,0:T(8,128)(2,1)} %bitcast.137, f32[2,8,64]{2,1,0:T(8,128)S(1)} %bitcast.158, f32[2,8,64]{2,1,0:T(8,128)S(1)} %log_add_fusion.1, bf16[2,64,8,72]{3,2,1,0:T(8,128)(2,1)S(1)} %copy-done.12), kind=kOutput, calls=%fused_computation.47 | convolution fusion | flops 307380224 | bytes 9216000 | tf_op jit(solution)/shard_map/chqk,ckhe->cqhe/dot_general | solution.py:123
  241.0 5.4 %fusion.42 = bf16[2,64,8,72]{3,1,2,0:T(8,128)(2,1)S(1)} fusion(bf16[2,1024,8,72]{1,3,2,0:T(8,128)(2,1)} %bitcast.130, f32[2,8,1024,64]{2,3,1,0:T(8,128)} %fusion.67, bf16[2,1024,8,72]{1,3,2,0:T(8,128)(2,1)} %bitcast.131, f32[2,8,1024]{2,1,0:T(8,128)S(1)} %copy.236, f32[2,8,1024]{2,1,0:T(8,128)S(1)} %copy.232, bf16[2,64,8,72]{3,2,1,0:T(8,128)(2,1)S(1)} %copy-done.10), kind=kOutput, calls=%fused_computation.48 | convolution fusion | flops 307380224 | bytes 9338880 | tf_op jit(solution)/shard_map/chqk,cqhe->ckhe/dot_general | solution.py:149
  246.4 71.6 %all-reduce.5.cloned.1.call-done = bf16[2,576,1152]{1,0,2:T(2,128)(2,1)} async-done(((bf16[2,576,1152]{1,0,2:T(2,128)(2,1)}), bf16[2,576,1152]{1,0,2:T(2,128)(2,1)}) %all-reduce.5.cloned.1.call-update) | async-done | bytes 2654224
  320.2 3.8 fusion.38
  327.1 144.7 %all-reduce.7.cloned.1.call-done = bf16[2,576,72]{2,0,1:T(2,128)(2,1)} async-done(((bf16[2,576,72]{2,0,1:T(2,128)(2,1)}), bf16[2,576,72]{2,0,1:T(2,128)(2,1)}) %all-reduce.7.cloned.1.call-update) | async-done | bytes 165904
  (112 shorter events, 44.2 us)
Async XLA Ops:
  7.2 28.3 %copy-start = (bf16[576,1152]{1,0:T(8,128)(2,1)S(1)}, bf16[576,1152]{1,0:T(8,128)(2,1)}, u32[]{:S(2)}) copy-start(bf16[576,1152]{1,0:T(8,128)(2,1)} %param.17) | copy-start | bytes 3981316
  7.2 41.8 %copy-start.2 = (bf16[2,1,64,1152]{3,2,1,0:T(8,128)(2,1)S(1)}, bf16[2,1,64,1152]{3,2,1,0:T(8,128)(2,1)}, u32[]{:S(2)}) copy-start(bf16[2,1,64,1152]{3,2,1,0:T(8,128)(2,1)} %param.15) | copy-start | bytes 884740
  7.2 41.8 %copy-start.5 = (bf16[576,1152]{1,0:T(8,128)(2,1)S(1)}, bf16[576,1152]{1,0:T(8,128)(2,1)}, u32[]{:S(2)}) copy-start(bf16[576,1152]{1,0:T(8,128)(2,1)} %param.16) | copy-start | bytes 3981316
  7.2 128.1 %all-gather.6.cloned.1.call-start = ((), (), s32[]{:S(2)}) async-start(), calls=%async_computation.8 | async-start | bytes 2785280 | tf_op jit(solution)/shard_map/all_gather | solution.py:87
  7.9 131.9 %all-gather.8.cloned.1.call-start = ((), (), s32[]{:S(2)}) async-start(), calls=%async_computation.9 | async-start | bytes 2785280 | tf_op jit(solution)/shard_map/all_gather | solution.py:88
  8.7 157.1 %all-gather.10.cloned.1.call-start = ((), (), s32[]{:S(2)}) async-start(), calls=%async_computation.10 | async-start | bytes 2785280 | tf_op jit(solution)/shard_map/all_gather | solution.py:130
  11.2 20.1 %all-to-all-start.1 = ((bf16[2,1,64,576]{3,0,1,2:T(2,128)(2,1)}), bf16[2,1,64,576]{3,0,1,2:T(2,128)(2,1)S(1)}, u32[]{:S(2)}, u32[]{:S(2)}) async-start(bf16[2,1,64,576]{3,0,1,2:T(2,128)(2,1)} %copy.241), calls=%async_computation.1 | async-start | bytes 327680 | tf_op jit(solution)/shard_map/all_to_all | solution.py:162
  31.3 13.8 %all-to-all-start = ((bf16[2,1,64,576]{3,0,1,2:T(2,128)(2,1)}), bf16[2,1,64,576]{3,0,1,2:T(2,128)(2,1)S(1)}, u32[]{:S(2)}, u32[]{:S(2)}) async-start(bf16[2,1,64,576]{3,0,1,2:T(2,128)(2,1)} %copy.239), calls=%async_computation | async-start | bytes 327680 | tf_op jit(solution)/shard_map/all_to_all | solution.py:161
  45.1 13.6 %all-to-all-start.2 = ((bf16[2,1,64,576]{3,0,1,2:T(2,128)(2,1)}), bf16[2,1,64,576]{3,0,1,2:T(2,128)(2,1)S(1)}, u32[]{:S(2)}, u32[]{:S(2)}) async-start(bf16[2,1,64,576]{3,0,1,2:T(2,128)(2,1)} %copy.245), calls=%async_computation.2 | async-start | bytes 327680 | tf_op jit(solution)/shard_map/all_to_all | solution.py:173
  49.0 181.8 %all-gather.12.cloned.1.call-start = ((), (), s32[]{:S(2)}) async-start(), calls=%async_computation.11 | async-start | bytes 2785280 | tf_op jit(solution)/shard_map/all_gather | solution.py:131
  58.6 13.6 %all-to-all-start.3 = ((bf16[2,1,64,576]{3,0,1,2:T(2,128)(2,1)}), bf16[2,1,64,576]{3,0,1,2:T(2,128)(2,1)S(1)}, u32[]{:S(2)}, u32[]{:S(2)}) async-start(bf16[2,1,64,576]{3,0,1,2:T(2,128)(2,1)} %copy.247), calls=%async_computation.3 | async-start | bytes 327680 | tf_op jit(solution)/shard_map/all_to_all | solution.py:163
  76.8 13.6 %all-to-all-start.4 = ((bf16[2,32,2,576]{3,2,0,1:T(2,128)(2,1)}), bf16[2,32,2,576]{3,2,0,1:T(2,128)(2,1)S(1)}, u32[]{:S(2)}, u32[]{:S(2)}) async-start(bf16[2,32,2,576]{3,2,0,1:T(2,128)(2,1)} %copy.258), calls=%async_computation.4 | async-start | bytes 327680 | tf_op jit(solution)/shard_map/all_to_all | solution.py:179
  81.0 41.3 %copy-start.8 = (bf16[2,1,64,576]{3,2,1,0:T(8,128)(2,1)S(1)}, bf16[2,1,64,576]{3,2,1,0:T(8,128)(2,1)}, u32[]{:S(2)}) copy-start(bf16[2,1,64,576]{3,2,1,0:T(8,128)(2,1)} %param.9) | copy-start | bytes 442372
  81.2 41.3 %copy-start.4 = (bf16[2,64,576]{2,1,0:T(8,128)(2,1)S(1)}, bf16[2,64,576]{2,1,0:T(8,128)(2,1)}, u32[]{:S(2)}) copy-start(bf16[2,64,576]{2,1,0:T(8,128)(2,1)} %fusion.43) | copy-start | bytes 442372
  82.0 41.5 %copy-start.6 = (bf16[2,1,64,576]{3,2,1,0:T(8,128)(2,1)S(1)}, bf16[2,1,64,576]{3,2,1,0:T(8,128)(2,1)}, u32[]{:S(2)}) copy-start(bf16[2,1,64,576]{3,2,1,0:T(8,128)(2,1)} %param.10) | copy-start | bytes 442372
  90.3 32.2 %copy-start.9 = (bf16[2,32,2,576]{3,2,0,1:T(2,128)(2,1)}, bf16[2,32,2,576]{3,2,0,1:T(2,128)(2,1)S(1)}, u32[]{:S(2)}) copy-start(bf16[2,32,2,576]{3,2,0,1:T(2,128)(2,1)S(1)} %all-to-all-done.4) | copy-start | bytes 442372
  90.3 14.2 %all-to-all-start.5 = ((bf16[2,32,2,576]{3,2,0,1:T(2,128)(2,1)}), bf16[2,32,2,576]{3,2,0,1:T(2,128)(2,1)}, u32[]{:S(2)}, u32[]{:S(2)}) async-start(bf16[2,32,2,576]{3,2,0,1:T(2,128)(2,1)} %copy.262), calls=%async_computation.5 | async-start | bytes 327680 | tf_op jit(solution)/shard_map/all_to_all | solution.py:180
  94.9 28.9 %copy-start.7 = (bf16[2,1,64,576]{3,2,1,0:T(8,128)(2,1)S(1)}, bf16[2,1,64,576]{3,2,1,0:T(8,128)(2,1)}, u32[]{:S(2)}) copy-start(bf16[2,1,64,576]{3,2,1,0:T(8,128)(2,1)} %param.11) | copy-start | bytes 442372
  104.6 13.6 %all-to-all-start.6 = ((bf16[2,32,2,576]{3,2,0,1:T(2,128)(2,1)}), bf16[2,32,2,576]{3,2,0,1:T(2,128)(2,1)S(1)}, u32[]{:S(2)}, u32[]{:S(2)}) async-start(bf16[2,32,2,576]{3,2,0,1:T(2,128)(2,1)} %copy.266), calls=%async_computation.6 | async-start | bytes 327680 | tf_op jit(solution)/shard_map/all_to_all | solution.py:181
  118.1 14.8 %all-to-all-start.7 = ((bf16[2,32,2,576]{3,2,0,1:T(2,128)(2,1)}), bf16[2,32,2,576]{3,2,0,1:T(2,128)(2,1)S(1)}, u32[]{:S(2)}, u32[]{:S(2)}) async-start(bf16[2,32,2,576]{3,2,0,1:T(2,128)(2,1)} %copy.270), calls=%async_computation.7 | async-start | bytes 327680 | tf_op jit(solution)/shard_map/all_to_all | solution.py:169
  122.0 196.0 %all-reduce.5.cloned.1.call-start = ((), (), s32[]{:S(2)}) async-start(), calls=%async_computation.12 | async-start | bytes 5898240
  146.7 4.4 copy-start.1
  146.7 3.2 copy-start.3
  146.7 3.2 copy-start.11
  174.6 297.2 %all-reduce.7.cloned.1.call-start = ((), (), s32[]{:S(2)}) async-start(), calls=%async_computation.13 | async-start | bytes 589824
  230.7 4.5 copy-start.12
  235.2 5.7 %copy-start.10 = (bf16[2,64,8,72]{3,2,1,0:T(8,128)(2,1)S(1)}, bf16[2,64,8,72]{3,2,1,0:T(8,128)(2,1)}, u32[]{:S(2)}) copy-start(bf16[2,64,8,72]{3,2,1,0:T(8,128)(2,1)} %reshape.171) | copy-start | bytes 442372
Sparse Core Ops, SparseCore 0:
  10.2 49.6 all-gather.5
  62.0 41.8 all-gather.7
  106.1 41.8 all-gather.9
  150.6 41.9 all-gather.11
  194.8 123.1 all-reduce.4
  321.2 150.5 all-reduce.6
where the time goes:
time: 485 us; the launch traced here: 480 us
  waiting for transfers between devices  273 us (56%)
  local copies, waits for them, and re-layouts  62.9 us (13%)
  blocking collectives  55 us (11%)
  starting transfers between devices  38.9 us (8%)
  matrix products  31 us (6%)
  between operations  15.9 us (3%)
    unnamed x8, waiting for transfers between devices  218 us
    all_gather x1, blocking collectives, on_device(): lax.all_gather(delta, 'pix', axis=2, tiled=True)  35.1 us
    all_gather x1, blocking collectives, on_device(): lax.all_gather(log_totals, 'pix', axis=2, tiled=True)  19.9 us
    unnamed x36, local copies, waits for them, and re-layouts  13.8 us
    all_to_all x1, starting transfers between devices, on_device(): lax.all_to_all(key_t, 'frame', split_axis=2, concat_axis=1, tiled=True)  10.5 us
    another operation x1, local copies, waits for them, and re-layouts, on_device(): jnp.stack([jnp.einsum('re,rd->ed', spatial_flat, flat_grad, preferred_ele...  10.4 us
  transfers between devices with their start and end apart: 14, of which 9 were waited for; matrix products, arithmetic and copies ran while one was open for 19% of the time, Pallas kernels for 0%

commit v1 on v0

v1 whole, which is shorter than its diff:
```python
import jax
import jax.numpy as jnp
from jax import lax
from jax.experimental import pallas as pl
from jax.experimental.pallas import tpu as pltpu
from jax.sharding import PartitionSpec as P

HSIZE = 72
HEADS = 8
HD = 576
WIDE = 640
D = 1152
HALF = 576
FACTOR = HSIZE ** (-0.5)
BF = jnp.bfloat16
F32 = jnp.float32


def dot(a, b):
    return lax.dot_general(a, b, (((1,), (0,)), ((), ())), preferred_element_type=F32)


def dot_nt(a, b):
    return lax.dot_general(a, b, (((1,), (1,)), ((), ())), preferred_element_type=F32)


def iota(shape, dim):
    return lax.broadcasted_iota(jnp.int32, shape, dim)


def choose(cond):
    return jnp.where(cond, 1.0, 0.0).astype(BF)


def window(h):
    start = (HSIZE * h) // 128 * 128
    return start, min(256, HD - start), HSIZE * h - start


def core_columns(core):
    col = iota((D, HALF), 1)
    z = col // HSIZE
    return choose(iota((D, HALF), 0) == col + HSIZE * z + HSIZE * core)


def whole(shape, dtype):
    return jax.ShapeDtypeStruct(shape, dtype)


def call(kernel, n_in, out_shape, flops, scalars=0, scratch=()):
    many = isinstance(out_shape, (tuple, list))
    vmem = pl.BlockSpec(memory_space=pltpu.VMEM)
    smem = pl.BlockSpec(memory_space=pltpu.SMEM)
    return pl.pallas_call(
        kernel,
        out_shape=out_shape,
        in_specs=[smem] * scalars + [vmem] * n_in,
        out_specs=[vmem] * len(out_shape) if many else vmem,
        scratch_shapes=list(scratch),
        compiler_params=pltpu.CompilerParams(vmem_limit_bytes=32 * 1024 * 1024),
        cost_estimate=pl.CostEstimate(flops=flops, bytes_accessed=1 << 20, transcendentals=0),
    )


def pack_kernel(q_ref, k_ref, v_ref, out_ref):
    rows = q_ref.shape[0] // 2
    for h in range(HEADS):
        start, width, offset = window(h)
        total = None
        for a, ref in enumerate((q_ref, k_ref, v_ref)):
            i, j = iota((width, 256), 0), iota((width, 256), 1) - HSIZE * a
            sel = choose((i - offset == j) & (j >= 0) & (j < HSIZE))
            part = dot(ref[:, start : start + width], sel)
            total = part if total is None else total + part
        total = total.astype(BF)[:, : 3 * HSIZE]
        out_ref[2 * h] = total[:rows]
        out_ref[2 * h + 1] = total[rows:]


def unpack_kernel(x_ref, *out_refs):
    rows = x_ref.shape[1]
    for a, ref in enumerate(out_refs):
        for start in range(0, HD, 128):
            width = min(128, HD - start)
            total = None
            for h in range(HEADS):
                low = HSIZE * h - start
                if low >= width or low + HSIZE <= 0:
                    continue
                pair = jnp.concatenate([x_ref[2 * h], x_ref[2 * h + 1]], 0)
                i, j = iota((3 * HSIZE, width), 0) - HSIZE * a, iota((3 * HSIZE, width), 1)
                sel = choose((i + low == j) & (i >= 0) & (i < HSIZE))
                part = dot(pair, sel)
                total = part if total is None else total + part
            ref[:, start : start + width] = total.astype(BF)


def spatial_kernel(core_ref, x_ref, g_ref, proj_ref, out_ref, keep_ref, send_ref, dkt_ref, dvt_ref):
    core = core_ref[0]
    rows = x_ref.shape[0]
    pairs = rows // 128
    step = 256

    def swapped(value):
        parts = value.reshape(pairs, 2, 64, value.shape[1])
        other = jnp.concatenate([parts[:, 1:], parts[:, :1]], 1)
        return jnp.where(core == 0, parts, other).reshape(value.shape)

    i, j = iota((3 * HSIZE, 384), 0), iota((3 * HSIZE, 384), 1)
    sel = choose((i == HSIZE * (j // 128) + j % 128) & (j % 128 < HSIZE))
    split = dot(x_ref[...], sel)
    queries = split[:, :128]
    queries_bf = queries.astype(BF)
    keys = split[:, 128:256].astype(BF)
    values = split[:, 256:].astype(BF)
    grads = swapped(dot_nt(g_ref[...], proj_ref[...])).astype(BF).astype(F32)
    grads_bf = grads.astype(BF)
    outs = []
    dqs = []
    for b in range(rows // step):
        block = slice(b * step, (b + 1) * step)
        q, do = queries[block], grads[block]
        q_bf, do_bf = queries_bf[block], grads_bf[block]
        scores = dot_nt(q_bf, keys) * FACTOR
        top = scores.max(-1, keepdims=True)
        e = jnp.exp(scores - top)
        inverse = 1.0 / e.sum(-1, keepdims=True)
        out = (dot(e.astype(BF), values) * inverse).astype(BF).astype(F32)
        outs.append(out)
        weights = e * inverse
        delta = (do * out).sum(-1, keepdims=True)
        dprob = dot_nt(do_bf, values)
        dscore = (weights * (dprob - delta)).astype(BF)
        dqs.append(dot(dscore, keys) * FACTOR)
        dkt = dot(q.T.astype(BF), dscore)
        dvt = dot(do.T.astype(BF), weights.astype(BF))
        if b == 0:
            dkt_ref[...] = dkt
            dvt_ref[...] = dvt
        else:
            dkt_ref[...] += dkt
            dvt_ref[...] += dvt
    grads_all = jnp.concatenate(
        [jnp.concatenate(dqs, 0), dkt_ref[...].T * FACTOR, dvt_ref[...].T], 1
    ).astype(BF)
    out_ref[...] = dot_nt(grads_all, sel).astype(BF)
    out_all = swapped(jnp.concatenate(outs, 0))
    part = dot(out_all.T.astype(BF), g_ref[...]).astype(BF)
    keep_ref[...] = dot(part, core_columns(core)).astype(BF)[:HSIZE]
    send_ref[...] = dot(part, core_columns(1 - core)).astype(BF)[:HSIZE]


def temporal_kernel(core_ref, x_ref, proj_ref, out_ref, keep_ref, send_ref):
    core = core_ref[0]
    rows = x_ref.shape[0]
    group = 4
    q = x_ref[:, :HD]
    k = x_ref[:, WIDE : WIDE + HD]
    v = x_ref[:, 2 * WIDE : 2 * WIDE + HD]
    g = x_ref[:, 3 * WIDE :]
    do = dot_nt(g, proj_ref[...]).astype(BF)
    same = iota((rows, rows), 0) % group == iota((rows, rows), 1) % group
    head = iota((1, HD), 1) // HSIZE
    masks = [choose(head == h) for h in range(HEADS)]
    weights = []
    out = None
    for h in range(HEADS):
        scores = jnp.where(same, dot_nt(q * masks[h], k) * FACTOR, -1e30)
        e = jnp.where(same, jnp.exp(scores - scores.max(-1, keepdims=True)), 0.0)
        inverse = 1.0 / e.sum(-1, keepdims=True)
        part = dot(e.astype(BF), v * masks[h]) * inverse
        out = part if out is None else out + part
        weights.append(e * inverse)
    out = out.astype(BF)
    product = do.astype(F32) * out.astype(F32)
    dq = dk = dv = None
    for h in range(HEADS):
        dom = do * masks[h]
        delta = (product * masks[h].astype(F32)).sum(-1, keepdims=True)
        dscore = weights[h] * (dot_nt(dom, v) - delta)
        terms = (
            dot(dscore.astype(BF), k * masks[h]),
            dot(dscore.T.astype(BF), q * masks[h]),
            dot(weights[h].T.astype(BF), dom),
        )
        dq, dk, dv = terms if dq is None else (dq + terms[0], dk + terms[1], dv + terms[2])
    out_ref[:, :HD] = (dq * FACTOR).astype(BF)
    out_ref[:, WIDE : WIDE + HD] = (dk * FACTOR).astype(BF)
    out_ref[:, 2 * WIDE : 2 * WIDE + HD] = dv.astype(BF)
    i, j = iota((HD, HD), 0), iota((HD, HD), 1)
    order = choose(j == 18 * (i % 64 // 2) + 2 * (i // 64) + i % 2)
    out_t = dot_nt(order, out).astype(BF)
    for ref, half in ((keep_ref, core), (send_ref, 1 - core)):
        part = dot(out_t, dot(g, core_columns(half)).astype(BF)).astype(BF)
        ref[...] = jnp.zeros(ref.shape, BF)
        for b in range(9):
            ref[:, WIDE * b : WIDE * b + HALF] = part[64 * b : 64 * b + 64]


def on_device(query_s, key_s, value_s, query_t, key_t, value_t, grad_out, proj_s, proj_t):
    frames = lax.axis_size("frame")
    n_pix = lax.axis_size("pix")
    n_z = n_pix // 2
    pix = lax.axis_index("pix")
    core, z = pix % 2, pix // 2
    core_arg = core.reshape(1).astype(jnp.int32)
    core_swap = [(p, p ^ 1) for p in range(n_pix)]
    same_core = [[2 * i + c for i in range(n_z)] for c in range(2)]

    with jax.named_scope("spatial_grad_gather"):
        grad = grad_out[:, 0]
        own = lax.dynamic_index_in_dim(grad, core, 0, keepdims=False)
        other = lax.dynamic_index_in_dim(grad, 1 - core, 0, keepdims=False)
        other = lax.ppermute(other, "pix", core_swap)
        gathered = lax.all_gather(
            jnp.concatenate([own, other], 0), "pix", axis=0, axis_index_groups=same_core, tiled=True
        )

    with jax.named_scope("temporal_in"):
        spread = [jnp.pad(a[:, 0], ((0, 0), (0, 0), (0, WIDE - HD))) for a in (query_t, key_t, value_t)]
        rows = jnp.concatenate(spread + [grad], -1).reshape(4, frames, 3 * WIDE + D)
        moved_t = lax.all_to_all(rows.transpose(1, 0, 2), "frame", 0, 0, tiled=True)
        moved_t = moved_t.reshape(4 * frames, 3 * WIDE + D)

    with jax.named_scope("spatial_in"):
        flat = [a.reshape(128, HD) for a in (query_s, key_s, value_s)]
        packed = call(pack_kernel, 3, whole((n_pix, 64, 3 * HSIZE), BF), 1 << 26)(*flat)
        moved_s = lax.all_to_all(packed, "pix", 0, 0, tiled=True)

    with jax.named_scope("temporal_attention"):
        grads_t, keep_t, send_t = call(
            temporal_kernel,
            2,
            (
                whole((4 * frames, 3 * WIDE), BF),
                whole((64, 9 * WIDE), BF),
                whole((64, 9 * WIDE), BF),
            ),
            1 << 30,
            scalars=1,
        )(core_arg, moved_t, proj_t)
        total_t = keep_t.astype(F32) + lax.ppermute(send_t, "pix", core_swap).astype(F32)
        total_t = total_t.astype(BF).reshape(frames, 2, 9 * WIDE)

    with jax.named_scope("spatial_attention"):
        proj_h = lax.dynamic_slice_in_dim(proj_s, HSIZE * z, HSIZE, 0)
        proj_h = jnp.pad(proj_h, ((0, 128 - HSIZE), (0, 0)))
        grads_s, keep_s, send_s = call(
            spatial_kernel,
            3,
            (
                whole((n_pix * 64, 3 * HSIZE), BF),
                whole((HSIZE, HALF), BF),
                whole((HSIZE, HALF), BF),
            ),
            1 << 32,
            scalars=1,
            scratch=[pltpu.VMEM((128, n_pix * 64), F32)] * 2,
        )(core_arg, moved_s.reshape(n_pix * 64, 3 * HSIZE), gathered, proj_h)
        total_s = keep_s.astype(F32) + lax.ppermute(send_s, "pix", core_swap).astype(F32)

    with jax.named_scope("temporal_out"):
        home_t = lax.all_to_all(grads_t.reshape(frames, 4, 3 * WIDE), "frame", 0, 0, tiled=True)
        home_t = home_t.transpose(1, 0, 2).reshape(2, 1, 64, 3 * WIDE)
        outs_t = [home_t[..., WIDE * a : WIDE * a + HD] for a in range(3)]

    with jax.named_scope("temporal_projection"):
        parts_t = lax.all_to_all(total_t, "frame", 0, 0, tiled=True)
        sums_t = parts_t.astype(F32).sum(0).astype(BF).reshape(2, 9, WIDE)[..., :HALF]
        sums_t = sums_t.reshape(2, 9, n_z, HSIZE).transpose(2, 1, 0, 3).reshape(n_z, 18, HSIZE)
        last_t = lax.all_to_all(sums_t, "pix", 0, 0, axis_index_groups=same_core, tiled=True)
        proj_t_grad = last_t.astype(F32).sum(0)

    with jax.named_scope("spatial_projection"):
        chunks = total_s.astype(BF).reshape(4, 18, 8, HSIZE).transpose(2, 0, 1, 3)
        parts_s = lax.all_to_all(chunks.reshape(frames, 18, HSIZE), "frame", 0, 0, tiled=True)
        sums_s = parts_s.astype(F32).sum(0)
        perm = []
        for y in range(8):
            for x in range(4):
                for zz in range(n_z):
                    for c in range(2):
                        source = (y * 4 + x) * n_pix + 2 * zz + c
                        perm.append((source, (zz * 4 + x) * n_pix + 2 * y + c))
        proj_s_grad = lax.ppermute(sums_s, ("frame", "pix"), perm)

    with jax.named_scope("spatial_out"):
        home_s = lax.all_to_all(grads_s.reshape(n_pix, 64, 3 * HSIZE), "pix", 0, 0, tiled=True)
        outs_s = call(unpack_kernel, 1, (whole((128, HD), BF),) * 3, 1 << 26)(home_s)
        outs_s = [a.reshape(2, 1, 64, HD) for a in outs_s]

    return (*outs_s, *outs_t, proj_s_grad, proj_t_grad)


def solution(mesh):
    rows = P(None, "frame", "pix", None)
    out_specs = (rows,) * 6 + (P("frame", "pix"),) * 2
    return jax.shard_map(
        on_device,
        mesh=mesh,
        in_specs=(rows,) * 7 + (P(), P()),
        out_specs=out_specs,
        check_vma=False,
    )
```

time: 485 us -> 196 us (0.40)
  waiting for transfers between devices: 273 us -> 68.8 us
  local copies, waits for them, and re-layouts: 62.9 us -> 14.6 us
  blocking collectives: 55 us -> 17.3 us
  matrix products: 31 us -> 0 us
  starting transfers between devices: 38.9 us -> 57.2 us
  Pallas kernels: 0 us -> 17.5 us
    unnamed x8 -> x1, waiting for transfers between devices: 218 us -> 0.02 us
    all_gather x2 -> x0, blocking collectives: 55 us -> none  [the longest x1 35.1 us: on_device(): lax.all_gather(delta, 'pix', axis=2, tiled=True)]
    dot_general x16 -> x0, matrix products: 31 us -> none  [the longest x1 5.7 us: on_device(): jnp.einsum('chqk,ckhe->cqhe', dscore, key_piece, preferred_element_type=j...]
    all_gather x6 -> x0, local copies, waits for them, and re-layouts: 18.6 us -> none  [the longest x1 4.5 us: on_device(): lax.all_gather(key_s, 'pix', axis=2, tiled=True)]
    pallas_call x0 -> x4, Pallas kernels: none -> 17.5 us  [the longest x1 8.12 us: on_device(): call(temporal_kernel, 2, (whole((4 * frames, 3 * WIDE), BF), whole((64, 9...]
    all_to_all x0 -> x1, blocking collectives: none -> 17.3 us  [on_device(): lax.all_to_all(chunks.reshape(frames, 18, HSIZE), 'frame', 0, 0, tiled=True)]
    all_to_all x8 -> x6, waiting for transfers between devices: 54.3 us -> 67.7 us  [the longest x1 19.4 us: on_device(): parts_t = lax.all_to_all(total_t, 'frame', 0, 0, tiled=True)]
    ppermute x0 -> x4, starting transfers between devices: none -> 12 us  [the longest x1 4.81 us: on_device(): lax.ppermute(send_t, 'pix', core_swap).astype(F32)]
  transfers between devices with their start and end apart: 14 -> 11, of which waited for: 9 -> 7; matrix products, arithmetic and copies ran while one was open for 19% -> 6% of each run, Pallas kernels for 0% -> 8%
where the time goes in v1:
time: 196 us; the launch traced here: 195 us
  waiting for transfers between devices  68.8 us (35%)
  starting transfers between devices  57.2 us (29%)
  Pallas kernels  17.5 us (9%)
  blocking collectives  17.3 us (9%)
  local copies, waits for them, and re-layouts  14.6 us (7%)
  between operations  14.4 us (7%)
  other arithmetic  5.53 us (3%)
    all_to_all x1, waiting for transfers between devices, on_device(): parts_t = lax.all_to_all(total_t, 'frame', 0, 0, tiled=True)  19.4 us
    all_to_all x1, blocking collectives, on_device(): lax.all_to_all(chunks.reshape(frames, 18, HSIZE), 'frame', 0, 0, tiled=True)  17.3 us
    all_to_all x1, waiting for transfers between devices, on_device(): moved_t = lax.all_to_all(rows.transpose(1, 0, 2), 'frame', 0, 0, tiled=True)  16.3 us
    all_to_all x1, waiting for transfers between devices, on_device(): lax.all_to_all(grads_s.reshape(n_pix, 64, 3 * HSIZE), 'pix', 0, 0, tiled=...  13.6 us
    all_to_all x1, waiting for transfers between devices, on_device(): moved_s = lax.all_to_all(packed, 'pix', 0, 0, tiled=True)  11.7 us
    all_to_all x1, starting transfers between devices, on_device(): moved_t = lax.all_to_all(rows.transpose(1, 0, 2), 'frame', 0, 0, tiled=True)  10.5 us
    all_to_all x1, starting transfers between devices, on_device(): moved_s = lax.all_to_all(packed, 'pix', 0, 0, tiled=True)  10.4 us
    pallas_call x1, Pallas kernels, on_device(): call(temporal_kernel, 2, (whole((4 * frames, 3 * WIDE), BF), whole((64, 9...  8.12 us
  transfers between devices with their start and end apart: 11, of which 7 were waited for; matrix products, arithmetic and copies ran while one was open for 6% of the time, Pallas kernels for 8%

profile of v1, /device:TPU:1, one launch (start us, length us, event | category | flops | bytes accessed | tf_op | source)
XLA Modules:
  0.0 195.4 jit_solution(7603281559728863747)
XLA Ops:
  7.2 1.2 copy.38
  8.4 0.9 pad.17
  9.5 0.9 pad.16
  10.6 1.3 maximum_bitcast_fusion
  11.9 10.5 %all-to-all-start.2 = ((bf16[32,4,3072]{2,1,0:T(4,128)(2,1)}), bf16[32,4,3072]{2,1,0:T(4,128)(2,1)S(1)}, u32[]{:S(2)}, u32[]{:S(2)}) async-start(bf16[32,4,3072]{2,1,0:T(4,128)(2,1)} %maximum_bitcast_fusion), calls=%async_computation.2 | async-start | bytes 1572864 | tf_op jit(solution)/shard_map/temporal_in/all_to_all | solution.py:222
  22.5 2.9 %collective-permute-start = (bf16[64,1152]{1,0:T(8,128)(2,1)S(1)}, bf16[64,1152]{1,0:T(8,128)(2,1)S(1)}, u32[]{:S(2)}, u32[]{:S(2)}) collective-permute-start(bf16[64,1152]{1,0:T(8,128)(2,1)S(1)} %get-tuple-element.54), channel_id=1, source_target_pairs={{0,1},{1,0},{2,3},{3,2},{4,5},{5,4},{6,7},{7,6},{8,9},{9,8},{10,11... | collective-permute-start | bytes 442376 | tf_op jit(solution)/shard_map/spatial_grad_gather/ppermute | solution.py:214
  25.4 1.0 collective-permute-done
  26.4 0.7 pad_maximum_fusion
  27.2 16.3 %all-to-all-done.2 = bf16[32,4,3072]{2,1,0:T(4,128)(2,1)S(1)} async-done(((bf16[32,4,3072]{2,1,0:T(4,128)(2,1)}), bf16[32,4,3072]{2,1,0:T(4,128)(2,1)S(1)}, u32[]{:S(2)}, u32[]{:S(2)}) %all-to-all-start.2) | async-done | bytes 786464 | tf_op jit(solution)/shard_map/temporal_in/all_to_all | solution.py:222
  43.7 1.3 copy-done.5
  45.0 8.1 %temporal_attention.1 = (bf16[128,1920]{1,0:T(8,128)(2,1)S(1)}, bf16[64,5760]{1,0:T(8,128)(2,1)S(1)}, bf16[64,5760]{1,0:T(8,128)(2,1)}) custom-call(s32[1]{0:T(128)} %bitcast.core_ref, bf16[128,3072]{1,0:T(8,128)(2,1)S(1)} %reshape.89.x_ref, bf16[576,1152]{1,0:T(8,128)(2,1)S(1)} %copy-done.5), custom_call_target="tpu_custom_call" | custom-call | flops 1073741824 | bytes 1048576 | tf_op jit(solution)/shard_map/temporal_attention/pallas_call | solution.py:231
  53.1 4.8 %collective-permute-start.3 = (bf16[64,5760]{1,0:T(8,128)(2,1)}, bf16[64,5760]{1,0:T(8,128)(2,1)}, u32[]{:S(2)}, u32[]{:S(2)}) collective-permute-start(bf16[64,5760]{1,0:T(8,128)(2,1)} %get-tuple-element.25), channel_id=1, source_target_pairs={{0,1},{1,0},{2,3},{3,2},{4,5},{5,4},{6,7},{7,6},{8,9},{9,8},{10,11... | collective-permute-start | bytes 2211848 | tf_op jit(solution)/shard_map/temporal_attention/ppermute | solution.py:242
  58.0 1.4 spatial_in.1
  59.3 10.4 %all-to-all-start = ((bf16[16,64,216]{2,1,0:T(8,128)(2,1)}), bf16[16,64,216]{2,1,0:T(8,128)(2,1)S(1)}, u32[]{:S(2)}, u32[]{:S(2)}) async-start(bf16[16,64,216]{2,1,0:T(8,128)(2,1)} %spatial_in.1), calls=%async_computation | async-start | bytes 1048576 | tf_op jit(solution)/shard_map/spatial_in/all_to_all | solution.py:228
  69.7 2.2 %add_convert_fusion = bf16[64,5760]{1,0:T(8,128)(2,1)} fusion(bf16[64,5760]{1,0:T(8,128)(2,1)} %collective-permute-done.3, bf16[64,5760]{1,0:T(8,128)(2,1)S(1)} %get-tuple-element.24), kind=kLoop, calls=%fused_computation | loop fusion | flops 1474560 | bytes 2211840 | tf_op jit(solution)/shard_map/temporal_attention/convert_element_type | solution.py:243
  71.9 2.8 %reshape.94 = bf16[32,2,5760]{2,1,0:T(2,128)(2,1)} reshape(bf16[64,5760]{1,0:T(8,128)(2,1)} %add_convert_fusion) | data formatting | bytes 1474560 | tf_op jit(solution)/shard_map/temporal_attention/reshape | solution.py:243
  74.7 11.7 %all-to-all-done = bf16[16,64,216]{2,1,0:T(8,128)(2,1)S(1)} async-done(((bf16[16,64,216]{2,1,0:T(8,128)(2,1)}), bf16[16,64,216]{2,1,0:T(8,128)(2,1)S(1)}, u32[]{:S(2)}, u32[]{:S(2)}) %all-to-all-start) | async-done | bytes 442400 | tf_op jit(solution)/shard_map/spatial_in/all_to_all | solution.py:228
  86.4 8.1 %all-to-all-start.5 = ((bf16[32,2,5760]{2,1,0:T(2,128)(2,1)}), bf16[32,2,5760]{2,1,0:T(2,128)(2,1)S(1)}, u32[]{:S(2)}, u32[]{:S(2)}) async-start(bf16[32,2,5760]{2,1,0:T(2,128)(2,1)} %reshape.94), calls=%async_computation.5 | async-start | bytes 1474560 | tf_op jit(solution)/shard_map/temporal_projection/all_to_all | solution.py:268
  94.4 0.9 reshape.90
  95.3 19.4 %all-to-all-done.5 = bf16[32,2,5760]{2,1,0:T(2,128)(2,1)S(1)} async-done(((bf16[32,2,5760]{2,1,0:T(2,128)(2,1)}), bf16[32,2,5760]{2,1,0:T(2,128)(2,1)S(1)}, u32[]{:S(2)}, u32[]{:S(2)}) %all-to-all-start.5) | async-done | bytes 737312 | tf_op jit(solution)/shard_map/temporal_projection/all_to_all | solution.py:268
  114.7 6.1 %all-to-all-start.3 = ((bf16[32,4,1920]{2,1,0:T(4,128)(2,1)}), bf16[32,4,1920]{2,1,0:T(4,128)(2,1)}, u32[]{:S(2)}, u32[]{:S(2)}) async-start(bf16[32,4,1920]{2,1,0:T(4,128)(2,1)} %reshape.90), calls=%async_computation.3 | async-start | bytes 983040 | tf_op jit(solution)/shard_map/temporal_out/all_to_all | solution.py:263
  121.0 1.7 copy-done.4
  122.7 6.6 %spatial_attention.1 = (bf16[1024,216]{1,0:T(8,128)(2,1)}, bf16[72,576]{1,0:T(8,128)(2,1)S(1)}, bf16[72,576]{1,0:T(8,128)(2,1)S(1)}) custom-call(s32[1]{0:T(128)} %bitcast.core_ref, bf16[1024,216]{1,0:T(8,128)(2,1)S(1)} %bitcast.39, bf16[1024,1152]{1,0:T(8,128)(2,1)S(1)} %copy-done.4, bf16[128,1152]{1,0:T(8,128)(2,1)S(1)} %pad.14.proj_ref), custom_call_target="tpu_custom_call" | custom-call | flops 4294967296 | bytes 1048576 | tf_op jit(solution)/shard_map/spatial_attention/pallas_call | solution.py:248
  129.3 3.7 %collective-permute-start.1 = (bf16[72,576]{1,0:T(8,128)(2,1)S(1)}, bf16[72,576]{1,0:T(8,128)(2,1)S(1)}, u32[]{:S(2)}, u32[]{:S(2)}) collective-permute-start(bf16[72,576]{1,0:T(8,128)(2,1)S(1)} %get-tuple-element.23), channel_id=1, source_target_pairs={{0,1},{1,0},{2,3},{3,2},{4,5},{5,4},{6,7},{7,6},{8,9},{9,8},{10,11... | collective-permute-start | bytes 248840 | tf_op jit(solution)/shard_map/spatial_attention/ppermute | solution.py:260
  135.3 3.8 %all-to-all-start.6 = ((bf16[8,2,648]{2,1,0:T(2,128)(2,1)}), bf16[8,2,648]{2,1,0:T(2,128)(2,1)S(1)}, u32[]{:S(2)}, u32[]{:S(2)}) async-start(bf16[8,2,648]{2,1,0:T(2,128)(2,1)} %reshape.100), calls=%async_computation.6 | async-start | bytes 49152 | tf_op jit(solution)/shard_map/temporal_projection/all_to_all | solution.py:271
  139.7 6.1 %all-to-all-done.6 = bf16[8,2,648]{2,1,0:T(2,128)(2,1)S(1)} async-done(((bf16[8,2,648]{2,1,0:T(2,128)(2,1)}), bf16[8,2,648]{2,1,0:T(2,128)(2,1)S(1)}, u32[]{:S(2)}, u32[]{:S(2)}) %all-to-all-start.6) | async-done | bytes 20768 | tf_op jit(solution)/shard_map/temporal_projection/all_to_all | solution.py:271
  145.7 17.3 %all_to_all.35 = bf16[32,2,648]{2,1,0:T(2,128)(2,1)S(1)} all-to-all(bf16[32,2,648]{2,1,0:T(2,128)(2,1)S(1)} %reshape.98), channel_id=1, replica_groups=mesh['frame'=32,'pix'=16] {'frame'}, dimensions={0} | all-to-all | bytes 165888 | tf_op jit(solution)/shard_map/spatial_projection/all_to_all | solution.py:276
  163.1 6.3 %all-to-all-start.1 = ((bf16[16,64,216]{2,1,0:T(8,128)(2,1)}), bf16[16,64,216]{2,1,0:T(8,128)(2,1)S(1)}, u32[]{:S(2)}, u32[]{:S(2)}) async-start(bf16[16,64,216]{2,1,0:T(8,128)(2,1)} %bitcast.7), calls=%async_computation.1 | async-start | bytes 1048576 | tf_op jit(solution)/shard_map/spatial_out/all_to_all | solution.py:288
  169.3 1.1 copy.39
  170.4 0.8 fusion
  172.9 13.6 %all-to-all-done.1.x_ref = bf16[16,64,216]{2,1,0:T(8,128)(2,1)S(1)} async-done(((bf16[16,64,216]{2,1,0:T(8,128)(2,1)}), bf16[16,64,216]{2,1,0:T(8,128)(2,1)S(1)}, u32[]{:S(2)}, u32[]{:S(2)}) %all-to-all-start.1) | async-done | bytes 442400 | tf_op jit(solution)/shard_map/spatial_out/all_to_all | solution.py:288
  186.5 1.4 spatial_out.1
  (50 shorter events, 5.8 us)
Async XLA Ops:
  7.2 113.7 %copy-start = (bf16[576,1152]{1,0:T(8,128)(2,1)S(1)}, bf16[576,1152]{1,0:T(8,128)(2,1)}, u32[]{:S(2)}) copy-start(bf16[576,1152]{1,0:T(8,128)(2,1)} %param.16) | copy-start | bytes 3981316
  7.2 3.3 %copy-start.9 = (bf16[2,1,64,576]{3,2,1,0:T(8,128)(2,1)S(1)}, bf16[2,1,64,576]{3,2,1,0:T(8,128)(2,1)}, u32[]{:S(2)}) copy-start(bf16[2,1,64,576]{3,2,1,0:T(8,128)(2,1)} %param.12) | copy-start | bytes 442372
  10.6 11.8 %copy-start.8 = (bf16[2,1,64,1152]{3,2,1,0:T(8,128)(2,1)S(1)}, bf16[2,1,64,1152]{3,2,1,0:T(8,128)(2,1)}, u32[]{:S(2)}) copy-start(bf16[2,1,64,1152]{3,2,1,0:T(8,128)(2,1)} %param.15) | copy-start | bytes 884740
  11.9 31.6 %all-to-all-start.2 = ((bf16[32,4,3072]{2,1,0:T(4,128)(2,1)}), bf16[32,4,3072]{2,1,0:T(4,128)(2,1)S(1)}, u32[]{:S(2)}, u32[]{:S(2)}) async-start(bf16[32,4,3072]{2,1,0:T(4,128)(2,1)} %maximum_bitcast_fusion), calls=%async_computation.2 | async-start | bytes 1572864 | tf_op jit(solution)/shard_map/temporal_in/all_to_all | solution.py:222
  22.4 98.6 %all-gather.2.cloned.1.call-start = ((), (), s32[]{:S(2)}) async-start(), calls=%async_computation.7 | async-start | bytes 2654208 | tf_op jit(solution)/shard_map/spatial_grad_gather/all_gather | solution.py:215
  22.5 3.9 %collective-permute-start = (bf16[64,1152]{1,0:T(8,128)(2,1)S(1)}, bf16[64,1152]{1,0:T(8,128)(2,1)S(1)}, u32[]{:S(2)}, u32[]{:S(2)}) collective-permute-start(bf16[64,1152]{1,0:T(8,128)(2,1)S(1)} %get-tuple-element.54), channel_id=1, source_target_pairs={{0,1},{1,0},{2,3},{3,2},{4,5},{5,4},{6,7},{7,6},{8,9},{9,8},{10,11... | collective-permute-start | bytes 442376 | tf_op jit(solution)/shard_map/spatial_grad_gather/ppermute | solution.py:214
  43.7 1.3 copy-start.5
  45.0 12.9 %copy-start.1 = (bf16[2,1,64,576]{3,2,1,0:T(8,128)(2,1)S(1)}, bf16[2,1,64,576]{3,2,1,0:T(8,128)(2,1)}, u32[]{:S(2)}) copy-start(bf16[2,1,64,576]{3,2,1,0:T(8,128)(2,1)} %param.9) | copy-start | bytes 442372
  45.0 13.0 %copy-start.2 = (bf16[2,1,64,576]{3,2,1,0:T(8,128)(2,1)S(1)}, bf16[2,1,64,576]{3,2,1,0:T(8,128)(2,1)}, u32[]{:S(2)}) copy-start(bf16[2,1,64,576]{3,2,1,0:T(8,128)(2,1)} %param.10) | copy-start | bytes 442372
  45.0 13.0 %copy-start.3 = (bf16[2,1,64,576]{3,2,1,0:T(8,128)(2,1)S(1)}, bf16[2,1,64,576]{3,2,1,0:T(8,128)(2,1)}, u32[]{:S(2)}) copy-start(bf16[2,1,64,576]{3,2,1,0:T(8,128)(2,1)} %param.11) | copy-start | bytes 442372
  53.1 16.6 %collective-permute-start.3 = (bf16[64,5760]{1,0:T(8,128)(2,1)}, bf16[64,5760]{1,0:T(8,128)(2,1)}, u32[]{:S(2)}, u32[]{:S(2)}) collective-permute-start(bf16[64,5760]{1,0:T(8,128)(2,1)} %get-tuple-element.25), channel_id=1, source_target_pairs={{0,1},{1,0},{2,3},{3,2},{4,5},{5,4},{6,7},{7,6},{8,9},{9,8},{10,11... | collective-permute-start | bytes 2211848 | tf_op jit(solution)/shard_map/temporal_attention/ppermute | solution.py:242
  59.3 27.0 %all-to-all-start = ((bf16[16,64,216]{2,1,0:T(8,128)(2,1)}), bf16[16,64,216]{2,1,0:T(8,128)(2,1)S(1)}, u32[]{:S(2)}, u32[]{:S(2)}) async-start(bf16[16,64,216]{2,1,0:T(8,128)(2,1)} %spatial_in.1), calls=%async_computation | async-start | bytes 1048576 | tf_op jit(solution)/shard_map/spatial_in/all_to_all | solution.py:228
  86.4 28.4 %all-to-all-start.5 = ((bf16[32,2,5760]{2,1,0:T(2,128)(2,1)}), bf16[32,2,5760]{2,1,0:T(2,128)(2,1)S(1)}, u32[]{:S(2)}, u32[]{:S(2)}) async-start(bf16[32,2,5760]{2,1,0:T(2,128)(2,1)} %reshape.94), calls=%async_computation.5 | async-start | bytes 1474560 | tf_op jit(solution)/shard_map/temporal_projection/all_to_all | solution.py:268
  114.7 6.2 %copy-start.6 = (bf16[32,2,5760]{2,1,0:T(2,128)(2,1)}, bf16[32,2,5760]{2,1,0:T(2,128)(2,1)S(1)}, u32[]{:S(2)}) copy-start(bf16[32,2,5760]{2,1,0:T(2,128)(2,1)S(1)} %all-to-all-done.5) | copy-start | bytes 2211844
  114.7 20.6 %all-to-all-start.3 = ((bf16[32,4,1920]{2,1,0:T(4,128)(2,1)}), bf16[32,4,1920]{2,1,0:T(4,128)(2,1)}, u32[]{:S(2)}, u32[]{:S(2)}) async-start(bf16[32,4,1920]{2,1,0:T(4,128)(2,1)} %reshape.90), calls=%async_computation.3 | async-start | bytes 983040 | tf_op jit(solution)/shard_map/temporal_out/all_to_all | solution.py:263
  121.0 1.7 copy-start.4
  122.7 10.3 %copy-start.7 = (bf16[32,2,5760]{2,1,0:T(2,128)(2,1)S(1)}, bf16[32,2,5760]{2,1,0:T(2,128)(2,1)}, u32[]{:S(2)}) copy-start(bf16[32,2,5760]{2,1,0:T(2,128)(2,1)} %copy-done.6) | copy-start | bytes 2211844
  129.3 9.8 %collective-permute-start.1 = (bf16[72,576]{1,0:T(8,128)(2,1)S(1)}, bf16[72,576]{1,0:T(8,128)(2,1)S(1)}, u32[]{:S(2)}, u32[]{:S(2)}) collective-permute-start(bf16[72,576]{1,0:T(8,128)(2,1)S(1)} %get-tuple-element.23), channel_id=1, source_target_pairs={{0,1},{1,0},{2,3},{3,2},{4,5},{5,4},{6,7},{7,6},{8,9},{9,8},{10,11... | collective-permute-start | bytes 248840 | tf_op jit(solution)/shard_map/spatial_attention/ppermute | solution.py:260
  135.3 10.4 %all-to-all-start.6 = ((bf16[8,2,648]{2,1,0:T(2,128)(2,1)}), bf16[8,2,648]{2,1,0:T(2,128)(2,1)S(1)}, u32[]{:S(2)}, u32[]{:S(2)}) async-start(bf16[8,2,648]{2,1,0:T(2,128)(2,1)} %reshape.100), calls=%async_computation.6 | async-start | bytes 49152 | tf_op jit(solution)/shard_map/temporal_projection/all_to_all | solution.py:271
  163.1 23.4 %all-to-all-start.1 = ((bf16[16,64,216]{2,1,0:T(8,128)(2,1)}), bf16[16,64,216]{2,1,0:T(8,128)(2,1)S(1)}, u32[]{:S(2)}, u32[]{:S(2)}) async-start(bf16[16,64,216]{2,1,0:T(8,128)(2,1)} %bitcast.7), calls=%async_computation.1 | async-start | bytes 1048576 | tf_op jit(solution)/shard_map/spatial_out/all_to_all | solution.py:288
  171.6 1.3 collective-permute-start.2
Sparse Core Ops, SparseCore 0:
  27.3 45.9 all-gather.1

commit v2 on v1

--- a/solution.py
+++ b/solution.py
@@ -8,9 +8,11 @@
 HSIZE = 72
 HEADS = 8
 HD = 576
-WIDE = 640
 D = 1152
 HALF = 576
+GRADS = 6 * HD
+SUMS_T = 9 * HALF
+SUMS_S = 9 * 2 * HSIZE
 FACTOR = HSIZE ** (-0.5)
 BF = jnp.bfloat16
 F32 = jnp.float32
@@ -58,7 +60,7 @@
         out_specs=[vmem] * len(out_shape) if many else vmem,
         scratch_shapes=list(scratch),
         compiler_params=pltpu.CompilerParams(vmem_limit_bytes=32 * 1024 * 1024),
-        cost_estimate=pl.CostEstimate(flops=flops, bytes_accessed=1 << 20, transcendentals=0),
+        cost_estimate=pl.CostEstimate(flops=flops, bytes_accessed=1, transcendentals=0),
     )
 
 
@@ -87,7 +89,7 @@
                 low = HSIZE * h - start
                 if low >= width or low + HSIZE <= 0:
                     continue
-                pair = jnp.concatenate([x_ref[2 * h], x_ref[2 * h + 1]], 0)
+                pair = jnp.concatenate([x_ref[2 * h], x_ref[2 * h + 1]], 0)[:, : 3 * HSIZE]
                 i, j = iota((3 * HSIZE, width), 0) - HSIZE * a, iota((3 * HSIZE, width), 1)
                 sel = choose((i + low == j) & (i >= 0) & (i < HSIZE))
                 part = dot(pair, sel)
@@ -95,7 +97,7 @@
             ref[:, start : start + width] = total.astype(BF)
 
 
-def spatial_kernel(core_ref, x_ref, g_ref, proj_ref, out_ref, keep_ref, send_ref, dkt_ref, dvt_ref):
+def spatial_kernel(core_ref, x_ref, g_ref, proj_ref, out_ref, part_ref, dkt_ref, dvt_ref, chunk_ref):
     core = core_ref[0]
     rows = x_ref.shape[0]
     pairs = rows // 128
@@ -146,18 +148,42 @@
     out_ref[...] = dot_nt(grads_all, sel).astype(BF)
     out_all = swapped(jnp.concatenate(outs, 0))
     part = dot(out_all.T.astype(BF), g_ref[...]).astype(BF)
-    keep_ref[...] = dot(part, core_columns(core)).astype(BF)[:HSIZE]
-    send_ref[...] = dot(part, core_columns(1 - core)).astype(BF)[:HSIZE]
+    i, j = iota((HSIZE, 128), 0), iota((HSIZE, 128), 1)
+    part = dot(choose(j == 18 * (i % 8 // 2) + 2 * (i // 8) + i % 2), part)
+    wide = 2 * HSIZE
+    for y in range(8):
+        columns = part[:, wide * y : wide * (y + 1)]
+        for b in range(9):
+            chunk_ref[8 * y : 8 * (y + 1), wide * b : wide * (b + 1)] = columns[8 * b : 8 * (b + 1)]
+    part_ref[...] = chunk_ref[...].astype(BF)
+
+
+def pack_time_kernel(q_ref, k_ref, v_ref, g_ref, out_ref):
+    rows, frames = q_ref.shape[0], out_ref.shape[0]
+    group = rows // frames
+    i, j = iota((rows, rows), 0), iota((rows, rows), 1)
+    order = choose(j == frames * (i % group) + i // group)
+    moved = [dot(order, ref[...]).astype(BF) for ref in (q_ref, k_ref, v_ref, g_ref)]
+    moved = jnp.concatenate(moved, 1)
+    for f in range(frames):
+        out_ref[f] = moved[group * f : group * (f + 1)]
+
+
+def merge_kernel(grads_ref, keep_ref, got_ref, part_ref, out_ref):
+    total = (keep_ref[...].astype(F32) + got_ref[...].astype(F32)).astype(BF)
+    for f in range(out_ref.shape[0]):
+        rows = slice(2 * f, 2 * f + 2)
+        out_ref[f, :, :GRADS] = grads_ref[rows]
+        out_ref[f, :, GRADS : GRADS + SUMS_T] = total[rows]
+        out_ref[f, :, GRADS + SUMS_T :] = part_ref[rows]
 
 
 def temporal_kernel(core_ref, x_ref, proj_ref, out_ref, keep_ref, send_ref):
     core = core_ref[0]
     rows = x_ref.shape[0]
     group = 4
-    q = x_ref[:, :HD]
-    k = x_ref[:, WIDE : WIDE + HD]
-    v = x_ref[:, 2 * WIDE : 2 * WIDE + HD]
-    g = x_ref[:, 3 * WIDE :]
+    q, k, v = [x_ref[:, HD * a : HD * (a + 1)] for a in range(3)]
+    g = x_ref[:, 3 * HD :]
     do = dot_nt(g, proj_ref[...]).astype(BF)
     same = iota((rows, rows), 0) % group == iota((rows, rows), 1) % group
     head = iota((1, HD), 1) // HSIZE
@@ -184,17 +210,21 @@
             dot(weights[h].T.astype(BF), dom),
         )
         dq, dk, dv = terms if dq is None else (dq + terms[0], dk + terms[1], dv + terms[2])
-    out_ref[:, :HD] = (dq * FACTOR).astype(BF)
-    out_ref[:, WIDE : WIDE + HD] = (dk * FACTOR).astype(BF)
-    out_ref[:, 2 * WIDE : 2 * WIDE + HD] = dv.astype(BF)
+    i, j = iota((rows, rows), 0), iota((rows, rows), 1)
+    half_rows = rows // 2
+    order = choose(j == group * (i % half_rows // 2) + 2 * (i // half_rows) + i % 2)
+    for a, grad in enumerate((dq * FACTOR, dk * FACTOR, dv)):
+        sorted_rows = dot(order, grad.astype(BF)).astype(BF)
+        for b in range(2):
+            low = HD * (3 * b + a)
+            out_ref[:, low : low + HD] = sorted_rows[half_rows * b : half_rows * (b + 1)]
     i, j = iota((HD, HD), 0), iota((HD, HD), 1)
     order = choose(j == 18 * (i % 64 // 2) + 2 * (i // 64) + i % 2)
     out_t = dot_nt(order, out).astype(BF)
     for ref, half in ((keep_ref, core), (send_ref, 1 - core)):
         part = dot(out_t, dot(g, core_columns(half)).astype(BF)).astype(BF)
-        ref[...] = jnp.zeros(ref.shape, BF)
         for b in range(9):
-            ref[:, WIDE * b : WIDE * b + HALF] = part[64 * b : 64 * b + 64]
+            ref[:, HALF * b : HALF * (b + 1)] = part[64 * b : 64 * b + 64]
 
 
 def on_device(query_s, key_s, value_s, query_t, key_t, value_t, grad_out, proj_s, proj_t):
@@ -217,10 +247,9 @@
         )
 
     with jax.named_scope("temporal_in"):
-        spread = [jnp.pad(a[:, 0], ((0, 0), (0, 0), (0, WIDE - HD))) for a in (query_t, key_t, value_t)]
-        rows = jnp.concatenate(spread + [grad], -1).reshape(4, frames, 3 * WIDE + D)
-        moved_t = lax.all_to_all(rows.transpose(1, 0, 2), "frame", 0, 0, tiled=True)
-        moved_t = moved_t.reshape(4 * frames, 3 * WIDE + D)
+        flat = [a.reshape(128, a.shape[3]) for a in (query_t, key_t, value_t, grad_out)]
+        sent_in = call(pack_time_kernel, 4, whole((frames, 4, 3 * HD + D), BF), 1)(*flat)
+        moved_t = lax.all_to_all(sent_in, "frame", 0, 0, tiled=True).reshape(128, 3 * HD + D)
 
     with jax.named_scope("spatial_in"):
         flat = [a.reshape(128, HD) for a in (query_s, key_s, value_s)]
@@ -231,50 +260,37 @@
         grads_t, keep_t, send_t = call(
             temporal_kernel,
             2,
-            (
-                whole((4 * frames, 3 * WIDE), BF),
-                whole((64, 9 * WIDE), BF),
-                whole((64, 9 * WIDE), BF),
-            ),
-            1 << 30,
+            (whole((64, GRADS), BF), whole((64, SUMS_T), BF), whole((64, SUMS_T), BF)),
+            1,
             scalars=1,
         )(core_arg, moved_t, proj_t)
-        total_t = keep_t.astype(F32) + lax.ppermute(send_t, "pix", core_swap).astype(F32)
-        total_t = total_t.astype(BF).reshape(frames, 2, 9 * WIDE)
-
+        got_t = lax.ppermute(send_t, "pix", core_swap)
     with jax.named_scope("spatial_attention"):
         proj_h = lax.dynamic_slice_in_dim(proj_s, HSIZE * z, HSIZE, 0)
         proj_h = jnp.pad(proj_h, ((0, 128 - HSIZE), (0, 0)))
-        grads_s, keep_s, send_s = call(
+        grads_s, part_s = call(
             spatial_kernel,
             3,
-            (
-                whole((n_pix * 64, 3 * HSIZE), BF),
-                whole((HSIZE, HALF), BF),
-                whole((HSIZE, HALF), BF),
-            ),
-            1 << 32,
+            (whole((n_pix * 64, 3 * HSIZE), BF), whole((2 * frames, SUMS_S), BF)),
+            1,
             scalars=1,
-            scratch=[pltpu.VMEM((128, n_pix * 64), F32)] * 2,
+            scratch=[pltpu.VMEM((128, n_pix * 64), F32)] * 2 + [pltpu.VMEM((2 * frames, SUMS_S), F32)],
         )(core_arg, moved_s.reshape(n_pix * 64, 3 * HSIZE), gathered, proj_h)
-        total_s = keep_s.astype(F32) + lax.ppermute(send_s, "pix", core_swap).astype(F32)
 
     with jax.named_scope("temporal_out"):
-        home_t = lax.all_to_all(grads_t.reshape(frames, 4, 3 * WIDE), "frame", 0, 0, tiled=True)
-        home_t = home_t.transpose(1, 0, 2).reshape(2, 1, 64, 3 * WIDE)
-        outs_t = [home_t[..., WIDE * a : WIDE * a + HD] for a in range(3)]
-
-    with jax.named_scope("temporal_projection"):
-        parts_t = lax.all_to_all(total_t, "frame", 0, 0, tiled=True)
-        sums_t = parts_t.astype(F32).sum(0).astype(BF).reshape(2, 9, WIDE)[..., :HALF]
-        sums_t = sums_t.reshape(2, 9, n_z, HSIZE).transpose(2, 1, 0, 3).reshape(n_z, 18, HSIZE)
-        last_t = lax.all_to_all(sums_t, "pix", 0, 0, axis_index_groups=same_core, tiled=True)
-        proj_t_grad = last_t.astype(F32).sum(0)
+        sent_out = call(merge_kernel, 4, whole((frames, 2, GRADS + SUMS_T + SUMS_S), BF), 1)(
+            grads_t, keep_t, got_t, part_s
+        )
+        home_t = lax.all_to_all(sent_out, "frame", 0, 0, tiled=True)
+        back = home_t[..., :GRADS].reshape(frames, 2, 2, 3, HD).transpose(3, 2, 1, 0, 4)
+        outs_t = [back[a].reshape(2, 1, 64, HD) for a in range(3)]
 
     with jax.named_scope("spatial_projection"):
-        chunks = total_s.astype(BF).reshape(4, 18, 8, HSIZE).transpose(2, 0, 1, 3)
-        parts_s = lax.all_to_all(chunks.reshape(frames, 18, HSIZE), "frame", 0, 0, tiled=True)
-        sums_s = parts_s.astype(F32).sum(0)
+        sums_s = home_t[..., GRADS + SUMS_T :].astype(F32).sum(0).reshape(2, 9, 2, HSIZE)
+        sums_s = sums_s.transpose(2, 1, 0, 3).reshape(2, 18, HSIZE)
+        own_s = lax.dynamic_index_in_dim(sums_s, core, 0, keepdims=False)
+        other_s = lax.dynamic_index_in_dim(sums_s, 1 - core, 0, keepdims=False)
+        sums_s = own_s + lax.ppermute(other_s, "pix", core_swap)
         perm = []
         for y in range(8):
             for x in range(4):
@@ -284,10 +300,20 @@
                         perm.append((source, (zz * 4 + x) * n_pix + 2 * y + c))
         proj_s_grad = lax.ppermute(sums_s, ("frame", "pix"), perm)
 
+    with jax.named_scope("temporal_projection"):
+        sums_t = home_t[..., GRADS : GRADS + SUMS_T].astype(F32).sum(0).astype(BF)
+        sums_t = sums_t.reshape(2, 9, n_z, HSIZE).transpose(2, 1, 0, 3).reshape(n_z, 36, 36)
+        sums_t = jnp.pad(sums_t, ((0, 0), (0, 28), (0, 0)))
+        sums_t = jnp.broadcast_to(sums_t[:, None], (n_z, 2, 64, 36)).reshape(n_pix, 64, 36)
+
     with jax.named_scope("spatial_out"):
-        home_s = lax.all_to_all(grads_s.reshape(n_pix, 64, 3 * HSIZE), "pix", 0, 0, tiled=True)
+        sent = jnp.concatenate([grads_s.reshape(n_pix, 64, 3 * HSIZE), sums_t], 2)
+        home_s = lax.all_to_all(sent, "pix", 0, 0, tiled=True)
         outs_s = call(unpack_kernel, 1, (whole((128, HD), BF),) * 3, 1 << 26)(home_s)
         outs_s = [a.reshape(2, 1, 64, HD) for a in outs_s]
+        last_t = home_s[:, :36, 3 * HSIZE :].reshape(n_z, 2, 36, 36)
+        last_t = lax.dynamic_index_in_dim(last_t, core, 1, keepdims=False)
+        proj_t_grad = last_t.astype(F32).sum(0).reshape(18, HSIZE)
 
     return (*outs_s, *outs_t, proj_s_grad, proj_t_grad)
 

time: 196 us -> 161 us (0.82)
  waiting for transfers between devices: 68.8 us -> 34.6 us
  blocking collectives: 17.3 us -> 39.2 us
  starting transfers between devices: 57.2 us -> 36.9 us
  other arithmetic: 5.53 us -> 2.63 us
  Pallas kernels: 17.5 us -> 20.4 us
  local copies, waits for them, and re-layouts: 14.6 us -> 11.9 us
    all_to_all x5 -> x2, waiting for transfers between devices: 56 us -> 29.6 us  [the longest x1 19.3 us: on_device(): lax.all_to_all(sent_in, 'frame', 0, 0, tiled=True).reshape(128, 3 * HD + D)]
    all_to_all x5 -> x2, starting transfers between devices: 34.7 us -> 10.1 us  [the longest x1 5.81 us: on_device(): home_s = lax.all_to_all(sent, 'pix', 0, 0, tiled=True)]
    all_to_all x1, blocking collectives: 17.3 us -> 39.2 us  [on_device(): home_t = lax.all_to_all(sent_out, 'frame', 0, 0, tiled=True)]
    all_to_all x1, waiting for transfers between devices: 11.7 us -> 3.98 us  [on_device(): moved_s = lax.all_to_all(packed, 'pix', 0, 0, tiled=True)]
    ppermute x1, starting transfers between devices: 2.86 us -> 8.79 us  [on_device(): other = lax.ppermute(other, 'pix', core_swap)]
    ppermute x2, starting transfers between devices: 8.49 us -> 4.2 us  [the longest x1 2.19 us: on_device(): got_t = lax.ppermute(send_t, 'pix', core_swap)]
    pallas_call x2 -> x4, Pallas kernels: 14.7 us -> 17.7 us  [the longest x1 8.45 us: on_device(): call(temporal_kernel, 2, (whole((64, GRADS), BF), whole((64, SUMS_T), BF)...]
    all_to_all x1, starting transfers between devices: 10.4 us -> 13.2 us  [on_device(): moved_s = lax.all_to_all(packed, 'pix', 0, 0, tiled=True)]
  transfers between devices with their start and end apart: 11 -> 8, of which waited for: 7 -> 4; matrix products, arithmetic and copies ran while one was open for 6% -> 3% of each run, Pallas kernels for 8% -> 11%
where the time goes in v2:
time: 161 us; the launch traced here: 160 us
  blocking collectives  39.2 us (24%)
  starting transfers between devices  36.9 us (23%)
  waiting for transfers between devices  34.6 us (21%)
  Pallas kernels  20.4 us (13%)
  between operations  14.4 us (9%)
  local copies, waits for them, and re-layouts  11.9 us (7%)
  other arithmetic  2.63 us (2%)
    all_to_all x1, blocking collectives, on_device(): home_t = lax.all_to_all(sent_out, 'frame', 0, 0, tiled=True)  39.2 us
    all_to_all x1, waiting for transfers between devices, on_device(): lax.all_to_all(sent_in, 'frame', 0, 0, tiled=True).reshape(128, 3 * HD + D)  19.3 us
    all_to_all x1, starting transfers between devices, on_device(): moved_s = lax.all_to_all(packed, 'pix', 0, 0, tiled=True)  13.2 us
    all_to_all x1, waiting for transfers between devices, on_device(): home_s = lax.all_to_all(sent, 'pix', 0, 0, tiled=True)  10.3 us
    ppermute x1, starting transfers between devices, on_device(): other = lax.ppermute(other, 'pix', core_swap)  8.79 us
    pallas_call x1, Pallas kernels, on_device(): call(temporal_kernel, 2, (whole((64, GRADS), BF), whole((64, SUMS_T), BF)...  8.45 us
    pallas_call x1, Pallas kernels, on_device(): call(spatial_kernel, 3, (whole((n_pix * 64, 3 * HSIZE), BF), whole((2 * f...  6.1 us
    all_to_all x1, starting transfers between devices, on_device(): home_s = lax.all_to_all(sent, 'pix', 0, 0, tiled=True)  5.81 us
  transfers between devices with their start and end apart: 8, of which 4 were waited for; matrix products, arithmetic and copies ran while one was open for 3% of the time, Pallas kernels for 11%

profile of v2, /device:TPU:1, one launch (start us, length us, event | category | flops | bytes accessed | tf_op | source)
XLA Modules:
  0.0 160.0 jit_solution(6412552131023335144)
XLA Ops:
  7.3 1.1 dynamic-slice_bitcast_fusion.1
  8.4 8.8 %collective-permute-start = (bf16[64,1152]{1,0:T(8,128)(2,1)S(1)}, bf16[64,1152]{1,0:T(8,128)(2,1)S(1)}, u32[]{:S(2)}, u32[]{:S(2)}) collective-permute-start(bf16[64,1152]{1,0:T(8,128)(2,1)S(1)} %get-tuple-element.52), channel_id=1, source_target_pairs={{0,1},{1,0},{2,3},{3,2},{4,5},{5,4},{6,7},{7,6},{8,9},{9,8},{10,11... | collective-permute-start | bytes 442376 | tf_op jit(solution)/shard_map/spatial_grad_gather/ppermute | solution.py:244
  17.2 1.0 collective-permute-done
  18.2 0.7 pad_maximum_fusion.1
  19.0 1.3 temporal_in.1
  20.4 4.3 %all-to-all-start.1 = ((bf16[32,4,2880]{2,1,0:T(4,128)(2,1)}), bf16[32,4,2880]{2,1,0:T(4,128)(2,1)S(1)}, u32[]{:S(2)}, u32[]{:S(2)}) async-start(bf16[32,4,2880]{2,1,0:T(4,128)(2,1)} %temporal_in.1), calls=%async_computation.1 | async-start | bytes 1507328 | tf_op jit(solution)/shard_map/temporal_in/all_to_all | solution.py:252
  24.7 1.4 spatial_in.1
  26.1 19.3 %all-to-all-done.1 = bf16[32,4,2880]{2,1,0:T(4,128)(2,1)S(1)} async-done(((bf16[32,4,2880]{2,1,0:T(4,128)(2,1)}), bf16[32,4,2880]{2,1,0:T(4,128)(2,1)S(1)}, u32[]{:S(2)}, u32[]{:S(2)}) %all-to-all-start.1) | async-done | bytes 737312 | tf_op jit(solution)/shard_map/temporal_in/all_to_all | solution.py:252
  45.3 13.2 %all-to-all-start = ((bf16[16,64,216]{2,1,0:T(8,128)(2,1)}), bf16[16,64,216]{2,1,0:T(8,128)(2,1)S(1)}, u32[]{:S(2)}, u32[]{:S(2)}) async-start(bf16[16,64,216]{2,1,0:T(8,128)(2,1)} %spatial_in.1), calls=%async_computation | async-start | bytes 1048576 | tf_op jit(solution)/shard_map/spatial_in/all_to_all | solution.py:257
  58.9 1.3 copy-done.2
  60.2 8.4 %temporal_attention.1 = (bf16[64,3456]{1,0:T(8,128)(2,1)S(1)}, bf16[64,5184]{1,0:T(8,128)(2,1)S(1)}, bf16[64,5184]{1,0:T(8,128)(2,1)}) custom-call(s32[1]{0:T(128)} %bitcast.core_ref, bf16[128,2880]{1,0:T(8,128)(2,1)S(1)} %reshape.98.x_ref, bf16[576,1152]{1,0:T(8,128)(2,1)S(1)} %copy-done.2), custom_call_target="tpu_custom_call" | custom-call | flops 1 | bytes 1 | tf_op jit(solution)/shard_map/temporal_attention/pallas_call | solution.py:260
  68.6 0.8 copy-done.6
  69.4 2.2 %collective-permute-start.1 = (bf16[64,5184]{1,0:T(8,128)(2,1)}, bf16[64,5184]{1,0:T(8,128)(2,1)}, u32[]{:S(2)}, u32[]{:S(2)}) collective-permute-start(bf16[64,5184]{1,0:T(8,128)(2,1)} %get-tuple-element.19), channel_id=1, source_target_pairs={{0,1},{1,0},{2,3},{3,2},{4,5},{5,4},{6,7},{7,6},{8,9},{9,8},{10,11... | collective-permute-start | bytes 1990664 | tf_op jit(solution)/shard_map/temporal_attention/ppermute | solution.py:267
  71.7 4.0 %all-to-all-done = bf16[16,64,216]{2,1,0:T(8,128)(2,1)S(1)} async-done(((bf16[16,64,216]{2,1,0:T(8,128)(2,1)}), bf16[16,64,216]{2,1,0:T(8,128)(2,1)S(1)}, u32[]{:S(2)}, u32[]{:S(2)}) %all-to-all-start) | async-done | bytes 442400 | tf_op jit(solution)/shard_map/spatial_in/all_to_all | solution.py:257
  75.7 1.7 %copy-done.1 = bf16[1024,1152]{1,0:T(8,128)(2,1)S(1)} copy-done((bf16[1024,1152]{1,0:T(8,128)(2,1)S(1)}, bf16[1024,1152]{1,0:T(8,128)(2,1)}, u32[]{:S(2)}) %copy-start.1) | copy-done | bytes 2359320
  77.3 6.1 %spatial_attention.1 = (bf16[1024,216]{1,0:T(8,128)(2,1)S(1)}, bf16[64,1296]{1,0:T(8,128)(2,1)S(1)}) custom-call(s32[1]{0:T(128)} %bitcast.core_ref, bf16[1024,216]{1,0:T(8,128)(2,1)S(1)} %bitcast.45, bf16[1024,1152]{1,0:T(8,128)(2,1)S(1)} %copy-done.1, bf16[128,1152]{1,0:T(8,128)(2,1)S(1)} %pad.8.proj_ref), custom_call_target="tpu_custom_call" | custom-call | flops 1 | bytes 1 | tf_op jit(solution)/shard_map/spatial_attention/pallas_call | solution.py:271
  83.4 0.8 copy-done.4
  84.2 1.8 %temporal_out.1 = bf16[32,2,9936]{2,1,0:T(2,128)(2,1)S(1)} custom-call(bf16[64,3456]{1,0:T(8,128)(2,1)S(1)} %copy-done.7, bf16[64,5184]{1,0:T(8,128)(2,1)S(1)} %get-tuple-element.18.keep_ref, bf16[64,5184]{1,0:T(8,128)(2,1)} %collective-permute-done.1.got_ref, bf16[64,1296]{1,0:T(8,128)(2,1)S(1)} %get-tuple-element.20.part_ref), custom_call_target="tpu_custom_call" | custom-call | flops 1 | bytes 1 | tf_op jit(solution)/shard_map/temporal_out/pallas_call | solution.py:281
  86.0 39.2 %all_to_all.20 = bf16[32,2,9936]{2,1,0:T(2,128)(2,1)S(1)} all-to-all(bf16[32,2,9936]{2,1,0:T(2,128)(2,1)S(1)} %temporal_out.1), channel_id=1, replica_groups=mesh['frame'=32,'pix'=16] {'frame'}, dimensions={0} | all-to-all | bytes 2543616 | tf_op jit(solution)/shard_map/temporal_out/all_to_all | solution.py:284
  126.2 1.0 pad_maximum_fusion
  127.2 5.8 %all-to-all-start.3 = ((bf16[16,64,252]{2,1,0:T(8,128)(2,1)}), bf16[16,64,252]{2,1,0:T(8,128)(2,1)S(1)}, u32[]{:S(2)}, u32[]{:S(2)}) async-start(bf16[16,64,252]{2,1,0:T(8,128)(2,1)} %pad_maximum_fusion), calls=%async_computation.3 | async-start | bytes 1048576 | tf_op jit(solution)/shard_map/spatial_out/all_to_all | solution.py:311
  133.5 2.0 %collective-permute-start.2 = (f32[18,72]{1,0:T(8,128)S(1)}, f32[18,72]{1,0:T(8,128)S(1)}, u32[]{:S(2)}, u32[]{:S(2)}) collective-permute-start(f32[18,72]{1,0:T(8,128)S(1)} %bitcast.63), channel_id=1, source_target_pairs={{0,1},{1,0},{2,3},{3,2},{4,5},{5,4},{6,7},{7,6},{8,9},{9,8},{10,11... | collective-permute-start | bytes 15560 | tf_op jit(solution)/shard_map/spatial_projection/ppermute | solution.py:293
  135.9 0.7 reshape.105
  136.6 0.7 collective-permute-start.3
  137.3 0.7 fusion
  138.0 0.7 copy.36
  138.6 0.7 copy.35
  139.3 0.7 copy.34
  140.0 10.3 %all-to-all-done.3.x_ref = bf16[16,64,252]{2,1,0:T(8,128)(2,1)S(1)} async-done(((bf16[16,64,252]{2,1,0:T(8,128)(2,1)}), bf16[16,64,252]{2,1,0:T(8,128)(2,1)S(1)}, u32[]{:S(2)}, u32[]{:S(2)}) %all-to-all-start.3) | async-done | bytes 516128 | tf_op jit(solution)/shard_map/spatial_out/all_to_all | solution.py:311
  150.5 0.7 reshape.109
  151.2 1.4 spatial_out.1
  152.6 0.6 copy.50
  (49 shorter events, 2.5 us)
Async XLA Ops:
  7.2 64.4 %copy-start = (bf16[576,1152]{1,0:T(8,128)(2,1)S(1)}, bf16[576,1152]{1,0:T(8,128)(2,1)}, u32[]{:S(2)}) copy-start(bf16[576,1152]{1,0:T(8,128)(2,1)} %param.16) | copy-start | bytes 3981316
  7.2 11.8 %copy-start.3 = (bf16[2,1,64,1152]{3,2,1,0:T(8,128)(2,1)S(1)}, bf16[2,1,64,1152]{3,2,1,0:T(8,128)(2,1)}, u32[]{:S(2)}) copy-start(bf16[2,1,64,1152]{3,2,1,0:T(8,128)(2,1)} %param.15) | copy-start | bytes 884740
  7.2 11.8 %copy-start.10 = (bf16[2,1,64,576]{3,2,1,0:T(8,128)(2,1)S(1)}, bf16[2,1,64,576]{3,2,1,0:T(8,128)(2,1)}, u32[]{:S(2)}) copy-start(bf16[2,1,64,576]{3,2,1,0:T(8,128)(2,1)} %param.14) | copy-start | bytes 442372
  7.2 11.8 %copy-start.9 = (bf16[2,1,64,576]{3,2,1,0:T(8,128)(2,1)S(1)}, bf16[2,1,64,576]{3,2,1,0:T(8,128)(2,1)}, u32[]{:S(2)}) copy-start(bf16[2,1,64,576]{3,2,1,0:T(8,128)(2,1)} %param.13) | copy-start | bytes 442372
  7.2 11.8 %copy-start.8 = (bf16[2,1,64,576]{3,2,1,0:T(8,128)(2,1)S(1)}, bf16[2,1,64,576]{3,2,1,0:T(8,128)(2,1)}, u32[]{:S(2)}) copy-start(bf16[2,1,64,576]{3,2,1,0:T(8,128)(2,1)} %param.12) | copy-start | bytes 442372
  7.2 68.4 %all-gather.2.cloned.1.call-start = ((), (), s32[]{:S(2)}) async-start(), calls=%async_computation.4 | async-start | bytes 2654208 | tf_op jit(solution)/shard_map/spatial_grad_gather/all_gather | solution.py:245
  8.4 9.8 %collective-permute-start = (bf16[64,1152]{1,0:T(8,128)(2,1)S(1)}, bf16[64,1152]{1,0:T(8,128)(2,1)S(1)}, u32[]{:S(2)}, u32[]{:S(2)}) collective-permute-start(bf16[64,1152]{1,0:T(8,128)(2,1)S(1)} %get-tuple-element.52), channel_id=1, source_target_pairs={{0,1},{1,0},{2,3},{3,2},{4,5},{5,4},{6,7},{7,6},{8,9},{9,8},{10,11... | collective-permute-start | bytes 442376 | tf_op jit(solution)/shard_map/spatial_grad_gather/ppermute | solution.py:244
  19.0 5.7 %copy-start.11 = (bf16[2,1,64,576]{3,2,1,0:T(8,128)(2,1)S(1)}, bf16[2,1,64,576]{3,2,1,0:T(8,128)(2,1)}, u32[]{:S(2)}) copy-start(bf16[2,1,64,576]{3,2,1,0:T(8,128)(2,1)} %param.9) | copy-start | bytes 442372
  19.0 5.7 %copy-start.12 = (bf16[2,1,64,576]{3,2,1,0:T(8,128)(2,1)S(1)}, bf16[2,1,64,576]{3,2,1,0:T(8,128)(2,1)}, u32[]{:S(2)}) copy-start(bf16[2,1,64,576]{3,2,1,0:T(8,128)(2,1)} %param.10) | copy-start | bytes 442372
  19.0 5.7 %copy-start.13 = (bf16[2,1,64,576]{3,2,1,0:T(8,128)(2,1)S(1)}, bf16[2,1,64,576]{3,2,1,0:T(8,128)(2,1)}, u32[]{:S(2)}) copy-start(bf16[2,1,64,576]{3,2,1,0:T(8,128)(2,1)} %param.11) | copy-start | bytes 442372
  20.4 24.9 %all-to-all-start.1 = ((bf16[32,4,2880]{2,1,0:T(4,128)(2,1)}), bf16[32,4,2880]{2,1,0:T(4,128)(2,1)S(1)}, u32[]{:S(2)}, u32[]{:S(2)}) async-start(bf16[32,4,2880]{2,1,0:T(4,128)(2,1)} %temporal_in.1), calls=%async_computation.1 | async-start | bytes 1507328 | tf_op jit(solution)/shard_map/temporal_in/all_to_all | solution.py:252
  45.3 30.3 %all-to-all-start = ((bf16[16,64,216]{2,1,0:T(8,128)(2,1)}), bf16[16,64,216]{2,1,0:T(8,128)(2,1)S(1)}, u32[]{:S(2)}, u32[]{:S(2)}) async-start(bf16[16,64,216]{2,1,0:T(8,128)(2,1)} %spatial_in.1), calls=%async_computation | async-start | bytes 1048576 | tf_op jit(solution)/shard_map/spatial_in/all_to_all | solution.py:257
  58.8 1.3 copy-start.2
  68.6 0.8 copy-start.6
  69.4 14.9 %collective-permute-start.1 = (bf16[64,5184]{1,0:T(8,128)(2,1)}, bf16[64,5184]{1,0:T(8,128)(2,1)}, u32[]{:S(2)}, u32[]{:S(2)}) collective-permute-start(bf16[64,5184]{1,0:T(8,128)(2,1)} %get-tuple-element.19), channel_id=1, source_target_pairs={{0,1},{1,0},{2,3},{3,2},{4,5},{5,4},{6,7},{7,6},{8,9},{9,8},{10,11... | collective-permute-start | bytes 1990664 | tf_op jit(solution)/shard_map/temporal_attention/ppermute | solution.py:267
  75.7 1.7 %copy-start.1 = (bf16[1024,1152]{1,0:T(8,128)(2,1)S(1)}, bf16[1024,1152]{1,0:T(8,128)(2,1)}, u32[]{:S(2)}) copy-start(bf16[1024,1152]{1,0:T(8,128)(2,1)} %all-gather.2.cloned.1.call-done.g_ref) | copy-start | bytes 7077892
  77.3 6.9 %copy-start.7 = (bf16[64,3456]{1,0:T(8,128)(2,1)S(1)}, bf16[64,3456]{1,0:T(8,128)(2,1)}, u32[]{:S(2)}) copy-start(bf16[64,3456]{1,0:T(8,128)(2,1)} %copy-done.6) | copy-start | bytes 1327108
  83.4 0.8 copy-start.4
  125.2 1.0 copy-start.5
  127.2 23.1 %all-to-all-start.3 = ((bf16[16,64,252]{2,1,0:T(8,128)(2,1)}), bf16[16,64,252]{2,1,0:T(8,128)(2,1)S(1)}, u32[]{:S(2)}, u32[]{:S(2)}) async-start(bf16[16,64,252]{2,1,0:T(8,128)(2,1)} %pad_maximum_fusion), calls=%async_computation.3 | async-start | bytes 1048576 | tf_op jit(solution)/shard_map/spatial_out/all_to_all | solution.py:311
  133.5 3.1 %collective-permute-start.2 = (f32[18,72]{1,0:T(8,128)S(1)}, f32[18,72]{1,0:T(8,128)S(1)}, u32[]{:S(2)}, u32[]{:S(2)}) collective-permute-start(f32[18,72]{1,0:T(8,128)S(1)} %bitcast.63), channel_id=1, source_target_pairs={{0,1},{1,0},{2,3},{3,2},{4,5},{5,4},{6,7},{7,6},{8,9},{9,8},{10,11... | collective-permute-start | bytes 15560 | tf_op jit(solution)/shard_map/spatial_projection/ppermute | solution.py:293
  136.6 3.4 %collective-permute-start.3 = (f32[18,72]{1,0:T(8,128)S(1)}, f32[18,72]{1,0:T(8,128)S(1)}, u32[]{:S(2)}, u32[]{:S(2)}) collective-permute-start(f32[18,72]{1,0:T(8,128)S(1)} %bitcast_add_fusion), channel_id=1, source_target_pairs={{0,0},{1,1},{2,64},{3,65},{4,128},{5,129},{6,192},{7,193},{8,256},... | collective-permute-start | bytes 15560 | tf_op jit(solution)/shard_map/spatial_projection/ppermute | solution.py:301
Sparse Core Ops, SparseCore 0:
  19.1 40.7 all-gather.1

commit v3 on v2

v3 whole, which is shorter than its diff:
```python
import jax
import jax.numpy as jnp
from jax import lax
from jax.experimental import pallas as pl
from jax.experimental.pallas import tpu as pltpu
from jax.sharding import PartitionSpec as P

HSIZE = 72
HEADS = 8
HD = 576
D = 1152
HALF = 576
GRADS = 6 * HD
SUMS_T = 9 * HALF
SUMS_S = 9 * 2 * HSIZE
THREE = 3 * HSIZE
FACTOR = HSIZE ** (-0.5)
BF = jnp.bfloat16
F32 = jnp.float32


def dot(a, b):
    return lax.dot_general(a, b, (((1,), (0,)), ((), ())), preferred_element_type=F32)


def dot_nt(a, b):
    return lax.dot_general(a, b, (((1,), (1,)), ((), ())), preferred_element_type=F32)


def iota(shape, dim):
    return lax.broadcasted_iota(jnp.int32, shape, dim)


def choose(cond):
    return jnp.where(cond, 1.0, 0.0).astype(BF)


def window(h):
    start = (HSIZE * h) // 128 * 128
    return start, min(256, HD - start), HSIZE * h - start


def core_columns(core):
    col = iota((D, HALF), 1)
    z = col // HSIZE
    return choose(iota((D, HALF), 0) == col + HSIZE * z + HSIZE * core)


def whole(shape, dtype):
    return jax.ShapeDtypeStruct(shape, dtype)


def call(kernel, n_in, out_shape, scalars=0, scratch=(), anywhere=0, mib=32):
    many = isinstance(out_shape, (tuple, list))
    vmem = pl.BlockSpec(memory_space=pltpu.VMEM)
    source = pl.BlockSpec(memory_space=pl.ANY)
    smem = pl.BlockSpec(memory_space=pltpu.SMEM)
    return pl.pallas_call(
        kernel,
        out_shape=out_shape,
        in_specs=[smem] * scalars + [vmem] * n_in + [source] * anywhere,
        out_specs=[vmem] * len(out_shape) if many else vmem,
        scratch_shapes=list(scratch),
        compiler_params=pltpu.CompilerParams(vmem_limit_bytes=mib * 1024 * 1024),
        cost_estimate=pl.CostEstimate(flops=1, bytes_accessed=1, transcendentals=0),
    )


def pack_kernel(q_ref, k_ref, v_ref, out_ref):
    for h in range(HEADS):
        start, width, offset = window(h)
        total = None
        for a, ref in enumerate((q_ref, k_ref, v_ref)):
            i, j = iota((width, 256), 0), iota((width, 256), 1) - HSIZE * a
            sel = choose((i - offset == j) & (j >= 0) & (j < HSIZE))
            part = dot(ref[:, start : start + width], sel)
            total = part if total is None else total + part
        total = total.astype(BF)[:, :THREE]
        for c in range(2):
            for n in range(4):
                low = 64 * c + 16 * n
                out_ref[2 * h + c, :, THREE * n : THREE * (n + 1)] = total[low : low + 16]


def ride_kernel(home_ref, grads_ref, out_ref, rows_ref):
    out_ref[...] = grads_ref[...]
    total = None
    for f in range(home_ref.shape[0]):
        part = home_ref[f, :, GRADS : GRADS + SUMS_T].astype(F32)
        total = part if total is None else total + part
    for z in range(out_ref.shape[0] // 2):
        for b in range(9):
            low = HALF * b + HSIZE * z
            rows_ref[z, 2 * b : 2 * b + 2] = total[:, low : low + HSIZE]
        for n in range(2):
            half = rows_ref[z, :, 36 * n : 36 * (n + 1)].astype(BF)
            for c in range(2):
                out_ref[2 * z + c, 32 * n : 32 * n + 18, THREE:] = half


def unpack_kernel(place_ref, x_ref, dq_ref, dk_ref, dv_ref, sum_ref):
    core = place_ref[0]
    for n in range(2):
        total = None
        for z in range(x_ref.shape[0] // 2):
            part = x_ref[2 * z + core, 32 * n : 32 * n + 18, THREE:].astype(F32)
            total = part if total is None else total + part
        sum_ref[:, 36 * n : 36 * (n + 1)] = total
    for a, ref in enumerate((dq_ref, dk_ref, dv_ref)):
        for start in range(0, HD, 128):
            width = min(128, HD - start)
            total = None
            for h in range(HEADS):
                low = HSIZE * h - start
                if low >= width or low + HSIZE <= 0:
                    continue
                pair = jnp.concatenate([x_ref[2 * h], x_ref[2 * h + 1]], 0)[:, :THREE]
                i, j = iota((THREE, width), 0) - HSIZE * a, iota((THREE, width), 1)
                sel = choose((i + low == j) & (i >= 0) & (i < HSIZE))
                part = dot(pair, sel)
                total = part if total is None else total + part
            ref[:, start : start + width] = total.astype(BF)


def split_heads(x_ref):
    sources, tall = x_ref.shape[0], x_ref.shape[1]
    i, j = iota((THREE, 384), 0), iota((THREE, 384), 1)
    sel = choose((i == HSIZE * (j // 128) + j % 128) & (j % 128 < HSIZE))
    blocks = [
        dot(x_ref[:, :, THREE * n : THREE * (n + 1)].reshape(sources * tall, THREE), sel)
        for n in range(x_ref.shape[2] // THREE)
    ]
    keys = jnp.concatenate([part[:, 128:256] for part in blocks], 0).astype(BF)
    values = jnp.concatenate([part[:, 256:] for part in blocks], 0).astype(BF)
    return sel, blocks, keys, values


def attend_block(queries, keys, values):
    scores = dot_nt(queries.astype(BF), keys) * FACTOR
    e = jnp.exp(scores - scores.max(-1, keepdims=True))
    inverse = 1.0 / e.sum(-1, keepdims=True)
    return e, inverse, (dot(e.astype(BF), values) * inverse).astype(BF)


def forward_kernel(
    place_ref, x_ref, got_ref, grads_any, g_any, keep_any, out_ref, chunk_ref, g_ref, keep_ref, sems
):
    core = place_ref[0]
    copies = [
        pltpu.make_async_copy(keep_any, keep_ref, sems.at[0]),
        pltpu.make_async_copy(g_any, g_ref, sems.at[1]),
        pltpu.make_async_copy(grads_any, out_ref.at[:, :, :GRADS], sems.at[2]),
    ]
    for copy in copies:
        copy.start()
    n_z = g_ref.shape[0]
    _, blocks, keys, values = split_heads(x_ref)
    pairs = []
    for part in blocks:
        out = attend_block(part[:, :128], keys, values)[2].astype(F32)
        pairs.append(out.reshape(n_z, 2, 16, 128))
    copies[0].wait()
    total = (keep_ref[...].astype(F32) + got_ref[...].astype(F32)).astype(BF)
    for f in range(out_ref.shape[0]):
        rows = slice(2 * f, 2 * f + 2)
        out_ref[f, :, GRADS : GRADS + SUMS_T] = total[rows]
    even = jnp.concatenate([pair[:, 0] for pair in pairs], 1)
    odd = jnp.concatenate([pair[:, 1] for pair in pairs], 1)
    sums = None
    copies[1].wait()
    for n, tokens in enumerate((jnp.where(core == 0, even, odd), jnp.where(core == 0, odd, even))):
        rows = n_z * 64
        term = dot(tokens.reshape(rows, 128).T.astype(BF), g_ref[:, n].reshape(rows, D))
        sums = term if sums is None else sums + term
    i, j = iota((HSIZE, 128), 0), iota((HSIZE, 128), 1)
    sums = dot(choose(j == 18 * (i % 8 // 2) + 2 * (i // 8) + i % 2), sums.astype(BF))
    wide = 2 * HSIZE
    for y in range(8):
        columns = sums[:, wide * y : wide * (y + 1)]
        for b in range(9):
            chunk_ref[8 * y : 8 * (y + 1), wide * b : wide * (b + 1)] = columns[8 * b : 8 * (b + 1)]
    chunks = chunk_ref[...].astype(BF)
    for f in range(out_ref.shape[0]):
        out_ref[f, :, GRADS + SUMS_T :] = chunks[2 * f : 2 * f + 2]
    copies[2].wait()


def backward_kernel(place_ref, x_ref, g_ref, proj_ref, out_ref, dkt_ref, dvt_ref):
    core = place_ref[0]
    n_z = g_ref.shape[0]
    sel, blocks, keys, values = split_heads(x_ref)
    own, other = [
        dot_nt(g_ref[:, n].reshape(n_z * 64, D), proj_ref[...]).reshape(n_z, 64, 128)
        for n in range(2)
    ]
    even, odd = jnp.where(core == 0, own, other), jnp.where(core == 0, other, own)
    grads = jnp.concatenate([even[:, None], odd[:, None]], 1).astype(BF).astype(F32)
    step = 2 * n_z * 16
    dqs = []
    for n, part in enumerate(blocks):
        q, do = part[:, :128], grads[:, :, 16 * n : 16 * (n + 1)].reshape(step, 128)
        e, inverse, out = attend_block(q, keys, values)
        weights = e * inverse
        delta = (do * out.astype(F32)).sum(-1, keepdims=True)
        dprob = dot_nt(do.astype(BF), values)
        dscore = (weights * (dprob - delta)).astype(BF)
        dqs.append((dot(dscore, keys) * FACTOR).astype(BF))
        dkt = dot(q.T.astype(BF), dscore)
        dvt = dot(do.T.astype(BF), weights.astype(BF))
        if n == 0:
            dkt_ref[...] = dkt
            dvt_ref[...] = dvt
        else:
            dkt_ref[...] += dkt
            dvt_ref[...] += dvt
    out_ref[:, :, THREE:] = jnp.zeros((2 * n_z, 64, 36), BF)
    for n in range(len(blocks)):
        rows = slice(step * n, step * (n + 1))
        dk = (dkt_ref[:, rows].T * FACTOR).astype(BF)
        dv = dvt_ref[:, rows].T.astype(BF)
        back = dot_nt(jnp.concatenate([dqs[n], dk, dv], 1), sel).astype(BF)
        out_ref[:, 16 * n : 16 * (n + 1), :THREE] = back.reshape(2 * n_z, 16, THREE)


def pack_time_kernel(q_ref, k_ref, v_ref, g_ref, out_ref):
    rows, frames = q_ref.shape[0], out_ref.shape[0]
    group = rows // frames
    i, j = iota((rows, rows), 0), iota((rows, rows), 1)
    order = choose(j == frames * (i % group) + i // group)
    moved = [dot(order, ref[...]).astype(BF) for ref in (q_ref, k_ref, v_ref, g_ref)]
    moved = jnp.concatenate(moved, 1)
    for f in range(frames):
        out_ref[f] = moved[group * f : group * (f + 1)]


def add_tiles(tiles, start, part):
    for low in range(0, part.shape[1], 128):
        piece = part[:, low : low + 128]
        n = (start + low) // 128
        tiles[n] = tiles[n] + piece if n in tiles else piece


def joined(tiles):
    return jnp.concatenate([tiles[n] for n in sorted(tiles)], 1)


def temporal_kernel(place_ref, x_ref, proj_any, out_ref, keep_ref, send_ref, proj_ref, sem):
    core = place_ref[0]
    copy = pltpu.make_async_copy(proj_any, proj_ref, sem)
    copy.start()
    rows = x_ref.shape[0]
    group = 4
    q, k, v = [x_ref[:, HD * a : HD * (a + 1)] for a in range(3)]
    g = x_ref[:, 3 * HD :]
    same = iota((rows, rows), 0) % group == iota((rows, rows), 1) % group
    views = []
    for h in range(HEADS):
        start, width, offset = window(h)
        lane = iota((1, width), 1)
        mask = choose((lane >= offset) & (lane < offset + HSIZE))
        views.append((start, slice(start, start + width), mask))
    weights = []
    tiles = {}
    for start, cols, mask in views:
        scores = jnp.where(same, dot_nt(q[:, cols] * mask, k[:, cols]) * FACTOR, -1e30)
        e = jnp.where(same, jnp.exp(scores - scores.max(-1, keepdims=True)), 0.0)
        inverse = 1.0 / e.sum(-1, keepdims=True)
        add_tiles(tiles, start, dot(e.astype(BF), v[:, cols] * mask) * inverse)
        weights.append(e * inverse)
    out = joined(tiles).astype(BF)
    copy.wait()
    do = dot_nt(g, proj_ref[...]).astype(BF)
    product = do.astype(F32) * out.astype(F32)
    dqs, dks, dvs = {}, {}, {}
    for weight, (start, cols, mask) in zip(weights, views):
        dom = do[:, cols] * mask
        delta = (product[:, cols] * mask.astype(F32)).sum(-1, keepdims=True)
        dscore = weight * (dot_nt(dom, v[:, cols]) - delta)
        add_tiles(dqs, start, dot(dscore.astype(BF), k[:, cols] * mask))
        add_tiles(dks, start, dot(dscore.T.astype(BF), q[:, cols] * mask))
        add_tiles(dvs, start, dot(weight.T.astype(BF), dom))
    dq, dk, dv = joined(dqs), joined(dks), joined(dvs)
    i, j = iota((rows, rows), 0), iota((rows, rows), 1)
    half_rows = rows // 2
    order = choose(j == group * (i % half_rows // 2) + 2 * (i // half_rows) + i % 2)
    for a, grad in enumerate((dq * FACTOR, dk * FACTOR, dv)):
        sorted_rows = dot(order, grad.astype(BF)).astype(BF)
        for b in range(2):
            low = HD * (3 * b + a)
            for f in range(out_ref.shape[0]):
                row = half_rows * b + 2 * f
                out_ref[f, :, low : low + HD] = sorted_rows[row : row + 2]
    i, j = iota((HD, HD), 0), iota((HD, HD), 1)
    order = choose(j == 18 * (i % 64 // 2) + 2 * (i // 64) + i % 2)
    out_t = dot_nt(order, out).astype(BF)
    for ref, half in ((keep_ref, core), (send_ref, 1 - core)):
        part = dot(out_t, dot(g, core_columns(half)).astype(BF)).astype(BF)
        for b in range(9):
            ref[:, HALF * b : HALF * (b + 1)] = part[64 * b : 64 * b + 64]


def on_device(query_s, key_s, value_s, query_t, key_t, value_t, grad_out, proj_s, proj_t):
    frames = lax.axis_size("frame")
    n_pix = lax.axis_size("pix")
    n_z = n_pix // 2
    pix = lax.axis_index("pix")
    core, z = pix % 2, pix // 2
    place = jnp.stack([core, z]).astype(jnp.int32)
    core_swap = [(p, p ^ 1) for p in range(n_pix)]
    same_core = [[2 * i + c for i in range(n_z)] for c in range(2)]

    with jax.named_scope("temporal_in"):
        flat = [a.reshape(128, a.shape[3]) for a in (query_t, key_t, value_t, grad_out)]
        sent_in = call(pack_time_kernel, 4, whole((frames, 4, 3 * HD + D), BF))(*flat)
        moved_t = lax.all_to_all(sent_in, "frame", 0, 0, tiled=True).reshape(128, 3 * HD + D)

    with jax.named_scope("spatial_grad_gather"):
        grad = grad_out[:, 0]
        own = lax.dynamic_index_in_dim(grad, core, 0, keepdims=False)
        other = lax.dynamic_index_in_dim(grad, 1 - core, 0, keepdims=False)
        other = lax.ppermute(other, "pix", core_swap)
        gathered = lax.all_gather(
            jnp.concatenate([own, other], 0), "pix", axis=0, axis_index_groups=same_core, tiled=True
        ).reshape(n_z, 2, 64, D)

    with jax.named_scope("spatial_in"):
        flat = [a.reshape(128, HD) for a in (query_s, key_s, value_s)]
        packed = call(pack_kernel, 3, whole((n_pix, 16, 4 * THREE), BF))(*flat)
        moved_s = lax.all_to_all(packed, "pix", 0, 0, tiled=True)

    with jax.named_scope("temporal_attention"):
        grads_t, keep_t, send_t = call(
            temporal_kernel,
            1,
            (whole((frames, 2, GRADS), BF), whole((64, SUMS_T), BF), whole((64, SUMS_T), BF)),
            scalars=1,
            scratch=[pltpu.VMEM((HD, D), BF), pltpu.SemaphoreType.DMA],
            anywhere=1,
        )(place, moved_t, proj_t)
        got_t = lax.ppermute(send_t, "pix", core_swap)

    with jax.named_scope("spatial_forward"):
        sent_out = call(
            forward_kernel,
            2,
            whole((frames, 2, GRADS + SUMS_T + SUMS_S), BF),
            scalars=1,
            scratch=[
                pltpu.VMEM((2 * frames, SUMS_S), F32),
                pltpu.VMEM(gathered.shape, BF),
                pltpu.VMEM(keep_t.shape, BF),
                pltpu.SemaphoreType.DMA((3,)),
            ],
            anywhere=3,
            mib=56,
        )(place, moved_s, got_t, grads_t, gathered, keep_t)

    with jax.named_scope("temporal_out"):
        home_t = lax.all_to_all(sent_out, "frame", 0, 0, tiled=True)
        back = home_t[..., :GRADS].reshape(frames, 2, 2, 3, HD).transpose(3, 2, 1, 0, 4)
        outs_t = [back[a].reshape(2, 1, 64, HD) for a in range(3)]

    with jax.named_scope("spatial_backward"):
        proj_h = lax.dynamic_slice_in_dim(proj_s, HSIZE * z, HSIZE, 0)
        proj_h = jnp.pad(proj_h, ((0, 128 - HSIZE), (0, 0)))
        grads_s = call(
            backward_kernel,
            3,
            whole((n_pix, 64, THREE + 36), BF),
            scalars=1,
            scratch=[pltpu.VMEM((128, n_pix * 64), F32)] * 2,
        )(place, moved_s, gathered, proj_h)

    with jax.named_scope("spatial_projection"):
        sums_s = home_t[..., GRADS + SUMS_T :].astype(F32).sum(0).reshape(2, 9, 2, HSIZE)
        sums_s = sums_s.transpose(2, 1, 0, 3).reshape(2, 18, HSIZE)
        own_s = lax.dynamic_index_in_dim(sums_s, core, 0, keepdims=False)
        other_s = lax.dynamic_index_in_dim(sums_s, 1 - core, 0, keepdims=False)
        sums_s = own_s + lax.ppermute(other_s, "pix", core_swap)
        perm = []
        for y in range(8):
            for x in range(4):
                for zz in range(n_z):
                    for c in range(2):
                        source = (y * 4 + x) * n_pix + 2 * zz + c
                        perm.append((source, (zz * 4 + x) * n_pix + 2 * y + c))
        proj_s_grad = lax.ppermute(sums_s, ("frame", "pix"), perm)

    with jax.named_scope("spatial_out"):
        sent = call(
            ride_kernel,
            2,
            whole(grads_s.shape, BF),
            scratch=[pltpu.VMEM((n_z, 18, HSIZE), F32)],
        )(home_t, grads_s)
        home_s = lax.all_to_all(sent, "pix", 0, 0, tiled=True)
        *outs_s, proj_t_grad = call(
            unpack_kernel,
            1,
            (whole((128, HD), BF),) * 3 + (whole((18, HSIZE), F32),),
            scalars=1,
        )(place, home_s)
        outs_s = [a.reshape(2, 1, 64, HD) for a in outs_s]

    return (*outs_s, *outs_t, proj_s_grad, proj_t_grad)


def solution(mesh):
    rows = P(None, "frame", "pix", None)
    out_specs = (rows,) * 6 + (P("frame", "pix"),) * 2
    return jax.shard_map(
        on_device,
        mesh=mesh,
        in_specs=(rows,) * 7 + (P(), P()),
        out_specs=out_specs,
        check_vma=False,
    )
```

time: 161 us -> 155 us (0.963)
  blocking collectives: 39.2 us -> 0 us
  waiting for transfers between devices: 34.6 us -> 57.3 us
  starting transfers between devices: 36.9 us -> 42.9 us
  Pallas kernels: 20.4 us -> 23.8 us
  local copies, waits for them, and re-layouts: 11.9 us -> 14.3 us
    all_to_all x1 -> x0, blocking collectives: 39.2 us -> none  [on_device(): home_t = lax.all_to_all(sent_out, 'frame', 0, 0, tiled=True)]
    all_to_all x0 -> x1, waiting for transfers between devices: none -> 23 us  [on_device(): home_t = lax.all_to_all(sent_out, 'frame', 0, 0, tiled=True)]
    all_to_all x0 -> x1, starting transfers between devices: none -> 6.44 us  [on_device(): home_t = lax.all_to_all(sent_out, 'frame', 0, 0, tiled=True)]
    unnamed x30 -> x42, local copies, waits for them, and re-layouts: 5.32 us -> 8.89 us
    pallas_call x6 -> x7, Pallas kernels: 20.4 us -> 23.8 us  [the longest x1 6.63 us: on_device(): call(temporal_kernel, 1, (whole((frames, 2, GRADS), BF), whole((64, SUMS_...]
  transfers between devices with their start and end apart: 8 -> 9, of which waited for: 4 -> 5; matrix products, arithmetic and copies ran while one was open for 3% -> 3% of each run, Pallas kernels for 11% -> 10%
where the time goes in v3:
time: 155 us; the launch traced here: 154 us
  waiting for transfers between devices  57.3 us (37%)
  starting transfers between devices  42.9 us (28%)
  Pallas kernels  23.8 us (15%)
  between operations  14.5 us (9%)
  local copies, waits for them, and re-layouts  14.3 us (9%)
    all_to_all x1, waiting for transfers between devices, on_device(): home_t = lax.all_to_all(sent_out, 'frame', 0, 0, tiled=True)  23 us
    all_to_all x1, waiting for transfers between devices, on_device(): lax.all_to_all(sent_in, 'frame', 0, 0, tiled=True).reshape(128, 3 * HD + D)  19.2 us
    all_to_all x1, starting transfers between devices, on_device(): moved_s = lax.all_to_all(packed, 'pix', 0, 0, tiled=True)  13.2 us
    all_to_all x1, waiting for transfers between devices, on_device(): home_s = lax.all_to_all(sent, 'pix', 0, 0, tiled=True)  10.3 us
    unnamed x42, local copies, waits for them, and re-layouts  8.89 us
    ppermute x1, starting transfers between devices, on_device(): other = lax.ppermute(other, 'pix', core_swap)  8.79 us
    pallas_call x1, Pallas kernels, on_device(): call(temporal_kernel, 1, (whole((frames, 2, GRADS), BF), whole((64, SUMS_...  6.63 us
    all_to_all x1, starting transfers between devices, on_device(): home_t = lax.all_to_all(sent_out, 'frame', 0, 0, tiled=True)  6.44 us
  transfers between devices with their start and end apart: 9, of which 5 were waited for; matrix products, arithmetic and copies ran while one was open for 3% of the time, Pallas kernels for 10%

profile of v3, /device:TPU:1, one launch (start us, length us, event | category | flops | bytes accessed | tf_op | source)
XLA Modules:
  0.0 153.9 jit_solution(10776377726638741229)
XLA Ops:
  7.3 1.1 dynamic-slice_bitcast_fusion.1
  8.4 8.8 %collective-permute-start.1 = (bf16[64,1152]{1,0:T(8,128)(2,1)S(1)}, bf16[64,1152]{1,0:T(8,128)(2,1)S(1)}, u32[]{:S(2)}, u32[]{:S(2)}) collective-permute-start(bf16[64,1152]{1,0:T(8,128)(2,1)S(1)} %get-tuple-element.50), channel_id=1, source_target_pairs={{0,1},{1,0},{2,3},{3,2},{4,5},{5,4},{6,7},{7,6},{8,9},{9,8},{10,11... | collective-permute-start | bytes 442376 | tf_op jit(solution)/shard_map/spatial_grad_gather/ppermute | solution.py:321
  17.2 1.0 collective-permute-done.1
  18.2 0.7 pad_maximum_fusion
  19.0 1.3 temporal_in.1
  20.4 4.3 %all-to-all-start.1 = ((bf16[32,4,2880]{2,1,0:T(4,128)(2,1)}), bf16[32,4,2880]{2,1,0:T(4,128)(2,1)S(1)}, u32[]{:S(2)}, u32[]{:S(2)}) async-start(bf16[32,4,2880]{2,1,0:T(4,128)(2,1)} %temporal_in.1), calls=%async_computation.1 | async-start | bytes 1507328 | tf_op jit(solution)/shard_map/temporal_in/all_to_all | solution.py:315
  24.7 1.4 spatial_in.1
  26.1 19.2 %all-to-all-done.1 = bf16[32,4,2880]{2,1,0:T(4,128)(2,1)S(1)} async-done(((bf16[32,4,2880]{2,1,0:T(4,128)(2,1)}), bf16[32,4,2880]{2,1,0:T(4,128)(2,1)S(1)}, u32[]{:S(2)}, u32[]{:S(2)}) %all-to-all-start.1) | async-done | bytes 737312 | tf_op jit(solution)/shard_map/temporal_in/all_to_all | solution.py:315
  45.3 13.2 %all-to-all-start = ((bf16[16,16,864]{2,1,0:T(8,128)(2,1)}), bf16[16,16,864]{2,1,0:T(8,128)(2,1)S(1)}, u32[]{:S(2)}, u32[]{:S(2)}) async-start(bf16[16,16,864]{2,1,0:T(8,128)(2,1)} %spatial_in.1), calls=%async_computation | async-start | bytes 917504 | tf_op jit(solution)/shard_map/spatial_in/all_to_all | solution.py:329
  58.9 1.3 copy-done.7
  60.2 6.6 %temporal_attention.1 = (bf16[32,2,3456]{2,1,0:T(2,128)(2,1)S(1)}, bf16[64,5184]{1,0:T(8,128)(2,1)S(1)}, bf16[64,5184]{1,0:T(8,128)(2,1)}) custom-call(s32[2]{0:T(128)S(1)} %pad_add_fusion.place_ref, bf16[128,2880]{1,0:T(8,128)(2,1)S(1)} %reshape.72.x_ref, bf16[576,1152]{1,0:T(8,128)(2,1)S(1)} %copy-done.7), custom_call_target="tpu_custom_call" | custom-call | flops 1 | bytes 1 | tf_op jit(solution)/shard_map/temporal_attention/pallas_call | solution.py:332
  66.9 0.8 copy-done.9
  67.7 0.8 copy-done.10
  68.5 2.0 %collective-permute-start = (bf16[64,5184]{1,0:T(8,128)(2,1)}, bf16[64,5184]{1,0:T(8,128)(2,1)S(1)}, u32[]{:S(2)}, u32[]{:S(2)}) collective-permute-start(bf16[64,5184]{1,0:T(8,128)(2,1)} %get-tuple-element.15), channel_id=1, source_target_pairs={{0,1},{1,0},{2,3},{3,2},{4,5},{5,4},{6,7},{7,6},{8,9},{9,8},{10,11... | collective-permute-start | bytes 1990664 | tf_op jit(solution)/shard_map/temporal_attention/ppermute | solution.py:340
  70.5 3.8 %all-to-all-done.x_ref = bf16[16,16,864]{2,1,0:T(8,128)(2,1)S(1)} async-done(((bf16[16,16,864]{2,1,0:T(8,128)(2,1)}), bf16[16,16,864]{2,1,0:T(8,128)(2,1)S(1)}, u32[]{:S(2)}, u32[]{:S(2)}) %all-to-all-start) | async-done | bytes 442400 | tf_op jit(solution)/shard_map/spatial_in/all_to_all | solution.py:329
  74.4 0.8 copy-done.2
  75.4 6.0 %spatial_forward.1 = bf16[32,2,9936]{2,1,0:T(2,128)(2,1)} custom-call(s32[2]{0:T(128)} %copy-done.17, bf16[16,16,864]{2,1,0:T(8,128)(2,1)} %copy-done.2, bf16[64,5184]{1,0:T(8,128)(2,1)} %copy-done.19, bf16[32,2,3456]{2,1,0:T(2,128)(2,1)} %copy-done.10, bf16[8,2,64,1152]{3,2,1,0:T(8,128)(2,1)} %bitcast.42, bf16[64,5184]{1,0:T(8,128)(2,1)} %copy-done.9), custom_call_target="tpu_custom_call" | custom-call | flops 1 | bytes 1 | tf_op jit(solution)/shard_map/spatial_forward/pallas_call | solution.py:343
  81.5 6.4 %all-to-all-start.2 = ((bf16[32,2,9936]{2,1,0:T(2,128)(2,1)}), bf16[32,2,9936]{2,1,0:T(2,128)(2,1)S(1)}, u32[]{:S(2)}, u32[]{:S(2)}) async-start(bf16[32,2,9936]{2,1,0:T(2,128)(2,1)} %spatial_forward.1), calls=%async_computation.2 | async-start | bytes 2555904 | tf_op jit(solution)/shard_map/temporal_out/all_to_all | solution.py:359
  88.0 1.7 %copy-done.1 = bf16[1024,1152]{1,0:T(8,128)(2,1)S(1)} copy-done((bf16[1024,1152]{1,0:T(8,128)(2,1)S(1)}, bf16[1024,1152]{1,0:T(8,128)(2,1)}, u32[]{:S(2)}) %copy-start.1) | copy-done | bytes 2359320
  89.7 6.0 %spatial_backward.1.grads_ref = bf16[16,64,252]{2,1,0:T(8,128)(2,1)S(1)} custom-call(s32[2]{0:T(128)S(1)} %copy-done.18, bf16[16,16,864]{2,1,0:T(8,128)(2,1)S(1)} %copy-done.3, bf16[8,2,64,1152]{3,2,1,0:T(8,128)(2,1)S(1)} %bitcast.43, bf16[128,1152]{1,0:T(8,128)(2,1)S(1)} %pad.4.proj_ref), custom_call_target="tpu_custom_call" | custom-call | flops 1 | bytes 1 | tf_op jit(solution)/shard_map/spatial_backward/pallas_call | solution.py:366
  95.7 0.8 copy-done.5
  96.5 23.0 %all-to-all-done.2.home_ref = bf16[32,2,9936]{2,1,0:T(2,128)(2,1)S(1)} async-done(((bf16[32,2,9936]{2,1,0:T(2,128)(2,1)}), bf16[32,2,9936]{2,1,0:T(2,128)(2,1)S(1)}, u32[]{:S(2)}, u32[]{:S(2)}) %all-to-all-start.2) | async-done | bytes 1271840 | tf_op jit(solution)/shard_map/temporal_out/all_to_all | solution.py:359
  119.6 1.0 copy-done.6
  121.0 0.8 copy-done.4
  121.8 5.5 %all-to-all-start.3 = ((bf16[16,64,252]{2,1,0:T(8,128)(2,1)}), bf16[16,64,252]{2,1,0:T(8,128)(2,1)S(1)}, u32[]{:S(2)}, u32[]{:S(2)}) async-start(bf16[16,64,252]{2,1,0:T(8,128)(2,1)} %copy-done.4), calls=%async_computation.3 | async-start | bytes 1048576 | tf_op jit(solution)/shard_map/spatial_out/all_to_all | solution.py:396
  127.7 2.0 %collective-permute-start.2 = (f32[18,72]{1,0:T(8,128)S(1)}, f32[18,72]{1,0:T(8,128)S(1)}, u32[]{:S(2)}, u32[]{:S(2)}) collective-permute-start(f32[18,72]{1,0:T(8,128)S(1)} %bitcast.57), channel_id=1, source_target_pairs={{0,1},{1,0},{2,3},{3,2},{4,5},{5,4},{6,7},{7,6},{8,9},{9,8},{10,11... | collective-permute-start | bytes 15560 | tf_op jit(solution)/shard_map/spatial_projection/ppermute | solution.py:379
  131.5 0.7 fusion
  132.2 0.7 copy.32
  132.9 0.7 copy.33
  133.6 0.7 copy.34
  134.3 10.3 %all-to-all-done.3.x_ref = bf16[16,64,252]{2,1,0:T(8,128)(2,1)S(1)} async-done(((bf16[16,64,252]{2,1,0:T(8,128)(2,1)}), bf16[16,64,252]{2,1,0:T(8,128)(2,1)S(1)}, u32[]{:S(2)}, u32[]{:S(2)}) %all-to-all-start.3) | async-done | bytes 516128 | tf_op jit(solution)/shard_map/spatial_out/all_to_all | solution.py:396
  144.5 2.0 %spatial_out.3 = (bf16[128,576]{1,0:T(8,128)(2,1)}, bf16[128,576]{1,0:T(8,128)(2,1)}, bf16[128,576]{1,0:T(8,128)(2,1)}, f32[18,72]{1,0:T(8,128)}) custom-call(s32[2]{0:T(128)S(1)} %copy-done.18, bf16[16,64,252]{2,1,0:T(8,128)(2,1)S(1)} %all-to-all-done.3.x_ref), custom_call_target="tpu_custom_call" | custom-call | flops 1 | bytes 1 | tf_op jit(solution)/shard_map/spatial_out/pallas_call | solution.py:397
  (54 shorter events, 4.0 us)
Async XLA Ops:
  7.2 80.7 %copy-start = (bf16[576,1152]{1,0:T(8,128)(2,1)S(1)}, bf16[576,1152]{1,0:T(8,128)(2,1)}, u32[]{:S(2)}) copy-start(bf16[576,1152]{1,0:T(8,128)(2,1)} %param.16) | copy-start | bytes 3981316
  7.2 11.8 %copy-start.8 = (bf16[2,1,64,1152]{3,2,1,0:T(8,128)(2,1)S(1)}, bf16[2,1,64,1152]{3,2,1,0:T(8,128)(2,1)}, u32[]{:S(2)}) copy-start(bf16[2,1,64,1152]{3,2,1,0:T(8,128)(2,1)} %param.15) | copy-start | bytes 884740
  7.2 11.8 %copy-start.11 = (bf16[2,1,64,576]{3,2,1,0:T(8,128)(2,1)S(1)}, bf16[2,1,64,576]{3,2,1,0:T(8,128)(2,1)}, u32[]{:S(2)}) copy-start(bf16[2,1,64,576]{3,2,1,0:T(8,128)(2,1)} %param.12) | copy-start | bytes 442372
  7.2 11.8 %copy-start.12 = (bf16[2,1,64,576]{3,2,1,0:T(8,128)(2,1)S(1)}, bf16[2,1,64,576]{3,2,1,0:T(8,128)(2,1)}, u32[]{:S(2)}) copy-start(bf16[2,1,64,576]{3,2,1,0:T(8,128)(2,1)} %param.13) | copy-start | bytes 442372
  7.2 11.8 %copy-start.13 = (bf16[2,1,64,576]{3,2,1,0:T(8,128)(2,1)S(1)}, bf16[2,1,64,576]{3,2,1,0:T(8,128)(2,1)}, u32[]{:S(2)}) copy-start(bf16[2,1,64,576]{3,2,1,0:T(8,128)(2,1)} %param.14) | copy-start | bytes 442372
  7.2 67.1 %all-gather.2.cloned.1.call-start = ((), (), s32[]{:S(2)}) async-start(), calls=%async_computation.4 | async-start | bytes 2654208 | tf_op jit(solution)/shard_map/spatial_grad_gather/all_gather | solution.py:322
  8.4 9.8 %collective-permute-start.1 = (bf16[64,1152]{1,0:T(8,128)(2,1)S(1)}, bf16[64,1152]{1,0:T(8,128)(2,1)S(1)}, u32[]{:S(2)}, u32[]{:S(2)}) collective-permute-start(bf16[64,1152]{1,0:T(8,128)(2,1)S(1)} %get-tuple-element.50), channel_id=1, source_target_pairs={{0,1},{1,0},{2,3},{3,2},{4,5},{5,4},{6,7},{7,6},{8,9},{9,8},{10,11... | collective-permute-start | bytes 442376 | tf_op jit(solution)/shard_map/spatial_grad_gather/ppermute | solution.py:321
  19.0 5.7 %copy-start.14 = (bf16[2,1,64,576]{3,2,1,0:T(8,128)(2,1)S(1)}, bf16[2,1,64,576]{3,2,1,0:T(8,128)(2,1)}, u32[]{:S(2)}) copy-start(bf16[2,1,64,576]{3,2,1,0:T(8,128)(2,1)} %param.9) | copy-start | bytes 442372
  19.0 5.7 %copy-start.15 = (bf16[2,1,64,576]{3,2,1,0:T(8,128)(2,1)S(1)}, bf16[2,1,64,576]{3,2,1,0:T(8,128)(2,1)}, u32[]{:S(2)}) copy-start(bf16[2,1,64,576]{3,2,1,0:T(8,128)(2,1)} %param.10) | copy-start | bytes 442372
  19.0 5.7 %copy-start.16 = (bf16[2,1,64,576]{3,2,1,0:T(8,128)(2,1)S(1)}, bf16[2,1,64,576]{3,2,1,0:T(8,128)(2,1)}, u32[]{:S(2)}) copy-start(bf16[2,1,64,576]{3,2,1,0:T(8,128)(2,1)} %param.11) | copy-start | bytes 442372
  20.4 24.9 %all-to-all-start.1 = ((bf16[32,4,2880]{2,1,0:T(4,128)(2,1)}), bf16[32,4,2880]{2,1,0:T(4,128)(2,1)S(1)}, u32[]{:S(2)}, u32[]{:S(2)}) async-start(bf16[32,4,2880]{2,1,0:T(4,128)(2,1)} %temporal_in.1), calls=%async_computation.1 | async-start | bytes 1507328 | tf_op jit(solution)/shard_map/temporal_in/all_to_all | solution.py:315
  45.3 29.0 %all-to-all-start = ((bf16[16,16,864]{2,1,0:T(8,128)(2,1)}), bf16[16,16,864]{2,1,0:T(8,128)(2,1)S(1)}, u32[]{:S(2)}, u32[]{:S(2)}) async-start(bf16[16,16,864]{2,1,0:T(8,128)(2,1)} %spatial_in.1), calls=%async_computation | async-start | bytes 917504 | tf_op jit(solution)/shard_map/spatial_in/all_to_all | solution.py:329
  58.6 8.3 %copy-start.17 = (s32[2]{0:T(128)}, s32[2]{0:T(128)S(1)}, u32[]{:S(2)}) copy-start(s32[2]{0:T(128)S(1)} %pad_add_fusion.place_ref) | copy-start | bytes 28
  58.9 1.3 copy-start.7
  66.9 0.8 copy-start.9
  67.7 0.8 copy-start.10
  68.5 5.8 %collective-permute-start = (bf16[64,5184]{1,0:T(8,128)(2,1)}, bf16[64,5184]{1,0:T(8,128)(2,1)S(1)}, u32[]{:S(2)}, u32[]{:S(2)}) collective-permute-start(bf16[64,5184]{1,0:T(8,128)(2,1)} %get-tuple-element.15), channel_id=1, source_target_pairs={{0,1},{1,0},{2,3},{3,2},{4,5},{5,4},{6,7},{7,6},{8,9},{9,8},{10,11... | collective-permute-start | bytes 1990664 | tf_op jit(solution)/shard_map/temporal_attention/ppermute | solution.py:340
  74.3 0.8 copy-start.2
  74.3 1.0 copy-start.19
  81.4 6.6 %copy-start.3 = (bf16[16,16,864]{2,1,0:T(8,128)(2,1)S(1)}, bf16[16,16,864]{2,1,0:T(8,128)(2,1)}, u32[]{:S(2)}) copy-start(bf16[16,16,864]{2,1,0:T(8,128)(2,1)} %copy-done.2) | copy-start | bytes 1327108
  81.4 6.6 %copy-start.18 = (s32[2]{0:T(128)S(1)}, s32[2]{0:T(128)}, u32[]{:S(2)}) copy-start(s32[2]{0:T(128)} %copy-done.17) | copy-start | bytes 28
  81.5 38.1 %all-to-all-start.2 = ((bf16[32,2,9936]{2,1,0:T(2,128)(2,1)}), bf16[32,2,9936]{2,1,0:T(2,128)(2,1)S(1)}, u32[]{:S(2)}, u32[]{:S(2)}) async-start(bf16[32,2,9936]{2,1,0:T(2,128)(2,1)} %spatial_forward.1), calls=%async_computation.2 | async-start | bytes 2555904 | tf_op jit(solution)/shard_map/temporal_out/all_to_all | solution.py:359
  88.0 1.7 %copy-start.1 = (bf16[1024,1152]{1,0:T(8,128)(2,1)S(1)}, bf16[1024,1152]{1,0:T(8,128)(2,1)}, u32[]{:S(2)}) copy-start(bf16[1024,1152]{1,0:T(8,128)(2,1)} %all-gather.2.cloned.1.call-done) | copy-start | bytes 7077892
  95.7 0.8 copy-start.5
  119.5 1.0 copy-start.6
  121.0 0.8 copy-start.4
  121.8 22.8 %all-to-all-start.3 = ((bf16[16,64,252]{2,1,0:T(8,128)(2,1)}), bf16[16,64,252]{2,1,0:T(8,128)(2,1)S(1)}, u32[]{:S(2)}, u32[]{:S(2)}) async-start(bf16[16,64,252]{2,1,0:T(8,128)(2,1)} %copy-done.4), calls=%async_computation.3 | async-start | bytes 1048576 | tf_op jit(solution)/shard_map/spatial_out/all_to_all | solution.py:396
  127.7 3.1 %collective-permute-start.2 = (f32[18,72]{1,0:T(8,128)S(1)}, f32[18,72]{1,0:T(8,128)S(1)}, u32[]{:S(2)}, u32[]{:S(2)}) collective-permute-start(f32[18,72]{1,0:T(8,128)S(1)} %bitcast.57), channel_id=1, source_target_pairs={{0,1},{1,0},{2,3},{3,2},{4,5},{5,4},{6,7},{7,6},{8,9},{9,8},{10,11... | collective-permute-start | bytes 15560 | tf_op jit(solution)/shard_map/spatial_projection/ppermute | solution.py:379
  130.8 3.4 %collective-permute-start.3 = (f32[18,72]{1,0:T(8,128)S(1)}, f32[18,72]{1,0:T(8,128)S(1)}, u32[]{:S(2)}, u32[]{:S(2)}) collective-permute-start(f32[18,72]{1,0:T(8,128)S(1)} %bitcast_add_fusion), channel_id=1, source_target_pairs={{0,0},{1,1},{2,64},{3,65},{4,128},{5,129},{6,192},{7,193},{8,256},... | collective-permute-start | bytes 15560 | tf_op jit(solution)/shard_map/spatial_projection/ppermute | solution.py:387
Sparse Core Ops, SparseCore 0:
  19.1 40.7 all-gather.1

commit v4 on v3

--- a/solution.py
+++ b/solution.py
@@ -66,7 +66,8 @@
     )
 
 
-def pack_kernel(q_ref, k_ref, v_ref, out_ref):
+def pack_kernel(place_ref, q_ref, k_ref, v_ref, keep_ref, send_ref):
+    core = place_ref[0]
     for h in range(HEADS):
         start, width, offset = window(h)
         total = None
@@ -75,35 +76,38 @@
             sel = choose((i - offset == j) & (j >= 0) & (j < HSIZE))
             part = dot(ref[:, start : start + width], sel)
             total = part if total is None else total + part
-        total = total.astype(BF)[:, :THREE]
-        for c in range(2):
-            for n in range(4):
-                low = 64 * c + 16 * n
-                out_ref[2 * h + c, :, THREE * n : THREE * (n + 1)] = total[low : low + 16]
-
-
-def ride_kernel(home_ref, grads_ref, out_ref, rows_ref):
-    out_ref[...] = grads_ref[...]
+        low, high = total[:64, :THREE], total[64:, :THREE]
+        own = jnp.where(core == 0, low, high).astype(BF)
+        other = jnp.where(core == 0, high, low).astype(BF)
+        for n in range(4):
+            cols, rows = slice(THREE * n, THREE * (n + 1)), slice(16 * n, 16 * (n + 1))
+            keep_ref[h, :, cols] = own[rows]
+            send_ref[h, :, cols] = other[rows]
+
+
+def ride_kernel(home_ref, own_ref, got_ref, out_ref, rows_ref):
+    out_ref[:, :64, :THREE] = own_ref[...]
+    out_ref[:, 64:, :THREE] = got_ref[...]
     total = None
     for f in range(home_ref.shape[0]):
         part = home_ref[f, :, GRADS : GRADS + SUMS_T].astype(F32)
         total = part if total is None else total + part
-    for z in range(out_ref.shape[0] // 2):
+    out_ref[:, :, THREE:] = jnp.zeros((out_ref.shape[0], 128, 36), BF)
+    for z in range(out_ref.shape[0]):
         for b in range(9):
             low = HALF * b + HSIZE * z
             rows_ref[z, 2 * b : 2 * b + 2] = total[:, low : low + HSIZE]
         for n in range(2):
             half = rows_ref[z, :, 36 * n : 36 * (n + 1)].astype(BF)
-            for c in range(2):
-                out_ref[2 * z + c, 32 * n : 32 * n + 18, THREE:] = half
+            out_ref[z, 32 * n : 32 * n + 18, THREE:] = half
 
 
 def unpack_kernel(place_ref, x_ref, dq_ref, dk_ref, dv_ref, sum_ref):
     core = place_ref[0]
     for n in range(2):
         total = None
-        for z in range(x_ref.shape[0] // 2):
-            part = x_ref[2 * z + core, 32 * n : 32 * n + 18, THREE:].astype(F32)
+        for z in range(x_ref.shape[0]):
+            part = x_ref[z, 32 * n : 32 * n + 18, THREE:].astype(F32)
             total = part if total is None else total + part
         sum_ref[:, 36 * n : 36 * (n + 1)] = total
     for a, ref in enumerate((dq_ref, dk_ref, dv_ref)):
@@ -114,7 +118,10 @@
                 low = HSIZE * h - start
                 if low >= width or low + HSIZE <= 0:
                     continue
-                pair = jnp.concatenate([x_ref[2 * h], x_ref[2 * h + 1]], 0)[:, :THREE]
+                first, second = x_ref[h, :64, :THREE], x_ref[h, 64:, :THREE]
+                pair = jnp.concatenate(
+                    [jnp.where(core == 0, first, second), jnp.where(core == 0, second, first)], 0
+                )
                 i, j = iota((THREE, width), 0) - HSIZE * a, iota((THREE, width), 1)
                 sel = choose((i + low == j) & (i >= 0) & (i < HSIZE))
                 part = dot(pair, sel)
@@ -143,9 +150,8 @@
 
 
 def forward_kernel(
-    place_ref, x_ref, got_ref, grads_any, g_any, keep_any, out_ref, chunk_ref, g_ref, keep_ref, sems
+    x_ref, got_ref, grads_any, g_any, keep_any, out_ref, chunk_ref, g_ref, keep_ref, sems
 ):
-    core = place_ref[0]
     copies = [
         pltpu.make_async_copy(keep_any, keep_ref, sems.at[0]),
         pltpu.make_async_copy(g_any, g_ref, sems.at[1]),
@@ -164,11 +170,11 @@
     for f in range(out_ref.shape[0]):
         rows = slice(2 * f, 2 * f + 2)
         out_ref[f, :, GRADS : GRADS + SUMS_T] = total[rows]
-    even = jnp.concatenate([pair[:, 0] for pair in pairs], 1)
-    odd = jnp.concatenate([pair[:, 1] for pair in pairs], 1)
+    own = jnp.concatenate([pair[:, 0] for pair in pairs], 1)
+    other = jnp.concatenate([pair[:, 1] for pair in pairs], 1)
     sums = None
     copies[1].wait()
-    for n, tokens in enumerate((jnp.where(core == 0, even, odd), jnp.where(core == 0, odd, even))):
+    for n, tokens in enumerate((own, other)):
         rows = n_z * 64
         term = dot(tokens.reshape(rows, 128).T.astype(BF), g_ref[:, n].reshape(rows, D))
         sums = term if sums is None else sums + term
@@ -185,16 +191,14 @@
     copies[2].wait()
 
 
-def backward_kernel(place_ref, x_ref, g_ref, proj_ref, out_ref, dkt_ref, dvt_ref):
-    core = place_ref[0]
+def backward_kernel(x_ref, g_ref, proj_ref, own_ref, other_ref, dkt_ref, dvt_ref):
     n_z = g_ref.shape[0]
     sel, blocks, keys, values = split_heads(x_ref)
     own, other = [
         dot_nt(g_ref[:, n].reshape(n_z * 64, D), proj_ref[...]).reshape(n_z, 64, 128)
         for n in range(2)
     ]
-    even, odd = jnp.where(core == 0, own, other), jnp.where(core == 0, other, own)
-    grads = jnp.concatenate([even[:, None], odd[:, None]], 1).astype(BF).astype(F32)
+    grads = jnp.concatenate([own[:, None], other[:, None]], 1).astype(BF).astype(F32)
     step = 2 * n_z * 16
     dqs = []
     for n, part in enumerate(blocks):
@@ -213,13 +217,14 @@
         else:
             dkt_ref[...] += dkt
             dvt_ref[...] += dvt
-    out_ref[:, :, THREE:] = jnp.zeros((2 * n_z, 64, 36), BF)
     for n in range(len(blocks)):
         rows = slice(step * n, step * (n + 1))
         dk = (dkt_ref[:, rows].T * FACTOR).astype(BF)
         dv = dvt_ref[:, rows].T.astype(BF)
         back = dot_nt(jnp.concatenate([dqs[n], dk, dv], 1), sel).astype(BF)
-        out_ref[:, 16 * n : 16 * (n + 1), :THREE] = back.reshape(2 * n_z, 16, THREE)
+        back = back.reshape(n_z, 2, 16, THREE)
+        own_ref[:, 16 * n : 16 * (n + 1)] = back[:, 0]
+        other_ref[:, 16 * n : 16 * (n + 1)] = back[:, 1]
 
 
 def pack_time_kernel(q_ref, k_ref, v_ref, g_ref, out_ref):
@@ -325,8 +330,11 @@
 
     with jax.named_scope("spatial_in"):
         flat = [a.reshape(128, HD) for a in (query_s, key_s, value_s)]
-        packed = call(pack_kernel, 3, whole((n_pix, 16, 4 * THREE), BF))(*flat)
-        moved_s = lax.all_to_all(packed, "pix", 0, 0, tiled=True)
+        keep_s, send_s = call(
+            pack_kernel, 3, (whole((n_z, 16, 4 * THREE), BF),) * 2, scalars=1
+        )(place, *flat)
+        packed = jnp.concatenate([keep_s, lax.ppermute(send_s, "pix", core_swap)], 1)
+        moved_s = lax.all_to_all(packed, "pix", 0, 0, axis_index_groups=same_core, tiled=True)
 
     with jax.named_scope("temporal_attention"):
         grads_t, keep_t, send_t = call(
@@ -336,6 +344,7 @@
             scalars=1,
             scratch=[pltpu.VMEM((HD, D), BF), pltpu.SemaphoreType.DMA],
             anywhere=1,
+            mib=56,
         )(place, moved_t, proj_t)
         got_t = lax.ppermute(send_t, "pix", core_swap)
 
@@ -344,7 +353,6 @@
             forward_kernel,
             2,
             whole((frames, 2, GRADS + SUMS_T + SUMS_S), BF),
-            scalars=1,
             scratch=[
                 pltpu.VMEM((2 * frames, SUMS_S), F32),
                 pltpu.VMEM(gathered.shape, BF),
@@ -353,7 +361,7 @@
             ],
             anywhere=3,
             mib=56,
-        )(place, moved_s, got_t, grads_t, gathered, keep_t)
+        )(moved_s, got_t, grads_t, gathered, keep_t)
 
     with jax.named_scope("temporal_out"):
         home_t = lax.all_to_all(sent_out, "frame", 0, 0, tiled=True)
@@ -363,20 +371,21 @@
     with jax.named_scope("spatial_backward"):
         proj_h = lax.dynamic_slice_in_dim(proj_s, HSIZE * z, HSIZE, 0)
         proj_h = jnp.pad(proj_h, ((0, 128 - HSIZE), (0, 0)))
-        grads_s = call(
+        own_s, other_s = call(
             backward_kernel,
             3,
-            whole((n_pix, 64, THREE + 36), BF),
-            scalars=1,
+            (whole((n_z, 64, THREE), BF),) * 2,
             scratch=[pltpu.VMEM((128, n_pix * 64), F32)] * 2,
-        )(place, moved_s, gathered, proj_h)
+        )(moved_s, gathered, proj_h)
+
+        got_s = lax.ppermute(other_s, "pix", core_swap)
 
     with jax.named_scope("spatial_projection"):
         sums_s = home_t[..., GRADS + SUMS_T :].astype(F32).sum(0).reshape(2, 9, 2, HSIZE)
         sums_s = sums_s.transpose(2, 1, 0, 3).reshape(2, 18, HSIZE)
-        own_s = lax.dynamic_index_in_dim(sums_s, core, 0, keepdims=False)
-        other_s = lax.dynamic_index_in_dim(sums_s, 1 - core, 0, keepdims=False)
-        sums_s = own_s + lax.ppermute(other_s, "pix", core_swap)
+        own_sums = lax.dynamic_index_in_dim(sums_s, core, 0, keepdims=False)
+        other_sums = lax.dynamic_index_in_dim(sums_s, 1 - core, 0, keepdims=False)
+        sums_s = own_sums + lax.ppermute(other_sums, "pix", core_swap)
         perm = []
         for y in range(8):
             for x in range(4):
@@ -389,11 +398,11 @@
     with jax.named_scope("spatial_out"):
         sent = call(
             ride_kernel,
-            2,
-            whole(grads_s.shape, BF),
+            3,
+            whole((n_z, 128, THREE + 36), BF),
             scratch=[pltpu.VMEM((n_z, 18, HSIZE), F32)],
-        )(home_t, grads_s)
-        home_s = lax.all_to_all(sent, "pix", 0, 0, tiled=True)
+        )(home_t, own_s, got_s)
+        home_s = lax.all_to_all(sent, "pix", 0, 0, axis_index_groups=same_core, tiled=True)
         *outs_s, proj_t_grad = call(
             unpack_kernel,
             1,

time: 155 us -> 151 us (0.974)
  the two profiles are of different devices: /device:TPU:1 before, /device:TPU:2 now
where the time goes in v4:
time: 151 us; the launch traced here: 150 us
  waiting for transfers between devices  55.6 us (37%)
  starting transfers between devices  43.8 us (29%)
  Pallas kernels  23.9 us (16%)
  between operations  14.4 us (10%)
  local copies, waits for them, and re-layouts  10.4 us (7%)
  other arithmetic  1.98 us (1%)
    all_to_all x1, waiting for transfers between devices, on_device(): home_t = lax.all_to_all(sent_out, 'frame', 0, 0, tiled=True)  21.3 us
    all_to_all x1, waiting for transfers between devices, on_device(): lax.all_to_all(sent_in, 'frame', 0, 0, tiled=True).reshape(128, 3 * HD + D)  16.5 us
    all_to_all x1, starting transfers between devices, on_device(): lax.all_to_all(packed, 'pix', 0, 0, axis_index_groups=same_core, tiled=True)  10.3 us
    all_to_all x1, starting transfers between devices, on_device(): lax.all_to_all(sent_in, 'frame', 0, 0, tiled=True).reshape(128, 3 * HD + D)  10.3 us
    all_to_all x1, starting transfers between devices, on_device(): home_t = lax.all_to_all(sent_out, 'frame', 0, 0, tiled=True)  9.42 us
    all_to_all x1, waiting for transfers between devices, on_device(): lax.all_to_all(sent, 'pix', 0, 0, axis_index_groups=same_core, tiled=True)  8.95 us
    pallas_call x1, Pallas kernels, on_device(): call(temporal_kernel, 1, (whole((frames, 2, GRADS), BF), whole((64, SUMS_...  7.54 us
    pallas_call x1, Pallas kernels, on_device(): call(forward_kernel, 2, whole((frames, 2, GRADS + SUMS_T + SUMS_S), BF),...  6.03 us
  transfers between devices with their start and end apart: 11, of which 8 were waited for; matrix products, arithmetic and copies ran while one was open for 4% of the time, Pallas kernels for 10%

profile of v4, /device:TPU:2, one launch (start us, length us, event | category | flops | bytes accessed | tf_op | source)
XLA Modules:
  0.0 150.1 jit_solution(10079666743077786710)
XLA Ops:
  7.3 1.1 dynamic-slice_bitcast_fusion.1
  8.4 1.9 %collective-permute-start.2 = (bf16[64,1152]{1,0:T(8,128)(2,1)S(1)}, bf16[64,1152]{1,0:T(8,128)(2,1)S(1)}, u32[]{:S(2)}, u32[]{:S(2)}) collective-permute-start(bf16[64,1152]{1,0:T(8,128)(2,1)S(1)} %get-tuple-element.58), channel_id=1, source_target_pairs={{0,1},{1,0},{2,3},{3,2},{4,5},{5,4},{6,7},{7,6},{8,9},{9,8},{10,11... | collective-permute-start | bytes 442376 | tf_op jit(solution)/shard_map/spatial_grad_gather/ppermute | solution.py:326
  10.4 1.3 collective-permute-done.2
  11.7 0.7 pad_maximum_fusion.1
  12.5 1.3 temporal_in.1
  13.8 10.3 %all-to-all-start.1 = ((bf16[32,4,2880]{2,1,0:T(4,128)(2,1)}), bf16[32,4,2880]{2,1,0:T(4,128)(2,1)S(1)}, u32[]{:S(2)}, u32[]{:S(2)}) async-start(bf16[32,4,2880]{2,1,0:T(4,128)(2,1)} %temporal_in.1), calls=%async_computation.1 | async-start | bytes 1507328 | tf_op jit(solution)/shard_map/temporal_in/all_to_all | solution.py:320
  24.2 1.2 spatial_in.1
  25.4 1.9 %collective-permute-start = (bf16[8,16,864]{2,1,0:T(8,128)(2,1)S(1)}, bf16[8,16,864]{2,1,0:T(8,128)(2,1)S(1)}, u32[]{:S(2)}, u32[]{:S(2)}) collective-permute-start(bf16[8,16,864]{2,1,0:T(8,128)(2,1)S(1)} %get-tuple-element.20), channel_id=1, source_target_pairs={{0,1},{1,0},{2,3},{3,2},{4,5},{5,4},{6,7},{7,6},{8,9},{9,8},{10,11... | collective-permute-start | bytes 663560 | tf_op jit(solution)/shard_map/spatial_in/ppermute | solution.py:336
  27.4 1.5 collective-permute-done
  28.8 0.8 pad_maximum_fusion
  29.6 16.5 %all-to-all-done.1 = bf16[32,4,2880]{2,1,0:T(4,128)(2,1)S(1)} async-done(((bf16[32,4,2880]{2,1,0:T(4,128)(2,1)}), bf16[32,4,2880]{2,1,0:T(4,128)(2,1)S(1)}, u32[]{:S(2)}, u32[]{:S(2)}) %all-to-all-start.1) | async-done | bytes 737312 | tf_op jit(solution)/shard_map/temporal_in/all_to_all | solution.py:320
  46.2 10.3 %all-to-all-start = ((bf16[8,32,864]{2,1,0:T(8,128)(2,1)}), bf16[8,32,864]{2,1,0:T(8,128)(2,1)S(1)}, u32[]{:S(2)}, u32[]{:S(2)}) async-start(bf16[8,32,864]{2,1,0:T(8,128)(2,1)} %pad_maximum_fusion), calls=%async_computation | async-start | bytes 917504 | tf_op jit(solution)/shard_map/spatial_in/all_to_all | solution.py:337
  56.5 1.2 reshape.72.x_ref
  57.7 7.5 %temporal_attention.1 = (bf16[32,2,3456]{2,1,0:T(2,128)(2,1)}, bf16[64,5184]{1,0:T(8,128)(2,1)}, bf16[64,5184]{1,0:T(8,128)(2,1)}) custom-call(s32[2]{0:T(128)} %copy-done.12, bf16[128,2880]{1,0:T(8,128)(2,1)} %reshape.72.x_ref, bf16[576,1152]{1,0:T(8,128)(2,1)} %proj_any.1), custom_call_target="tpu_custom_call" | custom-call | flops 1 | bytes 1 | tf_op jit(solution)/shard_map/temporal_attention/pallas_call | solution.py:340
  65.3 1.9 %collective-permute-start.1 = (bf16[64,5184]{1,0:T(8,128)(2,1)}, bf16[64,5184]{1,0:T(8,128)(2,1)S(1)}, u32[]{:S(2)}, u32[]{:S(2)}) collective-permute-start(bf16[64,5184]{1,0:T(8,128)(2,1)} %get-tuple-element.21), channel_id=1, source_target_pairs={{0,1},{1,0},{2,3},{3,2},{4,5},{5,4},{6,7},{7,6},{8,9},{9,8},{10,11... | collective-permute-start | bytes 1990664 | tf_op jit(solution)/shard_map/temporal_attention/ppermute | solution.py:349
  67.2 4.3 %all-to-all-done.x_ref = bf16[8,32,864]{2,1,0:T(8,128)(2,1)S(1)} async-done(((bf16[8,32,864]{2,1,0:T(8,128)(2,1)}), bf16[8,32,864]{2,1,0:T(8,128)(2,1)S(1)}, u32[]{:S(2)}, u32[]{:S(2)}) %all-to-all-start) | async-done | bytes 442400 | tf_op jit(solution)/shard_map/spatial_in/all_to_all | solution.py:337
  71.5 0.8 copy-done.2
  72.5 6.0 %spatial_forward.1 = bf16[32,2,9936]{2,1,0:T(2,128)(2,1)} custom-call(bf16[8,32,864]{2,1,0:T(8,128)(2,1)} %copy-done.2, bf16[64,5184]{1,0:T(8,128)(2,1)} %copy-done.14, bf16[32,2,3456]{2,1,0:T(2,128)(2,1)} %get-tuple-element.22.grads_any, bf16[8,2,64,1152]{3,2,1,0:T(8,128)(2,1)} %bitcast.42, bf16[64,5184]{1,0:T(8,128)(2,1)} %get-tuple-element.23.keep_any), custom_call_target="tpu_custom_call" | custom-call | flops 1 | bytes 1 | tf_op jit(solution)/shard_map/spatial_forward/pallas_call | solution.py:352
  78.6 9.4 %all-to-all-start.2 = ((bf16[32,2,9936]{2,1,0:T(2,128)(2,1)}), bf16[32,2,9936]{2,1,0:T(2,128)(2,1)S(1)}, u32[]{:S(2)}, u32[]{:S(2)}) async-start(bf16[32,2,9936]{2,1,0:T(2,128)(2,1)} %spatial_forward.1), calls=%async_computation.2 | async-start | bytes 2555904 | tf_op jit(solution)/shard_map/temporal_out/all_to_all | solution.py:367
  88.1 1.7 %copy-done.1 = bf16[1024,1152]{1,0:T(8,128)(2,1)S(1)} copy-done((bf16[1024,1152]{1,0:T(8,128)(2,1)S(1)}, bf16[1024,1152]{1,0:T(8,128)(2,1)}, u32[]{:S(2)}) %copy-start.1) | copy-done | bytes 2359320
  89.8 5.5 %spatial_backward.1 = (bf16[8,64,216]{2,1,0:T(8,128)(2,1)S(1)}, bf16[8,64,216]{2,1,0:T(8,128)(2,1)S(1)}) custom-call(bf16[8,32,864]{2,1,0:T(8,128)(2,1)S(1)} %copy-done.3, bf16[8,2,64,1152]{3,2,1,0:T(8,128)(2,1)S(1)} %bitcast.43, bf16[128,1152]{1,0:T(8,128)(2,1)S(1)} %pad.4.proj_ref), custom_call_target="tpu_custom_call" | custom-call | flops 1 | bytes 1 | tf_op jit(solution)/shard_map/spatial_backward/pallas_call | solution.py:374
  95.3 1.9 %collective-permute-start.3 = (bf16[8,64,216]{2,1,0:T(8,128)(2,1)S(1)}, bf16[8,64,216]{2,1,0:T(8,128)(2,1)S(1)}, u32[]{:S(2)}, u32[]{:S(2)}) collective-permute-start(bf16[8,64,216]{2,1,0:T(8,128)(2,1)S(1)} %get-tuple-element.25), channel_id=1, source_target_pairs={{0,1},{1,0},{2,3},{3,2},{4,5},{5,4},{6,7},{7,6},{8,9},{9,8},{10,11... | collective-permute-start | bytes 663560 | tf_op jit(solution)/shard_map/spatial_backward/ppermute | solution.py:381
  97.2 1.5 %collective-permute-done.3.got_ref = bf16[8,64,216]{2,1,0:T(8,128)(2,1)S(1)} collective-permute-done((bf16[8,64,216]{2,1,0:T(8,128)(2,1)S(1)}, bf16[8,64,216]{2,1,0:T(8,128)(2,1)S(1)}, u32[]{:S(2)}, u32[]{:S(2)}) %collective-permute-start.3) | collective-permute-done | bytes 221216 | tf_op jit(solution)/shard_map/spatial_backward/ppermute | solution.py:381
  98.7 21.3 %all-to-all-done.2.home_ref = bf16[32,2,9936]{2,1,0:T(2,128)(2,1)S(1)} async-done(((bf16[32,2,9936]{2,1,0:T(2,128)(2,1)}), bf16[32,2,9936]{2,1,0:T(2,128)(2,1)S(1)}, u32[]{:S(2)}, u32[]{:S(2)}) %all-to-all-start.2) | async-done | bytes 1271840 | tf_op jit(solution)/shard_map/temporal_out/all_to_all | solution.py:367
  120.4 0.8 copy-done.4
  121.2 3.5 %all-to-all-start.3 = ((bf16[8,128,252]{2,1,0:T(8,128)(2,1)}), bf16[8,128,252]{2,1,0:T(8,128)(2,1)S(1)}, u32[]{:S(2)}, u32[]{:S(2)}) async-start(bf16[8,128,252]{2,1,0:T(8,128)(2,1)} %copy-done.4), calls=%async_computation.3 | async-start | bytes 1048576 | tf_op jit(solution)/shard_map/spatial_out/all_to_all | solution.py:405
  125.2 1.9 %collective-permute-start.4 = (f32[18,72]{1,0:T(8,128)S(1)}, f32[18,72]{1,0:T(8,128)S(1)}, u32[]{:S(2)}, u32[]{:S(2)}) collective-permute-start(f32[18,72]{1,0:T(8,128)S(1)} %bitcast.57), channel_id=1, source_target_pairs={{0,1},{1,0},{2,3},{3,2},{4,5},{5,4},{6,7},{7,6},{8,9},{9,8},{10,11... | collective-permute-start | bytes 15560 | tf_op jit(solution)/shard_map/spatial_projection/ppermute | solution.py:388
  128.9 0.7 fusion
  129.6 0.7 copy.32
  130.3 0.7 copy.33
  131.7 9.0 %all-to-all-done.3.x_ref = bf16[8,128,252]{2,1,0:T(8,128)(2,1)S(1)} async-done(((bf16[8,128,252]{2,1,0:T(8,128)(2,1)}), bf16[8,128,252]{2,1,0:T(8,128)(2,1)S(1)}, u32[]{:S(2)}, u32[]{:S(2)}) %all-to-all-start.3) | async-done | bytes 516128 | tf_op jit(solution)/shard_map/spatial_out/all_to_all | solution.py:405
  140.6 2.0 %spatial_out.3 = (bf16[128,576]{1,0:T(8,128)(2,1)}, bf16[128,576]{1,0:T(8,128)(2,1)}, bf16[128,576]{1,0:T(8,128)(2,1)}, f32[18,72]{1,0:T(8,128)}) custom-call(s32[2]{0:T(128)S(1)} %copy-done.13, bf16[8,128,252]{2,1,0:T(8,128)(2,1)S(1)} %all-to-all-done.3.x_ref), custom_call_target="tpu_custom_call" | custom-call | flops 1 | bytes 1 | tf_op jit(solution)/shard_map/spatial_out/pallas_call | solution.py:406
  (49 shorter events, 4.4 us)
Async XLA Ops:
  7.2 80.8 %copy-start = (bf16[576,1152]{1,0:T(8,128)(2,1)S(1)}, bf16[576,1152]{1,0:T(8,128)(2,1)}, u32[]{:S(2)}) copy-start(bf16[576,1152]{1,0:T(8,128)(2,1)} %param.16) | copy-start | bytes 3981316
  7.2 5.3 %copy-start.5 = (bf16[2,1,64,1152]{3,2,1,0:T(8,128)(2,1)S(1)}, bf16[2,1,64,1152]{3,2,1,0:T(8,128)(2,1)}, u32[]{:S(2)}) copy-start(bf16[2,1,64,1152]{3,2,1,0:T(8,128)(2,1)} %param.15) | copy-start | bytes 884740
  7.2 5.3 %copy-start.6 = (bf16[2,1,64,576]{3,2,1,0:T(8,128)(2,1)S(1)}, bf16[2,1,64,576]{3,2,1,0:T(8,128)(2,1)}, u32[]{:S(2)}) copy-start(bf16[2,1,64,576]{3,2,1,0:T(8,128)(2,1)} %param.12) | copy-start | bytes 442372
  7.2 5.3 %copy-start.7 = (bf16[2,1,64,576]{3,2,1,0:T(8,128)(2,1)S(1)}, bf16[2,1,64,576]{3,2,1,0:T(8,128)(2,1)}, u32[]{:S(2)}) copy-start(bf16[2,1,64,576]{3,2,1,0:T(8,128)(2,1)} %param.13) | copy-start | bytes 442372
  7.2 5.3 %copy-start.8 = (bf16[2,1,64,576]{3,2,1,0:T(8,128)(2,1)S(1)}, bf16[2,1,64,576]{3,2,1,0:T(8,128)(2,1)}, u32[]{:S(2)}) copy-start(bf16[2,1,64,576]{3,2,1,0:T(8,128)(2,1)} %param.14) | copy-start | bytes 442372
  7.2 64.3 %all-gather.2.cloned.1.call-start = ((), (), s32[]{:S(2)}) async-start(), calls=%async_computation.4 | async-start | bytes 2654208 | tf_op jit(solution)/shard_map/spatial_grad_gather/all_gather | solution.py:327
  8.4 3.3 %collective-permute-start.2 = (bf16[64,1152]{1,0:T(8,128)(2,1)S(1)}, bf16[64,1152]{1,0:T(8,128)(2,1)S(1)}, u32[]{:S(2)}, u32[]{:S(2)}) collective-permute-start(bf16[64,1152]{1,0:T(8,128)(2,1)S(1)} %get-tuple-element.58), channel_id=1, source_target_pairs={{0,1},{1,0},{2,3},{3,2},{4,5},{5,4},{6,7},{7,6},{8,9},{9,8},{10,11... | collective-permute-start | bytes 442376 | tf_op jit(solution)/shard_map/spatial_grad_gather/ppermute | solution.py:326
  12.5 11.7 %copy-start.9 = (bf16[2,1,64,576]{3,2,1,0:T(8,128)(2,1)S(1)}, bf16[2,1,64,576]{3,2,1,0:T(8,128)(2,1)}, u32[]{:S(2)}) copy-start(bf16[2,1,64,576]{3,2,1,0:T(8,128)(2,1)} %param.9) | copy-start | bytes 442372
  12.5 11.7 %copy-start.10 = (bf16[2,1,64,576]{3,2,1,0:T(8,128)(2,1)S(1)}, bf16[2,1,64,576]{3,2,1,0:T(8,128)(2,1)}, u32[]{:S(2)}) copy-start(bf16[2,1,64,576]{3,2,1,0:T(8,128)(2,1)} %param.10) | copy-start | bytes 442372
  12.5 11.7 %copy-start.11 = (bf16[2,1,64,576]{3,2,1,0:T(8,128)(2,1)S(1)}, bf16[2,1,64,576]{3,2,1,0:T(8,128)(2,1)}, u32[]{:S(2)}) copy-start(bf16[2,1,64,576]{3,2,1,0:T(8,128)(2,1)} %param.11) | copy-start | bytes 442372
  13.8 32.3 %all-to-all-start.1 = ((bf16[32,4,2880]{2,1,0:T(4,128)(2,1)}), bf16[32,4,2880]{2,1,0:T(4,128)(2,1)S(1)}, u32[]{:S(2)}, u32[]{:S(2)}) async-start(bf16[32,4,2880]{2,1,0:T(4,128)(2,1)} %temporal_in.1), calls=%async_computation.1 | async-start | bytes 1507328 | tf_op jit(solution)/shard_map/temporal_in/all_to_all | solution.py:320
  24.2 33.5 %copy-start.12 = (s32[2]{0:T(128)}, s32[2]{0:T(128)S(1)}, u32[]{:S(2)}) copy-start(s32[2]{0:T(128)S(1)} %pad_add_fusion.place_ref) | copy-start | bytes 28
  25.4 3.4 %collective-permute-start = (bf16[8,16,864]{2,1,0:T(8,128)(2,1)S(1)}, bf16[8,16,864]{2,1,0:T(8,128)(2,1)S(1)}, u32[]{:S(2)}, u32[]{:S(2)}) collective-permute-start(bf16[8,16,864]{2,1,0:T(8,128)(2,1)S(1)} %get-tuple-element.20), channel_id=1, source_target_pairs={{0,1},{1,0},{2,3},{3,2},{4,5},{5,4},{6,7},{7,6},{8,9},{9,8},{10,11... | collective-permute-start | bytes 663560 | tf_op jit(solution)/shard_map/spatial_in/ppermute | solution.py:336
  46.2 25.3 %all-to-all-start = ((bf16[8,32,864]{2,1,0:T(8,128)(2,1)}), bf16[8,32,864]{2,1,0:T(8,128)(2,1)S(1)}, u32[]{:S(2)}, u32[]{:S(2)}) async-start(bf16[8,32,864]{2,1,0:T(8,128)(2,1)} %pad_maximum_fusion), calls=%async_computation | async-start | bytes 917504 | tf_op jit(solution)/shard_map/spatial_in/all_to_all | solution.py:337
  65.3 6.3 %collective-permute-start.1 = (bf16[64,5184]{1,0:T(8,128)(2,1)}, bf16[64,5184]{1,0:T(8,128)(2,1)S(1)}, u32[]{:S(2)}, u32[]{:S(2)}) collective-permute-start(bf16[64,5184]{1,0:T(8,128)(2,1)} %get-tuple-element.21), channel_id=1, source_target_pairs={{0,1},{1,0},{2,3},{3,2},{4,5},{5,4},{6,7},{7,6},{8,9},{9,8},{10,11... | collective-permute-start | bytes 1990664 | tf_op jit(solution)/shard_map/temporal_attention/ppermute | solution.py:349
  71.5 0.8 copy-start.2
  71.5 1.0 copy-start.14
  78.6 9.5 %copy-start.3 = (bf16[8,32,864]{2,1,0:T(8,128)(2,1)S(1)}, bf16[8,32,864]{2,1,0:T(8,128)(2,1)}, u32[]{:S(2)}) copy-start(bf16[8,32,864]{2,1,0:T(8,128)(2,1)} %copy-done.2) | copy-start | bytes 1327108
  78.6 41.4 %all-to-all-start.2 = ((bf16[32,2,9936]{2,1,0:T(2,128)(2,1)}), bf16[32,2,9936]{2,1,0:T(2,128)(2,1)S(1)}, u32[]{:S(2)}, u32[]{:S(2)}) async-start(bf16[32,2,9936]{2,1,0:T(2,128)(2,1)} %spatial_forward.1), calls=%async_computation.2 | async-start | bytes 2555904 | tf_op jit(solution)/shard_map/temporal_out/all_to_all | solution.py:367
  88.1 1.7 %copy-start.1 = (bf16[1024,1152]{1,0:T(8,128)(2,1)S(1)}, bf16[1024,1152]{1,0:T(8,128)(2,1)}, u32[]{:S(2)}) copy-start(bf16[1024,1152]{1,0:T(8,128)(2,1)} %all-gather.2.cloned.1.call-done) | copy-start | bytes 7077892
  95.3 3.4 %collective-permute-start.3 = (bf16[8,64,216]{2,1,0:T(8,128)(2,1)S(1)}, bf16[8,64,216]{2,1,0:T(8,128)(2,1)S(1)}, u32[]{:S(2)}, u32[]{:S(2)}) collective-permute-start(bf16[8,64,216]{2,1,0:T(8,128)(2,1)S(1)} %get-tuple-element.25), channel_id=1, source_target_pairs={{0,1},{1,0},{2,3},{3,2},{4,5},{5,4},{6,7},{7,6},{8,9},{9,8},{10,11... | collective-permute-start | bytes 663560 | tf_op jit(solution)/shard_map/spatial_backward/ppermute | solution.py:381
  120.4 0.8 copy-start.4
  121.2 19.5 %all-to-all-start.3 = ((bf16[8,128,252]{2,1,0:T(8,128)(2,1)}), bf16[8,128,252]{2,1,0:T(8,128)(2,1)S(1)}, u32[]{:S(2)}, u32[]{:S(2)}) async-start(bf16[8,128,252]{2,1,0:T(8,128)(2,1)} %copy-done.4), calls=%async_computation.3 | async-start | bytes 1048576 | tf_op jit(solution)/shard_map/spatial_out/all_to_all | solution.py:405
  125.2 3.1 %collective-permute-start.4 = (f32[18,72]{1,0:T(8,128)S(1)}, f32[18,72]{1,0:T(8,128)S(1)}, u32[]{:S(2)}, u32[]{:S(2)}) collective-permute-start(f32[18,72]{1,0:T(8,128)S(1)} %bitcast.57), channel_id=1, source_target_pairs={{0,1},{1,0},{2,3},{3,2},{4,5},{5,4},{6,7},{7,6},{8,9},{9,8},{10,11... | collective-permute-start | bytes 15560 | tf_op jit(solution)/shard_map/spatial_projection/ppermute | solution.py:388
  128.3 3.4 %collective-permute-start.5 = (f32[18,72]{1,0:T(8,128)S(1)}, f32[18,72]{1,0:T(8,128)S(1)}, u32[]{:S(2)}, u32[]{:S(2)}) collective-permute-start(f32[18,72]{1,0:T(8,128)S(1)} %bitcast_add_fusion), channel_id=1, source_target_pairs={{0,0},{1,1},{2,64},{3,65},{4,128},{5,129},{6,192},{7,193},{8,256},... | collective-permute-start | bytes 15560 | tf_op jit(solution)/shard_map/spatial_projection/ppermute | solution.py:396
  128.9 11.7 %copy-start.13 = (s32[2]{0:T(128)S(1)}, s32[2]{0:T(128)}, u32[]{:S(2)}) copy-start(s32[2]{0:T(128)} %copy-done.12) | copy-start | bytes 28
Sparse Core Ops, SparseCore 0:
  12.6 54.6 all-gather.1

commit v5 on v4

--- a/solution.py
+++ b/solution.py
@@ -15,6 +15,7 @@
 SUMS_S = 9 * 2 * HSIZE
 THREE = 3 * HSIZE
 FACTOR = HSIZE ** (-0.5)
+FACTOR_LOG2 = FACTOR * 1.4426950408889634
 BF = jnp.bfloat16
 F32 = jnp.float32
 
@@ -102,8 +103,9 @@
             out_ref[z, 32 * n : 32 * n + 18, THREE:] = half
 
 
-def unpack_kernel(place_ref, x_ref, dq_ref, dk_ref, dv_ref, sum_ref):
+def unpack_kernel(place_ref, x_ref, other_ref, dq_ref, dk_ref, dv_ref, sum_ref, other_out_ref):
     core = place_ref[0]
+    other_out_ref[...] = other_ref[...]
     for n in range(2):
         total = None
         for z in range(x_ref.shape[0]):
@@ -143,8 +145,8 @@
 
 
 def attend_block(queries, keys, values):
-    scores = dot_nt(queries.astype(BF), keys) * FACTOR
-    e = jnp.exp(scores - scores.max(-1, keepdims=True))
+    scores = dot_nt(queries.astype(BF), keys)
+    e = jnp.exp2((scores - scores.max(-1, keepdims=True)) * FACTOR_LOG2)
     inverse = 1.0 / e.sum(-1, keepdims=True)
     return e, inverse, (dot(e.astype(BF), values) * inverse).astype(BF)
 
@@ -393,7 +395,7 @@
                     for c in range(2):
                         source = (y * 4 + x) * n_pix + 2 * zz + c
                         perm.append((source, (zz * 4 + x) * n_pix + 2 * y + c))
-        proj_s_grad = lax.ppermute(sums_s, ("frame", "pix"), perm)
+        sums_s = lax.ppermute(sums_s, ("frame", "pix"), perm)
 
     with jax.named_scope("spatial_out"):
         sent = call(
@@ -403,12 +405,12 @@
             scratch=[pltpu.VMEM((n_z, 18, HSIZE), F32)],
         )(home_t, own_s, got_s)
         home_s = lax.all_to_all(sent, "pix", 0, 0, axis_index_groups=same_core, tiled=True)
-        *outs_s, proj_t_grad = call(
+        *outs_s, proj_t_grad, proj_s_grad = call(
             unpack_kernel,
-            1,
-            (whole((128, HD), BF),) * 3 + (whole((18, HSIZE), F32),),
+            2,
+            (whole((128, HD), BF),) * 3 + (whole((18, HSIZE), F32),) * 2,
             scalars=1,
-        )(place, home_s)
+        )(place, home_s, sums_s)
         outs_s = [a.reshape(2, 1, 64, HD) for a in outs_s]
 
     return (*outs_s, *outs_t, proj_s_grad, proj_t_grad)

time: 151 us -> 150 us (level)
    unnamed x32 -> x31, local copies, waits for them, and re-layouts: 4.13 us -> 3.53 us
where the time goes in v5:
time: 150 us; the launch traced here: 149 us
  waiting for transfers between devices  55.7 us (37%)
  starting transfers between devices  43.7 us (29%)
  Pallas kernels  23.7 us (16%)
  between operations  14.4 us (10%)
  local copies, waits for them, and re-layouts  9.83 us (7%)
  other arithmetic  1.98 us (1%)
    all_to_all x1, waiting for transfers between devices, on_device(): home_t = lax.all_to_all(sent_out, 'frame', 0, 0, tiled=True)  21.4 us
    all_to_all x1, waiting for transfers between devices, on_device(): lax.all_to_all(sent_in, 'frame', 0, 0, tiled=True).reshape(128, 3 * HD + D)  16.5 us
    all_to_all x1, starting transfers between devices, on_device(): lax.all_to_all(packed, 'pix', 0, 0, axis_index_groups=same_core, tiled=True)  10.3 us
    all_to_all x1, starting transfers between devices, on_device(): lax.all_to_all(sent_in, 'frame', 0, 0, tiled=True).reshape(128, 3 * HD + D)  10.3 us
    all_to_all x1, starting transfers between devices, on_device(): home_t = lax.all_to_all(sent_out, 'frame', 0, 0, tiled=True)  9.39 us
    all_to_all x1, waiting for transfers between devices, on_device(): lax.all_to_all(sent, 'pix', 0, 0, axis_index_groups=same_core, tiled=True)  8.97 us
    pallas_call x1, Pallas kernels, on_device(): call(temporal_kernel, 1, (whole((frames, 2, GRADS), BF), whole((64, SUMS_...  7.53 us
    pallas_call x1, Pallas kernels, on_device(): call(forward_kernel, 2, whole((frames, 2, GRADS + SUMS_T + SUMS_S), BF),...  5.9 us
  transfers between devices with their start and end apart: 11, of which 8 were waited for; matrix products, arithmetic and copies ran while one was open for 4% of the time, Pallas kernels for 10%

profile of v5, /device:TPU:2, one launch (start us, length us, event | category | flops | bytes accessed | tf_op | source)
XLA Modules:
  0.0 149.4 jit_solution(13941495343605453767)
XLA Ops:
  7.3 1.1 dynamic-slice_bitcast_fusion.1
  8.4 1.9 %collective-permute-start.2 = (bf16[64,1152]{1,0:T(8,128)(2,1)S(1)}, bf16[64,1152]{1,0:T(8,128)(2,1)S(1)}, u32[]{:S(2)}, u32[]{:S(2)}) collective-permute-start(bf16[64,1152]{1,0:T(8,128)(2,1)S(1)} %get-tuple-element.60), channel_id=1, source_target_pairs={{0,1},{1,0},{2,3},{3,2},{4,5},{5,4},{6,7},{7,6},{8,9},{9,8},{10,11... | collective-permute-start | bytes 442376 | tf_op jit(solution)/shard_map/spatial_grad_gather/ppermute | solution.py:328
  10.4 1.3 collective-permute-done.2
  11.7 0.7 pad_maximum_fusion.1
  12.5 1.3 temporal_in.1
  13.8 10.3 %all-to-all-start.1 = ((bf16[32,4,2880]{2,1,0:T(4,128)(2,1)}), bf16[32,4,2880]{2,1,0:T(4,128)(2,1)S(1)}, u32[]{:S(2)}, u32[]{:S(2)}) async-start(bf16[32,4,2880]{2,1,0:T(4,128)(2,1)} %temporal_in.1), calls=%async_computation.1 | async-start | bytes 1507328 | tf_op jit(solution)/shard_map/temporal_in/all_to_all | solution.py:322
  24.2 1.2 spatial_in.1
  25.4 1.9 %collective-permute-start = (bf16[8,16,864]{2,1,0:T(8,128)(2,1)S(1)}, bf16[8,16,864]{2,1,0:T(8,128)(2,1)S(1)}, u32[]{:S(2)}, u32[]{:S(2)}) collective-permute-start(bf16[8,16,864]{2,1,0:T(8,128)(2,1)S(1)} %get-tuple-element.21), channel_id=1, source_target_pairs={{0,1},{1,0},{2,3},{3,2},{4,5},{5,4},{6,7},{7,6},{8,9},{9,8},{10,11... | collective-permute-start | bytes 663560 | tf_op jit(solution)/shard_map/spatial_in/ppermute | solution.py:338
  27.4 1.5 collective-permute-done
  28.8 0.8 pad_maximum_fusion
  29.6 16.5 %all-to-all-done.1 = bf16[32,4,2880]{2,1,0:T(4,128)(2,1)S(1)} async-done(((bf16[32,4,2880]{2,1,0:T(4,128)(2,1)}), bf16[32,4,2880]{2,1,0:T(4,128)(2,1)S(1)}, u32[]{:S(2)}, u32[]{:S(2)}) %all-to-all-start.1) | async-done | bytes 737312 | tf_op jit(solution)/shard_map/temporal_in/all_to_all | solution.py:322
  46.2 10.3 %all-to-all-start = ((bf16[8,32,864]{2,1,0:T(8,128)(2,1)}), bf16[8,32,864]{2,1,0:T(8,128)(2,1)S(1)}, u32[]{:S(2)}, u32[]{:S(2)}) async-start(bf16[8,32,864]{2,1,0:T(8,128)(2,1)} %pad_maximum_fusion), calls=%async_computation | async-start | bytes 917504 | tf_op jit(solution)/shard_map/spatial_in/all_to_all | solution.py:339
  56.5 1.2 reshape.72.x_ref
  57.7 7.5 %temporal_attention.1 = (bf16[32,2,3456]{2,1,0:T(2,128)(2,1)}, bf16[64,5184]{1,0:T(8,128)(2,1)}, bf16[64,5184]{1,0:T(8,128)(2,1)}) custom-call(s32[2]{0:T(128)} %copy-done.12, bf16[128,2880]{1,0:T(8,128)(2,1)} %reshape.72.x_ref, bf16[576,1152]{1,0:T(8,128)(2,1)} %proj_any.1), custom_call_target="tpu_custom_call" | custom-call | flops 1 | bytes 1 | tf_op jit(solution)/shard_map/temporal_attention/pallas_call | solution.py:342
  65.3 1.9 %collective-permute-start.1 = (bf16[64,5184]{1,0:T(8,128)(2,1)}, bf16[64,5184]{1,0:T(8,128)(2,1)S(1)}, u32[]{:S(2)}, u32[]{:S(2)}) collective-permute-start(bf16[64,5184]{1,0:T(8,128)(2,1)} %get-tuple-element.22), channel_id=1, source_target_pairs={{0,1},{1,0},{2,3},{3,2},{4,5},{5,4},{6,7},{7,6},{8,9},{9,8},{10,11... | collective-permute-start | bytes 1990664 | tf_op jit(solution)/shard_map/temporal_attention/ppermute | solution.py:351
  67.2 4.3 %all-to-all-done.x_ref = bf16[8,32,864]{2,1,0:T(8,128)(2,1)S(1)} async-done(((bf16[8,32,864]{2,1,0:T(8,128)(2,1)}), bf16[8,32,864]{2,1,0:T(8,128)(2,1)S(1)}, u32[]{:S(2)}, u32[]{:S(2)}) %all-to-all-start) | async-done | bytes 442400 | tf_op jit(solution)/shard_map/spatial_in/all_to_all | solution.py:339
  71.6 0.8 copy-done.2
  72.6 5.9 %spatial_forward.1 = bf16[32,2,9936]{2,1,0:T(2,128)(2,1)} custom-call(bf16[8,32,864]{2,1,0:T(8,128)(2,1)} %copy-done.2, bf16[64,5184]{1,0:T(8,128)(2,1)} %copy-done.14, bf16[32,2,3456]{2,1,0:T(2,128)(2,1)} %get-tuple-element.23.grads_any, bf16[8,2,64,1152]{3,2,1,0:T(8,128)(2,1)} %bitcast.42, bf16[64,5184]{1,0:T(8,128)(2,1)} %get-tuple-element.24.keep_any), custom_call_target="tpu_custom_call" | custom-call | flops 1 | bytes 1 | tf_op jit(solution)/shard_map/spatial_forward/pallas_call | solution.py:354
  78.5 9.4 %all-to-all-start.2 = ((bf16[32,2,9936]{2,1,0:T(2,128)(2,1)}), bf16[32,2,9936]{2,1,0:T(2,128)(2,1)S(1)}, u32[]{:S(2)}, u32[]{:S(2)}) async-start(bf16[32,2,9936]{2,1,0:T(2,128)(2,1)} %spatial_forward.1), calls=%async_computation.2 | async-start | bytes 2555904 | tf_op jit(solution)/shard_map/temporal_out/all_to_all | solution.py:369
  88.0 1.7 %copy-done.1 = bf16[1024,1152]{1,0:T(8,128)(2,1)S(1)} copy-done((bf16[1024,1152]{1,0:T(8,128)(2,1)S(1)}, bf16[1024,1152]{1,0:T(8,128)(2,1)}, u32[]{:S(2)}) %copy-start.1) | copy-done | bytes 2359320
  89.6 5.4 %spatial_backward.1 = (bf16[8,64,216]{2,1,0:T(8,128)(2,1)S(1)}, bf16[8,64,216]{2,1,0:T(8,128)(2,1)S(1)}) custom-call(bf16[8,32,864]{2,1,0:T(8,128)(2,1)S(1)} %copy-done.3, bf16[8,2,64,1152]{3,2,1,0:T(8,128)(2,1)S(1)} %bitcast.43, bf16[128,1152]{1,0:T(8,128)(2,1)S(1)} %pad.4.proj_ref), custom_call_target="tpu_custom_call" | custom-call | flops 1 | bytes 1 | tf_op jit(solution)/shard_map/spatial_backward/pallas_call | solution.py:376
  95.0 1.9 %collective-permute-start.3 = (bf16[8,64,216]{2,1,0:T(8,128)(2,1)S(1)}, bf16[8,64,216]{2,1,0:T(8,128)(2,1)S(1)}, u32[]{:S(2)}, u32[]{:S(2)}) collective-permute-start(bf16[8,64,216]{2,1,0:T(8,128)(2,1)S(1)} %get-tuple-element.26), channel_id=1, source_target_pairs={{0,1},{1,0},{2,3},{3,2},{4,5},{5,4},{6,7},{7,6},{8,9},{9,8},{10,11... | collective-permute-start | bytes 663560 | tf_op jit(solution)/shard_map/spatial_backward/ppermute | solution.py:383
  97.0 1.5 %collective-permute-done.3.got_ref = bf16[8,64,216]{2,1,0:T(8,128)(2,1)S(1)} collective-permute-done((bf16[8,64,216]{2,1,0:T(8,128)(2,1)S(1)}, bf16[8,64,216]{2,1,0:T(8,128)(2,1)S(1)}, u32[]{:S(2)}, u32[]{:S(2)}) %collective-permute-start.3) | collective-permute-done | bytes 221216 | tf_op jit(solution)/shard_map/spatial_backward/ppermute | solution.py:383
  98.5 21.4 %all-to-all-done.2.home_ref = bf16[32,2,9936]{2,1,0:T(2,128)(2,1)S(1)} async-done(((bf16[32,2,9936]{2,1,0:T(2,128)(2,1)}), bf16[32,2,9936]{2,1,0:T(2,128)(2,1)S(1)}, u32[]{:S(2)}, u32[]{:S(2)}) %all-to-all-start.2) | async-done | bytes 1271840 | tf_op jit(solution)/shard_map/temporal_out/all_to_all | solution.py:369
  120.3 0.8 copy-done.4
  121.1 3.5 %all-to-all-start.3 = ((bf16[8,128,252]{2,1,0:T(8,128)(2,1)}), bf16[8,128,252]{2,1,0:T(8,128)(2,1)S(1)}, u32[]{:S(2)}, u32[]{:S(2)}) async-start(bf16[8,128,252]{2,1,0:T(8,128)(2,1)} %copy-done.4), calls=%async_computation.3 | async-start | bytes 1048576 | tf_op jit(solution)/shard_map/spatial_out/all_to_all | solution.py:407
  125.1 1.9 %collective-permute-start.4 = (f32[18,72]{1,0:T(8,128)S(1)}, f32[18,72]{1,0:T(8,128)S(1)}, u32[]{:S(2)}, u32[]{:S(2)}) collective-permute-start(f32[18,72]{1,0:T(8,128)S(1)} %bitcast.57), channel_id=1, source_target_pairs={{0,1},{1,0},{2,3},{3,2},{4,5},{5,4},{6,7},{7,6},{8,9},{9,8},{10,11... | collective-permute-start | bytes 15560 | tf_op jit(solution)/shard_map/spatial_projection/ppermute | solution.py:390
  128.8 0.7 fusion
  129.5 0.7 copy.33
  130.2 0.7 copy.34
  131.6 9.0 %all-to-all-done.3.x_ref = bf16[8,128,252]{2,1,0:T(8,128)(2,1)S(1)} async-done(((bf16[8,128,252]{2,1,0:T(8,128)(2,1)}), bf16[8,128,252]{2,1,0:T(8,128)(2,1)S(1)}, u32[]{:S(2)}, u32[]{:S(2)}) %all-to-all-start.3) | async-done | bytes 516128 | tf_op jit(solution)/shard_map/spatial_out/all_to_all | solution.py:407
  140.5 2.0 %spatial_out.3 = (bf16[128,576]{1,0:T(8,128)(2,1)}, bf16[128,576]{1,0:T(8,128)(2,1)}, bf16[128,576]{1,0:T(8,128)(2,1)}, f32[18,72]{1,0:T(8,128)}, f32[18,72]{1,0:T(8,128)}) custom-call(s32[2]{0:T(128)S(1)} %copy-done.13, bf16[8,128,252]{2,1,0:T(8,128)(2,1)S(1)} %all-to-all-done.3.x_ref, f32[18,72]{1,0:T(8,128)S(1)} %collective-permute-done.5.other_ref), custom_call_target="tpu_custom_call" | custom-call | flops 1 | bytes 1 | tf_op jit(solution)/shard_map/spatial_out/pallas_call | solution.py:408
  (48 shorter events, 3.8 us)
Async XLA Ops:
  7.2 80.7 %copy-start = (bf16[576,1152]{1,0:T(8,128)(2,1)S(1)}, bf16[576,1152]{1,0:T(8,128)(2,1)}, u32[]{:S(2)}) copy-start(bf16[576,1152]{1,0:T(8,128)(2,1)} %param.16) | copy-start | bytes 3981316
  7.2 5.3 %copy-start.5 = (bf16[2,1,64,1152]{3,2,1,0:T(8,128)(2,1)S(1)}, bf16[2,1,64,1152]{3,2,1,0:T(8,128)(2,1)}, u32[]{:S(2)}) copy-start(bf16[2,1,64,1152]{3,2,1,0:T(8,128)(2,1)} %param.15) | copy-start | bytes 884740
  7.2 5.3 %copy-start.6 = (bf16[2,1,64,576]{3,2,1,0:T(8,128)(2,1)S(1)}, bf16[2,1,64,576]{3,2,1,0:T(8,128)(2,1)}, u32[]{:S(2)}) copy-start(bf16[2,1,64,576]{3,2,1,0:T(8,128)(2,1)} %param.12) | copy-start | bytes 442372
  7.2 5.3 %copy-start.7 = (bf16[2,1,64,576]{3,2,1,0:T(8,128)(2,1)S(1)}, bf16[2,1,64,576]{3,2,1,0:T(8,128)(2,1)}, u32[]{:S(2)}) copy-start(bf16[2,1,64,576]{3,2,1,0:T(8,128)(2,1)} %param.13) | copy-start | bytes 442372
  7.2 5.3 %copy-start.8 = (bf16[2,1,64,576]{3,2,1,0:T(8,128)(2,1)S(1)}, bf16[2,1,64,576]{3,2,1,0:T(8,128)(2,1)}, u32[]{:S(2)}) copy-start(bf16[2,1,64,576]{3,2,1,0:T(8,128)(2,1)} %param.14) | copy-start | bytes 442372
  7.2 64.3 %all-gather.2.cloned.1.call-start = ((), (), s32[]{:S(2)}) async-start(), calls=%async_computation.4 | async-start | bytes 2654208 | tf_op jit(solution)/shard_map/spatial_grad_gather/all_gather | solution.py:329
  8.4 3.3 %collective-permute-start.2 = (bf16[64,1152]{1,0:T(8,128)(2,1)S(1)}, bf16[64,1152]{1,0:T(8,128)(2,1)S(1)}, u32[]{:S(2)}, u32[]{:S(2)}) collective-permute-start(bf16[64,1152]{1,0:T(8,128)(2,1)S(1)} %get-tuple-element.60), channel_id=1, source_target_pairs={{0,1},{1,0},{2,3},{3,2},{4,5},{5,4},{6,7},{7,6},{8,9},{9,8},{10,11... | collective-permute-start | bytes 442376 | tf_op jit(solution)/shard_map/spatial_grad_gather/ppermute | solution.py:328
  12.5 11.7 %copy-start.9 = (bf16[2,1,64,576]{3,2,1,0:T(8,128)(2,1)S(1)}, bf16[2,1,64,576]{3,2,1,0:T(8,128)(2,1)}, u32[]{:S(2)}) copy-start(bf16[2,1,64,576]{3,2,1,0:T(8,128)(2,1)} %param.9) | copy-start | bytes 442372
  12.5 11.7 %copy-start.10 = (bf16[2,1,64,576]{3,2,1,0:T(8,128)(2,1)S(1)}, bf16[2,1,64,576]{3,2,1,0:T(8,128)(2,1)}, u32[]{:S(2)}) copy-start(bf16[2,1,64,576]{3,2,1,0:T(8,128)(2,1)} %param.10) | copy-start | bytes 442372
  12.5 11.7 %copy-start.11 = (bf16[2,1,64,576]{3,2,1,0:T(8,128)(2,1)S(1)}, bf16[2,1,64,576]{3,2,1,0:T(8,128)(2,1)}, u32[]{:S(2)}) copy-start(bf16[2,1,64,576]{3,2,1,0:T(8,128)(2,1)} %param.11) | copy-start | bytes 442372
  13.8 32.3 %all-to-all-start.1 = ((bf16[32,4,2880]{2,1,0:T(4,128)(2,1)}), bf16[32,4,2880]{2,1,0:T(4,128)(2,1)S(1)}, u32[]{:S(2)}, u32[]{:S(2)}) async-start(bf16[32,4,2880]{2,1,0:T(4,128)(2,1)} %temporal_in.1), calls=%async_computation.1 | async-start | bytes 1507328 | tf_op jit(solution)/shard_map/temporal_in/all_to_all | solution.py:322
  24.2 33.5 %copy-start.12 = (s32[2]{0:T(128)}, s32[2]{0:T(128)S(1)}, u32[]{:S(2)}) copy-start(s32[2]{0:T(128)S(1)} %pad_add_fusion.place_ref) | copy-start | bytes 28
  25.4 3.4 %collective-permute-start = (bf16[8,16,864]{2,1,0:T(8,128)(2,1)S(1)}, bf16[8,16,864]{2,1,0:T(8,128)(2,1)S(1)}, u32[]{:S(2)}, u32[]{:S(2)}) collective-permute-start(bf16[8,16,864]{2,1,0:T(8,128)(2,1)S(1)} %get-tuple-element.21), channel_id=1, source_target_pairs={{0,1},{1,0},{2,3},{3,2},{4,5},{5,4},{6,7},{7,6},{8,9},{9,8},{10,11... | collective-permute-start | bytes 663560 | tf_op jit(solution)/shard_map/spatial_in/ppermute | solution.py:338
  46.2 25.4 %all-to-all-start = ((bf16[8,32,864]{2,1,0:T(8,128)(2,1)}), bf16[8,32,864]{2,1,0:T(8,128)(2,1)S(1)}, u32[]{:S(2)}, u32[]{:S(2)}) async-start(bf16[8,32,864]{2,1,0:T(8,128)(2,1)} %pad_maximum_fusion), calls=%async_computation | async-start | bytes 917504 | tf_op jit(solution)/shard_map/spatial_in/all_to_all | solution.py:339
  65.3 6.3 %collective-permute-start.1 = (bf16[64,5184]{1,0:T(8,128)(2,1)}, bf16[64,5184]{1,0:T(8,128)(2,1)S(1)}, u32[]{:S(2)}, u32[]{:S(2)}) collective-permute-start(bf16[64,5184]{1,0:T(8,128)(2,1)} %get-tuple-element.22), channel_id=1, source_target_pairs={{0,1},{1,0},{2,3},{3,2},{4,5},{5,4},{6,7},{7,6},{8,9},{9,8},{10,11... | collective-permute-start | bytes 1990664 | tf_op jit(solution)/shard_map/temporal_attention/ppermute | solution.py:351
  71.5 0.8 copy-start.2
  71.5 1.0 copy-start.14
  78.5 9.5 %copy-start.3 = (bf16[8,32,864]{2,1,0:T(8,128)(2,1)S(1)}, bf16[8,32,864]{2,1,0:T(8,128)(2,1)}, u32[]{:S(2)}) copy-start(bf16[8,32,864]{2,1,0:T(8,128)(2,1)} %copy-done.2) | copy-start | bytes 1327108
  78.5 41.4 %all-to-all-start.2 = ((bf16[32,2,9936]{2,1,0:T(2,128)(2,1)}), bf16[32,2,9936]{2,1,0:T(2,128)(2,1)S(1)}, u32[]{:S(2)}, u32[]{:S(2)}) async-start(bf16[32,2,9936]{2,1,0:T(2,128)(2,1)} %spatial_forward.1), calls=%async_computation.2 | async-start | bytes 2555904 | tf_op jit(solution)/shard_map/temporal_out/all_to_all | solution.py:369
  88.0 1.7 %copy-start.1 = (bf16[1024,1152]{1,0:T(8,128)(2,1)S(1)}, bf16[1024,1152]{1,0:T(8,128)(2,1)}, u32[]{:S(2)}) copy-start(bf16[1024,1152]{1,0:T(8,128)(2,1)} %all-gather.2.cloned.1.call-done) | copy-start | bytes 7077892
  95.0 3.4 %collective-permute-start.3 = (bf16[8,64,216]{2,1,0:T(8,128)(2,1)S(1)}, bf16[8,64,216]{2,1,0:T(8,128)(2,1)S(1)}, u32[]{:S(2)}, u32[]{:S(2)}) collective-permute-start(bf16[8,64,216]{2,1,0:T(8,128)(2,1)S(1)} %get-tuple-element.26), channel_id=1, source_target_pairs={{0,1},{1,0},{2,3},{3,2},{4,5},{5,4},{6,7},{7,6},{8,9},{9,8},{10,11... | collective-permute-start | bytes 663560 | tf_op jit(solution)/shard_map/spatial_backward/ppermute | solution.py:383
  120.3 0.8 copy-start.4
  121.1 19.5 %all-to-all-start.3 = ((bf16[8,128,252]{2,1,0:T(8,128)(2,1)}), bf16[8,128,252]{2,1,0:T(8,128)(2,1)S(1)}, u32[]{:S(2)}, u32[]{:S(2)}) async-start(bf16[8,128,252]{2,1,0:T(8,128)(2,1)} %copy-done.4), calls=%async_computation.3 | async-start | bytes 1048576 | tf_op jit(solution)/shard_map/spatial_out/all_to_all | solution.py:407
  125.1 3.1 %collective-permute-start.4 = (f32[18,72]{1,0:T(8,128)S(1)}, f32[18,72]{1,0:T(8,128)S(1)}, u32[]{:S(2)}, u32[]{:S(2)}) collective-permute-start(f32[18,72]{1,0:T(8,128)S(1)} %bitcast.57), channel_id=1, source_target_pairs={{0,1},{1,0},{2,3},{3,2},{4,5},{5,4},{6,7},{7,6},{8,9},{9,8},{10,11... | collective-permute-start | bytes 15560 | tf_op jit(solution)/shard_map/spatial_projection/ppermute | solution.py:390
  128.1 3.4 %collective-permute-start.5 = (f32[18,72]{1,0:T(8,128)S(1)}, f32[18,72]{1,0:T(8,128)S(1)}, u32[]{:S(2)}, u32[]{:S(2)}) collective-permute-start(f32[18,72]{1,0:T(8,128)S(1)} %bitcast_add_fusion), channel_id=1, source_target_pairs={{0,0},{1,1},{2,64},{3,65},{4,128},{5,129},{6,192},{7,193},{8,256},... | collective-permute-start | bytes 15560 | tf_op jit(solution)/shard_map/spatial_projection/ppermute | solution.py:398
  128.8 11.8 %copy-start.13 = (s32[2]{0:T(128)S(1)}, s32[2]{0:T(128)}, u32[]{:S(2)}) copy-start(s32[2]{0:T(128)} %copy-done.12) | copy-start | bytes 28
Sparse Core Ops, SparseCore 0:
  12.6 54.1 all-gather.1
